TPU v7x, 128 devices: a whole 4x4x4 slice. The times are simulated.
128 devices in a mesh: tiles: 32 (over x, z, core), swath: 4 (over y).
Axes of the slice: x: 4, y: 4, z: 4, core: 2. Of those that a mesh axis runs over, the one named last changes fastest.
Arguments:
- blk_temp: bfloat16 [1536, 128, 512], P(('tiles', 'swath')), may hold values from -6 to 6
- blk_qual: bfloat16 [1536, 128, 512], P(('tiles', 'swath')), may hold values from 0.25 to 4
- dest_tile: int32 [1536], P(('tiles', 'swath')), may hold values from 0 to 31, as said below
- blk_offset: int32 [1536], P(('tiles', 'swath')), may hold values from 0 to 384
- background: float32 [16384, 512], P('tiles', 'swath'), may hold values from -6 to 6
- reflect: bfloat16 [6, 16384, 512], P(None, 'tiles', 'swath'), may hold values from -6 to 6
- land: int32 [16384, 512], P('tiles', 'swath'), may hold values 0 or 1
- conv_first: bfloat16 [16, 16, 3, 3], replicated, may hold values from -0.75 to 0.75
- bias_first: float32 [16], replicated, may hold values from -3 to 3
- conv_second: bfloat16 [16, 16, 3, 3], replicated, may hold values from -0.75 to 0.75
- bias_second: float32 [16], replicated, may hold values from -3 to 3
- conv_third: bfloat16 [16, 16, 3, 3], replicated, may hold values from -0.75 to 0.75
- bias_third: float32 [16], replicated, may hold values from -3 to 3
- head: bfloat16 [16], replicated, may hold values from -2 to 2
Outputs:
- sharp_temp: float32 [16384, 512], P('tiles', 'swath')
- fit_coefs: float32 [7], replicated
Inputs may be any that keep to these rules, and one draw needn't show every extreme that they name: `dest_tile`: at most 2 of the blocks of one device have destination tile i, for each index i of tiles; one index of tiles receives exactly 2 blocks from every device.
All inputs are finite; a program needn't handle non-finite values. No bound on the sum of `land` on one device may be relied on, other than what follows from the above.
Results may differ from a plain program's by a relative error of at most 0.0072.
Values may be sent and summed in bfloat16 or wider, within the bound.
No kernel may reach another device: no remote copies, remote signals or barrier semaphores. Data moves between devices by JAX's collectives and lax.ppermute only.
A program may use at most 192 MiB of HBM per device.

v0:
```python
import jax
import jax.numpy as jnp
from jax import lax
from jax.sharding import PartitionSpec as P

TR = 512
BR = 128
RADIUS = 7
NBANDS = 6


prior_weight = 0.5
ridge_term = 1.0
highest = lax.Precision.HIGHEST


def extended(cells, sides, width):
    for axis, dim in sides:
        count = lax.axis_size(axis)
        ends = count - 1
        head = lax.slice_in_dim(cells, 0, width, axis=dim)
        tail = lax.slice_in_dim(cells, cells.shape[dim] - width, cells.shape[dim], axis=dim)
        cells = jnp.concatenate(
            [
                lax.ppermute(tail, axis, [(i, (i + 1) % count) for i in range(ends)]),
                cells,
                lax.ppermute(head, axis, [((i + 1) % count, i) for i in range(ends)]),
            ],
            axis=dim,
        )
    return cells


def gauss_taps():
    offsets = jnp.arange(2 * RADIUS + 1, dtype=jnp.float32) - RADIUS
    raw_taps = jnp.exp(-0.125 * offsets * offsets)
    return raw_taps / jnp.sum(raw_taps)


def blur(field, weights):
    full_span = 2 * RADIUS
    height = field.shape[1] - full_span
    width = field.shape[2] - full_span
    across = weights[0] * field[:, 0:height, :]
    for tap_index in range(1, full_span + 1):
        across = across + weights[tap_index] * field[:, tap_index : tap_index + height, :]
    result = weights[0] * across[:, :, 0:width]
    for tap_index in range(1, full_span + 1):
        result = result + weights[tap_index] * across[:, :, tap_index : tap_index + width]
    return result


def solve_small(matrix, vector):
    dimension = matrix.shape[0]
    working = matrix
    solution = vector
    for pivot_index in range(dimension):
        scale_row = working[pivot_index] / working[pivot_index, pivot_index]
        scale_val = solution[pivot_index] / working[pivot_index, pivot_index]
        factor = working[:, pivot_index]
        working = working - factor[:, None] * scale_row[None, :]
        solution = solution - factor * scale_val
        working = working.at[pivot_index].set(scale_row)
        solution = solution.at[pivot_index].set(scale_val)
    return solution


def fit(smooth, land_frac):
    feature_count = smooth.shape[0]
    cell_count = smooth.shape[1] * smooth.shape[2]
    columns = jnp.concatenate(
        [jnp.ones((1, cell_count), jnp.float32), smooth[1:].reshape(feature_count - 1, cell_count)],
        axis=0,
    )
    target = smooth[0].reshape(cell_count)
    masked = columns * land_frac.reshape(1, cell_count)
    normal = lax.dot_general(masked, columns, (((1,), (1,)), ((), ())), precision=highest)
    right_side = jnp.dot(masked, target, precision=highest)
    return (normal, right_side)


def build_stack(raw_fields, smooth, land_frac, fit_coefs):
    detail = jnp.tensordot(fit_coefs[1:], raw_fields[1:] - smooth[1:], axes=1, precision=highest)
    base_field = smooth[0] + detail
    stacked = jnp.concatenate(
        [
            base_field[None],
            raw_fields[0:1],
            smooth[0:1],
            land_frac[None],
            raw_fields[1:],
            smooth[1:],
        ],
        axis=0,
    )
    return (base_field, stacked)


def convolve(field, kernel, bias_term):
    out_field = lax.conv_general_dilated(
        field[None],
        kernel,
        (1, 1),
        "VALID",
        dimension_numbers=("NCHW", "OIHW", "NCHW"),
        preferred_element_type=jnp.float32,
    )[0]
    return jnp.maximum(out_field + bias_term[:, None, None], 0.0)


def block_ranks(owners):
    block_count = owners.shape[-1]
    position = jnp.arange(block_count, dtype=jnp.int32)
    before = position[None, :] < position[:, None]
    same_owner = owners[..., :, None] == owners[..., None, :]
    return jnp.sum((same_owner & before).astype(jnp.int32), axis=-1)


def shards(
    blk_temp,
    blk_qual,
    dest_tile,
    blk_offset,
    background,
    reflect,
    land,
    conv_first,
    bias_first,
    conv_second,
    bias_second,
    conv_third,
    bias_third,
    head,
):
    tiles_size = lax.axis_size("tiles")
    swath_size = lax.axis_size("swath")
    devices = tiles_size * swath_size
    block_count = blk_temp.shape[0]
    height = background.shape[0]
    width = background.shape[1]
    tile_count = height // TR
    capacity = max(2, (2 * block_count + tiles_size - 1) // tiles_size)
    my_group = lax.axis_index("tiles")
    dest_all, offset_all = (
        lax.all_gather(dest_tile, ("tiles", "swath"), axis=0, tiled=True),
        lax.all_gather(blk_offset, ("tiles", "swath"), axis=0, tiled=True),
    )
    own_owner = dest_tile // tile_count
    slot_id = own_owner * capacity + block_ranks(own_owner)
    slot_list = jnp.arange(tiles_size * capacity, dtype=jnp.int32)
    slot_hits = slot_id[None, :] == slot_list[:, None]
    source = jnp.sum(
        jnp.where(slot_hits, jnp.arange(block_count, dtype=jnp.int32)[None, :], 0), axis=1
    )
    filled = jnp.any(slot_hits, axis=1)

    def pick_blocks(blocks):
        chosen = jnp.take(blocks, source, axis=0)
        return jnp.where(filled[:, None, None], chosen, jnp.zeros((), blocks.dtype))

    def pack(blocks):
        chosen = pick_blocks(blocks).reshape(tiles_size, capacity, BR, swath_size, width)
        return jnp.transpose(chosen, (0, 3, 1, 2, 4)).reshape(devices, capacity, BR, width)

    temp_recv, qual_recv = (
        lax.all_to_all(pack(blk_temp), ("tiles", "swath"), split_axis=0, concat_axis=0, tiled=True),
        lax.all_to_all(pack(blk_qual), ("tiles", "swath"), split_axis=0, concat_axis=0, tiled=True),
    )
    dest_grid = dest_all.reshape(devices, block_count)
    all_owner = dest_grid // tile_count
    all_rank = block_ranks(all_owner)
    all_start = (dest_grid - my_group * tile_count) * TR + offset_all.reshape(devices, block_count)
    mine = all_owner == my_group
    slot_index = jnp.arange(capacity, dtype=jnp.int32)
    picked = mine[:, None, :] & (all_rank[:, None, :] == slot_index[None, :, None])
    starts = jnp.sum(jnp.where(picked, all_start[:, None, :], 0), axis=2)
    row_list = (
        starts.reshape(devices * capacity, 1) + jnp.arange(BR, dtype=jnp.int32)[None, :]
    ).reshape(devices * capacity * BR)
    quality = qual_recv.reshape(devices * capacity * BR, width).astype(jnp.float32)
    weighted = quality * temp_recv.reshape(devices * capacity * BR, width).astype(jnp.float32)
    numerator = (prior_weight * background).at[row_list].add(weighted)
    denominator = jnp.full(background.shape, prior_weight, jnp.float32).at[row_list].add(quality)
    blended = numerator / denominator
    weights = gauss_taps()
    land_frac = land.astype(jnp.float32)
    raw_fields = jnp.concatenate([blended[None], reflect.astype(jnp.float32)], axis=0)
    rimmed = extended(raw_fields, (("tiles", 1), ("swath", 2)), RADIUS)
    smooth = blur(rimmed, weights)
    normal, right_side = fit(smooth, land_frac)
    normal, right_side = lax.psum((normal, right_side), ("tiles", "swath"))
    fit_coefs = solve_small(
        normal + ridge_term * jnp.eye(NBANDS + 1, dtype=jnp.float32), right_side
    )
    kernels = ((conv_first, bias_first), (conv_second, bias_second), (conv_third, bias_third))
    base_field, stacked = build_stack(raw_fields, smooth, land_frac, fit_coefs)
    hidden = stacked.astype(jnp.bfloat16)
    for layer_index in range(3):
        padded = extended(hidden, (("tiles", 1), ("swath", 2)), 1)
        hidden = convolve(padded, kernels[layer_index][0], kernels[layer_index][1]).astype(
            jnp.bfloat16
        )
    correction = jnp.einsum("c,chw->hw", head, hidden, preferred_element_type=jnp.float32)
    sharp_temp = base_field + land_frac * correction
    return (sharp_temp, fit_coefs)


def solution(mesh):
    placed = (
        P(("tiles", "swath"), None, None),
        P(("tiles", "swath"), None, None),
        P(("tiles", "swath")),
        P(("tiles", "swath")),
        P("tiles", "swath"),
        P(None, "tiles", "swath"),
        P("tiles", "swath"),
        P(),
        P(),
        P(),
        P(),
        P(),
        P(),
        P(),
    )
    return jax.shard_map(
        shards, mesh=mesh, in_specs=placed, out_specs=(P("tiles", "swath"), P()), check_vma=False
    )
```

profile of v0, /device:TPU:2, one launch (start us, length us, event | category | flops | bytes accessed | tf_op | source)
XLA Modules:
  0.0 1124.2 jit_solution(6668936687304427578)
XLA Ops:
  2.5 5.3 gather_fusion.1
  7.9 5.3 gather_fusion
  13.2 11.8 %select_select_fusion = (bf16[64,128,512]{2,1,0:T(8,128)(2,1)}, bf16[64,128,512]{2,1,0:T(8,128)(2,1)}) fusion(bf16[64,128,512]{2,1,0:T(8,128)(2,1)} %gather_fusion.1, pred[64]{0:T(512)(128)(4,1)S(1)} %compare_and_fusion, pred[64]{0:T(512)(128)(4,1)S(1)} %fusion.95, bf16[64,128,512]{2,1,0:T(8,128)(2,1)} %gather_fusion), kind=kLoop, calls=%fused_computation.37 | loop fusion | flops 16777216 | bytes 33554560 | tf_op jit(solution)/shard_map/jit(_where)/select_n | solution.py:159
  24.9 11.7 %copy.140 = bf16[64,128,512]{1,2,0:T(8,128)(2,1)} copy(bf16[64,128,512]{2,1,0:T(8,128)(2,1)} %get-tuple-element.184) | data formatting | bytes 16777216 | tf_op jit(solution)/shard_map/jit(_where)/select_n | solution.py:159
  36.6 12.0 %copy.141 = bf16[32,4,2,128,128]{4,3,2,1,0:T(8,128)(2,1)} copy(bf16[32,4,2,128,128]{3,4,1,2,0:T(8,128)(2,1)} %bitcast.170) | data formatting | bytes 16777216 | tf_op jit(solution)/shard_map/transpose | solution.py:163
  48.6 11.0 all-to-all-start
  60.2 157.7 %all-reduce.3 = (s32[1536]{0:T(1024)S(1)}, s32[1536]{0:T(1024)S(1)}) all-reduce(s32[1536]{0:T(1024)S(1)} %dynamic-update-slice.32, s32[1536]{0:T(1024)S(1)} %dynamic-update-slice.33), channel_id=1, replica_groups=mesh['tiles'=32,'swath'=4] {'tiles','swath'}, use_global_device_ids=true, to_apply=%add.1 | all-reduce | flops 3072 | bytes 24576
  218.8 11.9 %copy.142 = bf16[64,128,512]{1,2,0:T(8,128)(2,1)} copy(bf16[64,128,512]{2,1,0:T(8,128)(2,1)} %get-tuple-element.183) | data formatting | bytes 16777216 | tf_op jit(solution)/shard_map/jit(_where)/select_n | solution.py:159
  230.8 11.9 %copy.143 = bf16[32,4,2,128,128]{4,3,2,1,0:T(8,128)(2,1)} copy(bf16[32,4,2,128,128]{3,4,1,2,0:T(8,128)(2,1)} %bitcast.171) | data formatting | bytes 16777216 | tf_op jit(solution)/shard_map/transpose | solution.py:163
  243.4 5.5 all-to-all-start.1
  249.9 175.4 %scatter_custom_fusion.1 = f32[512,128]{1,0:T(8,128)S(1)} fusion(s32[32768]{0:T(1024)S(1)} %bitcast.182, bf16[32768,128]{1,0:T(8,128)(2,1)} %bitcast.11, f32[]{:T(128)} %constant.363.clone.1), kind=kCustom, calls=%fused_computation.8 | custom fusion | flops 8388608 | bytes 8650756 | tf_op jit(solution)/shard_map/scatter-add | solution.py:183
  425.3 158.8 %scatter_custom_fusion = f32[512,128]{1,0:T(8,128)S(1)} fusion(f32[512,128]{1,0:T(8,128)S(1)} %broadcast_multiply_fusion, s32[32768]{0:T(1024)S(1)} %bitcast.183, bf16[32768,128]{1,0:T(8,128)(2,1)} %bitcast.11, bf16[32768,128]{1,0:T(8,128)(2,1)} %bitcast.86), kind=kCustom, calls=%fused_computation.32 | custom fusion | flops 16777216 | bytes 17039360 | tf_op jit(solution)/shard_map/scatter-add | solution.py:182
  584.1 2.1 collective-permute-start
  586.2 5.6 collective-permute-start.1
  595.4 2.9 copy.144
  600.9 5.2 collective-permute-start.2
  609.9 2.7 copy.147
  612.6 5.0 pad_maximum_fusion
  617.6 35.7 %fusion.46 = f32[7,512,142]{2,1,0:T(8,128)} fusion(f32[7,526,142]{2,1,0:T(8,128)} %pad_maximum_fusion, f32[]{:T(128)} %bitcast.26, f32[]{:T(128)} %bitcast.25, f32[]{:T(128)} %bitcast.24, f32[]{:T(128)} %bitcast.23, f32[]{:T(128)} %bitcast.22, f32[]{:T(128)} %bitcast.21, f32[]{:T(128)} %bitcast.20, f32[]{:T(128)} %bitcast.19, f32[]{:T(128)} %bitcast.18, ...), kind=kLoop, calls=%fused_computation.54 | loop fusion | flops 14758912 | bytes 32571452 | tf_op jit(solution)/shard_map/add | solution.py:46
  653.3 35.0 %fusion.70 = f32[7,512,128]{2,1,0:T(8,128)S(1)} fusion(f32[7,512,142]{2,1,0:T(8,128)} %fusion.46, f32[]{:T(128)} %bitcast.26, f32[]{:T(128)} %bitcast.25, f32[]{:T(128)} %bitcast.24, f32[]{:T(128)} %bitcast.23, f32[]{:T(128)} %bitcast.22, f32[]{:T(128)} %bitcast.21, f32[]{:T(128)} %bitcast.20, f32[]{:T(128)} %bitcast.19, f32[]{:T(128)} %bitcast.18, ...), kind=kLoop, calls=%fused_computation.97 | loop fusion | flops 13303808 | bytes 29360188 | tf_op jit(solution)/shard_map/add | solution.py:49
  690.7 4.4 fusion.60
  695.2 4.6 fusion.84
  699.8 67.3 %all-reduce.4 = (f32[7]{0:T(128)S(1)}, f32[7,7]{1,0:T(8,128)S(1)}) all-reduce(f32[7]{0:T(128)S(1)} %fusion.84, f32[7,7]{1,0:T(8,128)S(1)} %fusion.60), channel_id=1, replica_groups=mesh['tiles'=32,'swath'=4] {'tiles','swath'}, use_global_device_ids=true, to_apply=%region_8.10 | all-reduce | flops 56 | bytes 448 | tf_op jit(solution)/shard_map/psum | solution.py:191
  793.0 4.1 fusion.64
  797.6 1.9 collective-permute-start.4
  799.5 5.8 collective-permute-start.5
  807.2 2.7 fusion.113
  810.0 2.1 copy.148
  812.1 2.2 collective-permute-start.6
  814.4 2.1 copy.149
  817.8 2.1 copy.150
  819.9 2.3 collective-permute-done.7
  822.2 1.9 copy.151
  824.1 7.3 maximum_bitcast_fusion
  831.3 8.3 copy.165
  839.6 3.5 pad.27.clone
  843.1 17.7 %copy.154 = bf16[16,514,1,8,17]{0,3,4,1,2:T(8,128)(2,1)} copy(bf16[16,514,1,8,17]{1,0,4,3,2:T(8,128)(2,1)} %bitcast.177) | data formatting | bytes 4473856 | tf_op jit(solution)/shard_map/conv_general_dilated | solution.py:100
  860.9 2.2 slice.597
  863.1 28.8 %broadcast_select_fusion.2 = f32[512,8,17,16]{3,1,2,0:T(8,128)} fusion(pred[8,17]{0,1:T(8,128)(4,1)S(1)} %copy-done.26, bf16[16,16,3,3]{1,0,3,2:T(8,128)(2,1)S(1)} %copy-done.21, bf16[16,514,1,7,2]{0,3,4,1,2:T(8,128)(2,1)S(1)} %slice.597, bf16[16,514,1,8,17]{0,3,4,1,2:T(8,128)(2,1)} %copy.154), kind=kOutput, calls=%fused_computation.31 | convolution fusion | flops 329478656 | bytes 6928392 | tf_op jit(solution)/shard_map/conv_general_dilated | solution.py:100
  891.8 22.1 %copy.155 = f32[512,8,17,16]{0,3,2,1:T(8,128)} copy(f32[512,8,17,16]{3,1,2,0:T(8,128)} %broadcast_select_fusion.2) | data formatting | bytes 8912896 | tf_op jit(solution)/shard_map/conv_general_dilated | solution.py:100
  914.0 2.9 fusion.45
  917.1 2.1 collective-permute-start.8
  919.3 5.8 collective-permute-start.9
  925.0 4.9 collective-permute-done.8
  931.8 2.7 collective-permute-start.10
  935.9 4.2 collective-permute-done.11
  940.2 1.9 maximum_bitcast_fusion.1
  943.8 17.7 %copy.157 = bf16[16,514,1,8,17]{0,3,4,1,2:T(8,128)(2,1)} copy(bf16[16,514,1,8,17]{1,0,4,3,2:T(8,128)(2,1)} %bitcast.178) | data formatting | bytes 4473856 | tf_op jit(solution)/shard_map/conv_general_dilated | solution.py:100
  961.5 2.2 slice.601
  963.7 28.8 %broadcast_select_fusion.1 = f32[512,8,17,16]{3,1,2,0:T(8,128)} fusion(pred[8,17]{0,1:T(8,128)(4,1)S(1)} %copy-done.26, bf16[16,16,3,3]{1,0,3,2:T(8,128)(2,1)S(1)} %copy-done.22, bf16[16,514,1,7,2]{0,3,4,1,2:T(8,128)(2,1)S(1)} %slice.601, bf16[16,514,1,8,17]{0,3,4,1,2:T(8,128)(2,1)} %copy.157), kind=kOutput, calls=%fused_computation.30 | convolution fusion | flops 329478656 | bytes 6928392 | tf_op jit(solution)/shard_map/conv_general_dilated | solution.py:100
  992.5 22.1 %copy.158 = f32[512,8,17,16]{0,3,2,1:T(8,128)} copy(f32[512,8,17,16]{3,1,2,0:T(8,128)} %broadcast_select_fusion.1) | data formatting | bytes 8912896 | tf_op jit(solution)/shard_map/conv_general_dilated | solution.py:100
  1014.6 2.9 fusion.42
  1017.8 1.9 collective-permute-start.12
  1019.7 5.8 collective-permute-start.13
  1025.5 4.9 collective-permute-done.12
  1032.2 3.8 collective-permute-start.14
  1037.6 4.1 collective-permute-done.15
  1041.7 1.9 maximum_bitcast_fusion.2
  1045.4 17.7 %copy.160 = bf16[16,514,1,8,17]{0,3,4,1,2:T(8,128)(2,1)} copy(bf16[16,514,1,8,17]{1,0,4,3,2:T(8,128)(2,1)} %bitcast.176) | data formatting | bytes 4473856 | tf_op jit(solution)/shard_map/conv_general_dilated | solution.py:100
  1063.1 2.2 slice.605
  1065.3 28.8 %broadcast_select_fusion = f32[512,8,17,16]{3,1,2,0:T(8,128)} fusion(pred[8,17]{0,1:T(8,128)(4,1)S(1)} %copy-done.26, bf16[16,16,3,3]{1,0,3,2:T(8,128)(2,1)S(1)} %copy-done.23, bf16[16,514,1,7,2]{0,3,4,1,2:T(8,128)(2,1)S(1)} %slice.605, bf16[16,514,1,8,17]{0,3,4,1,2:T(8,128)(2,1)} %copy.160), kind=kOutput, calls=%fused_computation.29 | convolution fusion | flops 329478656 | bytes 6928392 | tf_op jit(solution)/shard_map/conv_general_dilated | solution.py:100
  1094.1 22.3 %copy.161 = f32[512,8,17,16]{0,3,2,1:T(8,128)} copy(f32[512,8,17,16]{3,1,2,0:T(8,128)} %broadcast_select_fusion) | data formatting | bytes 8912896 | tf_op jit(solution)/shard_map/conv_general_dilated | solution.py:100
  1116.3 3.7 fusion.66
  1121.9 1.9 fusion.90
  (185 shorter events, 50.7 us)
Async XLA Ops:
  0.6 1.9 copy-start
  2.5 5.4 copy-start.2
  48.6 11.0 copy-start.24
  48.6 11.3 %copy-start.25 = (s32[12]{0:T(128)S(1)}, s32[12]{0:T(128)}, u32[]{:S(2)}) copy-start(s32[12]{0:T(128)} %param.45) | copy-start | bytes 148
  48.6 170.1 %copy-start.7 = (bf16[6,512,128]{2,1,0:T(8,128)(2,1)S(1)}, bf16[6,512,128]{2,1,0:T(8,128)(2,1)}, u32[]{:S(2)}) copy-start(bf16[6,512,128]{2,1,0:T(8,128)(2,1)} %param.47) | copy-start | bytes 2359300
  48.6 194.8 %all-to-all-start = ((bf16[128,2,128,128]{3,2,1,0:T(8,128)(2,1)}), bf16[128,2,128,128]{3,2,1,0:T(8,128)(2,1)}, u32[]{:S(2)}, u32[]{:S(2)}) async-start(bf16[128,2,128,128]{3,2,1,0:T(8,128)(2,1)} %bitcast.168), calls=%async_computation | async-start | bytes 16777216 | tf_op jit(solution)/shard_map/all_to_all | solution.py:167
  230.7 12.6 %copy-start.15 = (f32[512,128]{1,0:T(8,128)S(1)}, f32[512,128]{1,0:T(8,128)}, u32[]{:S(2)}) copy-start(f32[512,128]{1,0:T(8,128)} %param.46) | copy-start | bytes 786436
  243.4 5.6 copy-start.12
  243.4 181.8 %all-to-all-start.1 = ((bf16[128,2,128,128]{3,2,1,0:T(8,128)(2,1)}), bf16[128,2,128,128]{3,2,1,0:T(8,128)(2,1)}, u32[]{:S(2)}, u32[]{:S(2)}) async-start(bf16[128,2,128,128]{3,2,1,0:T(8,128)(2,1)} %bitcast.169), calls=%async_computation.1 | async-start | bytes 16777216 | tf_op jit(solution)/shard_map/all_to_all | solution.py:166
  584.1 9.3 copy-start.9
  584.1 8.4 collective-permute-start
  586.2 7.2 collective-permute-start.1
  599.6 10.3 collective-permute-start.3
  600.9 7.5 collective-permute-start.2
  653.3 35.0 %copy-start.8 = (bf16[6,512,128]{2,1,0:T(8,128)(2,1)S(1)}, bf16[6,512,128]{2,1,0:T(8,128)(2,1)}, u32[]{:S(2)}) copy-start(bf16[6,512,128]{2,1,0:T(8,128)(2,1)} %param.47) | copy-start | bytes 2359300
  688.3 2.4 copy-start.3
  688.3 2.4 copy-start.14
  690.7 4.5 slice-start
  695.1 102.0 %copy-start.4 = (f32[7,512,128]{2,1,0:T(8,128)S(1)}, f32[7,512,128]{2,1,0:T(8,128)}, u32[]{:S(2)}) copy-start(f32[7,512,128]{2,1,0:T(8,128)} %copy-done.3) | copy-start | bytes 5505028
  695.1 102.1 %copy-start.10 = (f32[1,512,128]{2,1,0:T(8,128)S(1)}, f32[1,512,128]{2,1,0:T(8,128)}, u32[]{:S(2)}) copy-start(f32[1,512,128]{2,1,0:T(8,128)} %copy-done.9) | copy-start | bytes 786436
  695.1 102.1 %copy-start.13 = (s32[512,128]{1,0:T(8,128)S(1)}, s32[512,128]{1,0:T(8,128)}, u32[]{:S(2)}) copy-start(s32[512,128]{1,0:T(8,128)} %param.48) | copy-start | bytes 786436
  793.0 12.3 %copy-start.20 = (f32[7]{0:T(128)}, f32[7]{0:T(128)S(1)}, u32[]{:S(2)}) copy-start(f32[7]{0:T(128)S(1)} %constant_dynamic-update-slice_fusion.1) | copy-start | bytes 88
  797.1 10.1 copy-start.11
  797.6 9.1 copy-start.6
  797.6 7.7 collective-permute-start.4
  799.5 7.1 collective-permute-start.5
  812.1 5.7 collective-permute-start.6
  816.5 5.7 collective-permute-start.7
  860.9 2.2 copy-start.21
  860.9 2.2 copy-start.26
  891.8 22.1 %copy-start.16 = (f32[16]{0:T(128)S(1)}, f32[16]{0:T(128)}, u32[]{:S(2)}) copy-start(f32[16]{0:T(128)} %param.50) | copy-start | bytes 196
  917.1 12.8 %collective-permute-start.8 = (bf16[16,1,128]{1,0,2:T(8,128)(2,1)S(1)}, bf16[16,1,128]{1,0,2:T(8,128)(2,1)S(1)}, u32[]{:S(2)}, u32[]{:S(2)}) collective-permute-start(bf16[16,1,128]{1,0,2:T(8,128)(2,1)S(1)} %get-tuple-element.173), channel_id=1, source_target_pairs={{0,4},{4,8},{8,12},{12,16},{16,20},{20,24},{24,28},{28,32},{32,36}... | collective-permute-start | bytes 12296 | tf_op jit(solution)/shard_map/ppermute | solution.py:25
  919.3 12.4 %collective-permute-start.9 = (bf16[16,1,128]{1,0,2:T(8,128)(2,1)S(1)}, bf16[16,1,128]{1,0,2:T(8,128)(2,1)S(1)}, u32[]{:S(2)}, u32[]{:S(2)}) collective-permute-start(bf16[16,1,128]{1,0,2:T(8,128)(2,1)S(1)} %get-tuple-element.174), channel_id=1, source_target_pairs={{4,0},{8,4},{12,8},{16,12},{20,16},{24,20},{28,24},{32,28},{36,32}... | collective-permute-start | bytes 12296 | tf_op jit(solution)/shard_map/ppermute | solution.py:27
  931.8 4.1 collective-permute-start.10
  934.5 5.7 collective-permute-start.11
  961.5 2.2 copy-start.22
  992.5 22.1 %copy-start.17 = (f32[16]{0:T(128)S(1)}, f32[16]{0:T(128)}, u32[]{:S(2)}) copy-start(f32[16]{0:T(128)} %param.52) | copy-start | bytes 196
  1017.8 12.6 %collective-permute-start.12 = (bf16[16,1,128]{1,0,2:T(8,128)(2,1)S(1)}, bf16[16,1,128]{1,0,2:T(8,128)(2,1)S(1)}, u32[]{:S(2)}, u32[]{:S(2)}) collective-permute-start(bf16[16,1,128]{1,0,2:T(8,128)(2,1)S(1)} %get-tuple-element.171), channel_id=1, source_target_pairs={{0,4},{4,8},{8,12},{12,16},{16,20},{20,24},{24,28},{28,32},{32,36}... | collective-permute-start | bytes 12296 | tf_op jit(solution)/shard_map/ppermute | solution.py:25
  1019.7 12.4 %collective-permute-start.13 = (bf16[16,1,128]{1,0,2:T(8,128)(2,1)S(1)}, bf16[16,1,128]{1,0,2:T(8,128)(2,1)S(1)}, u32[]{:S(2)}, u32[]{:S(2)}) collective-permute-start(bf16[16,1,128]{1,0,2:T(8,128)(2,1)S(1)} %get-tuple-element.172), channel_id=1, source_target_pairs={{4,0},{8,4},{12,8},{16,12},{20,16},{24,20},{28,24},{32,28},{36,32}... | collective-permute-start | bytes 12296 | tf_op jit(solution)/shard_map/ppermute | solution.py:27
  1032.2 5.4 collective-permute-start.14
  1036.1 5.7 collective-permute-start.15
  1063.1 2.2 copy-start.23
  1094.1 22.3 %copy-start.18 = (f32[16]{0:T(128)S(1)}, f32[16]{0:T(128)}, u32[]{:S(2)}) copy-start(f32[16]{0:T(128)} %param.54) | copy-start | bytes 196
  1094.1 22.3 %copy-start.19 = (bf16[16]{0:T(256)(128)(2,1)S(1)}, bf16[16]{0:T(256)(128)(2,1)}, u32[]{:S(2)}) copy-start(bf16[16]{0:T(256)(128)(2,1)} %param.55) | copy-start | bytes 100
  1094.1 29.6 %copy-start.1 = (bf16[12,128,512]{2,1,0:T(8,128)(2,1)S(1)}, bf16[12,128,512]{2,1,0:T(8,128)(2,1)}, u32[]{:S(2)}) copy-start(bf16[12,128,512]{2,1,0:T(8,128)(2,1)} %param.42) | copy-start | bytes 4718596
  1116.3 5.5 copy-start.5
where the time goes:
time: 1140 us; the launch traced here: 1120 us
  other arithmetic  455 us (40%)
  local copies, waits for them, and re-layouts  236 us (21%)
  blocking collectives  225 us (20%)
  matrix products  103 us (9%)
  starting transfers between devices  66.8 us (6%)
  waiting for transfers between devices  27.9 us (2%)
    scatter-add x1, other arithmetic, shards(): jnp.full(background.shape, prior_weight, jnp.float32).at[row_list]  175 us
    scatter-add x1, other arithmetic, shards(): numerator = (prior_weight * background).at[row_list].add(weighted)  159 us
    unnamed x1, blocking collectives  158 us
    conv_general_dilated x9, local copies, waits for them, and re-layouts, convolve(): lax.conv_general_dilated(field[None], kernel, (1, 1), 'VALID', dimension_...  126 us
    conv_general_dilated x3, matrix products, convolve(): lax.conv_general_dilated(field[None], kernel, (1, 1), 'VALID', dimension_...  86.3 us
    psum x1, blocking collectives, shards(): normal, right_side = lax.psum((normal, right_side), ('tiles', 'swath'))  67.3 us
    add x1, other arithmetic, blur(): across + weights[tap_index] * field[:, tap_index:tap_index + height, :]  35.7 us
    add x1, other arithmetic, blur(): result + weights[tap_index] * across[:, :, tap_index:tap_index + width]  35 us
  transfers between devices with their start and end apart: 18, of which 11 were waited for; matrix products, arithmetic and copies ran while one was open for 19% of the time, Pallas kernels for 0%

commit v1 on v0

v1 whole, which is shorter than its diff:
```python
import jax
import jax.numpy as jnp
import numpy as np
from jax import lax
from jax.experimental import pallas as pl
from jax.experimental.pallas import tpu as pltpu
from jax.sharding import PartitionSpec as P

TR = 512
BR = 128
RADIUS = 7
NBANDS = 6
CH = 16
NX = 4
NZ = 4
NY = 4
LANES = 128
HALO = 16
WIN = TR + 2 * HALO
ACC = WIN + 2 * HALO
QROWS = TR // NY
RQ = QROWS + 2 * HALO
COLS = NY * LANES
GROUPS = RQ // 8
KROWS = CH * 8 + 2 * CH
STRIP = 64
STEPS = 6
STRIPS = TR // STRIP

prior_weight = 0.5
ridge_term = 1.0
f32 = jnp.float32
bf16 = jnp.bfloat16
VMEM = pl.BlockSpec(memory_space=pltpu.VMEM)
SMEM = pl.BlockSpec(memory_space=pltpu.SMEM)
ANY = pl.BlockSpec(memory_space=pl.ANY)


def tile_id(x, z, c):
    return (x * NZ + z) * 2 + c


def along_y(k):
    return [(i, (i + k) % NY) for i in range(NY)]


def along_x(k):
    return [
        (tile_id(x, z, c), tile_id((x + k) % NX, z, c))
        for x in range(NX)
        for z in range(NZ)
        for c in range(2)
    ]


def along_z(k):
    return [
        (tile_id(x, z, c), tile_id(x, (z + k) % NZ, c))
        for x in range(NX)
        for z in range(NZ)
        for c in range(2)
    ]


core_pair = [(i, i ^ 1) for i in range(2 * NX * NZ)]


def call(kernel, outs, ins, scratch=(), flops=0, nbytes=0, name=None, grid=(), place=VMEM, alias={}):
    return pl.pallas_call(
        kernel,
        grid=grid,
        out_shape=outs,
        in_specs=ins,
        out_specs=place
        if isinstance(place, tuple)
        else jax.tree.map(lambda o: SMEM if o.shape == (NBANDS + 1,) else place, outs),
        scratch_shapes=list(scratch),
        input_output_aliases=alias,
        compiler_params=pltpu.CompilerParams(vmem_limit_bytes=56 * 1024 * 1024),
        cost_estimate=pl.CostEstimate(flops=flops, bytes_accessed=nbytes, transcendentals=0),
        name=name,
    )


def sds(shape, dtype):
    return jax.ShapeDtypeStruct(shape, dtype)


def add_blocks(meta, info, count, arrivals, add):
    c = info[2]
    for piece in range(8):
        arrivals[piece].wait()

        def body(j, carry, piece=piece):
            code = meta[piece, j]
            tile = code >> 9
            off = code & (TR - 1)
            mine = (tile & 1) == c

            @pl.when(mine)
            def _():
                add(piece, j, tile >> 1, off + 2 * HALO, 0, BR)

            @pl.when(jnp.logical_not(mine) & ((off > TR - BR - HALO) | (off < HALO)))
            def _():
                @pl.when((off > TR - BR - HALO) & (tile < 2 * NX * NZ - 1))
                def _():
                    add(piece, j, (tile + 1) >> 1, off - (TR - BR - HALO), BR - HALO, HALO)

                @pl.when((off < HALO) & (tile > 0))
                def _():
                    add(piece, j, (tile - 1) >> 1, off + 2 * HALO + TR, 0, HALO)

            return carry

        lax.fori_loop(0, count, body, 0, unroll=2)


def pack_kernel(info, dest, offset, temp, qual, *outs):
    s = info[3]
    count = temp.shape[0]
    lane = lax.broadcasted_iota(jnp.int32, (HALO, LANES), 1)
    row = lax.broadcasted_iota(jnp.int32, (HALO, LANES), 0)
    places = jnp.zeros((HALO, LANES), jnp.int32)
    for j in range(count):
        numbers = (dest[j], offset[j] >> 4, offset[j] & 15)
        for i, number in enumerate(numbers):
            places = jnp.where((lane == j) & (row == i), number, places)
    places = places.astype(f32).astype(bf16)
    for k, out in enumerate(outs):
        lanes = pl.ds(pl.multiple_of(lax.rem(s + k, NY) * LANES, LANES), LANES)
        for j in range(count):
            out[BR * j : BR * (j + 1), :] = qual[j, :, lanes]
            out[BR * (count + j) : BR * (count + j + 1), :] = temp[j, :, lanes]
        out[2 * count * BR :, :] = places

def scatter_kernel(info, *refs):
    pieces, outs = refs[0:8], refs[9:17]
    acc_n, acc_d, places, meta, sem, held, numbers, staged, in_sems, place_sems, out_sems = refs[17:]
    x, z = info[0], info[1]
    count = (pieces[0].shape[0] - HALO) // (2 * BR)
    small, large = [], []
    for i, piece in enumerate(pieces):
        tail = piece.at[pl.ds(2 * count * BR, HALO)]
        small.append(pltpu.make_async_copy(tail, numbers.at[i], place_sems.at[i]))
        small[i].start()
    for i, piece in enumerate(pieces):
        body = piece.at[pl.ds(0, 2 * count * BR)]
        large.append(pltpu.make_async_copy(body, held.at[i], in_sems.at[i]))
        large[i].start()
    for i in range(8):
        small[i].wait()
        number = numbers[i].astype(f32)
        code = number[0:1] * TR + number[1:2] * 16.0 + number[2:3]
        places[i : i + 1, :] = code.astype(jnp.int32)
    copy = pltpu.make_async_copy(places, meta, sem)
    copy.start()

    def clear(i, carry):
        acc_n[i] = jnp.zeros((ACC, LANES), f32)
        acc_d[i] = jnp.zeros((ACC, LANES), f32)
        return carry

    def add(piece, j, slot, start, row, rows):
        span = pl.ds(start, rows)
        at = pl.multiple_of(j * BR + row, HALO)
        q = held[piece, pl.ds(at, rows), :].astype(f32)
        t = held[piece, pl.ds(count * BR + at, rows), :].astype(f32)
        acc_d[slot, span, :] = acc_d[slot, span, :] + q
        acc_n[slot, span, :] = acc_n[slot, span, :] + q * t

    lax.fori_loop(0, NX * NZ, clear, 0)
    copy.wait()
    add_blocks(meta, info, count, large, add)
    leaving = []
    for kx in range(NX):
        for kz in range(NZ):
            slot = lax.rem(x + kx, NX) * NZ + lax.rem(z + kz, NZ)
            targets = (outs[kx].at[kz], outs[NX + kz].at[kx])
            for acc, target in zip((acc_n, acc_d), targets):
                i = len(leaving)
                staged[i] = acc[slot, HALO : HALO + WIN, :].astype(bf16)
                leaving.append(pltpu.make_async_copy(staged.at[i], target, out_sems.at[i]))
                leaving[i].start()
    for copy in leaving:
        copy.wait()


def scatter_scratch(rows):
    return [pltpu.VMEM((NX * NZ, ACC, LANES), f32)] * 2 + [
        pltpu.VMEM((8, LANES), jnp.int32),
        pltpu.SMEM((8, LANES), jnp.int32),
        pltpu.SemaphoreType.DMA,
        pltpu.VMEM((8, rows, LANES), bf16),
        pltpu.VMEM((8, HALO, LANES), bf16),
        pltpu.VMEM((2 * NX * NZ, WIN, LANES), bf16),
        pltpu.SemaphoreType.DMA((8,)),
        pltpu.SemaphoreType.DMA((8,)),
        pltpu.SemaphoreType.DMA((2 * NX * NZ,)),
    ]


def sum_kernel(a, b, c, d, *refs):
    for k, out in enumerate(refs[-4:]):
        out[...] = (a[k].astype(f32) + b[k].astype(f32)) + (c[k].astype(f32) + d[k].astype(f32))


def order_kernel(*refs):
    pass


def slab_kernel(reflect, land, first, last):
    lane = lax.broadcasted_iota(jnp.int32, (STRIP, LANES), 1)

    for plane in range(NBANDS + 1):
        sides = [jnp.zeros((STRIP, LANES), f32) for _ in range(2)]
        for i in range(STRIPS):
            rows = slice(STRIP * i, STRIP * (i + 1))
            cells = (reflect[plane, rows, :] if plane < NBANDS else land[rows, :]).astype(f32)
            for side, source in enumerate((0, LANES - HALO)):
                moved = pltpu.roll(cells, (HALO * i - source) % LANES, 1)
                sides[side] = jnp.where(lane >> 4 == i, moved, sides[side])
        first[plane] = sides[0].astype(bf16)
        last[plane] = sides[1].astype(bf16)


def beside_of(left, right, i):
    lane = lax.broadcasted_iota(jnp.int32, left.shape, 1)
    after = pltpu.roll(right, (-HALO * i) % LANES, 1)
    before = pltpu.roll(left, (HALO - HALO * i) % LANES, 1)
    return jnp.where(lane < HALO, after, jnp.where(lane < 2 * HALO, before, 0.0)).astype(bf16)


def edges_kernel(r0, r1, l0, l1, b0, b1, left, right, top, bottom):
    own = slice(0, LANES)
    sides = ((top, r0, l0, b0, 0, 0), (bottom, r1, l1, b1, STRIPS - 1, STRIP - HALO))
    for out, reflect, land, background, strip, row in sides:
        out[0:NBANDS, :, own] = reflect[...]
        out[NBANDS, :, own] = land[...].astype(f32).astype(bf16)
        high, low = split(background[...])
        out[NBANDS + 1, :, own] = high
        out[NBANDS + 2, :, own] = low
        for plane in range(NBANDS + 1):
            rows = slice(row, row + HALO)
            out[plane, :, LANES:] = beside_of(
                left[plane, rows, :].astype(f32), right[plane, rows, :].astype(f32), strip
            )
        for plane in range(NBANDS + 1, NBANDS + 3):
            out[plane, :, LANES:] = jnp.zeros((HALO, LANES), bf16)


def adjoint_kernel(
    reflect, land, above, below, left, right, row_h, row_l, col_h, col_l,
    adjoint, normal, window, beside, bands,
):
    for rows, edge in ((slice(0, HALO), above), (slice(HALO + TR, WIN), below)):
        window[:, rows, :] = edge[0 : NBANDS + 1, :, 0:LANES]
        beside[:, rows, :] = edge[0 : NBANDS + 1, :, LANES:]
    window[0:NBANDS, HALO : HALO + TR, :] = reflect[...]
    window[NBANDS, HALO : HALO + TR, :] = land[...].astype(f32).astype(bf16)

    def spread(plane, carry):
        before = left[plane].astype(f32)
        after = right[plane].astype(f32)
        for i in range(STRIPS):
            rows = slice(HALO + STRIP * i, HALO + STRIP * (i + 1))
            beside[plane, rows, :] = beside_of(before, after, i)
        return carry

    lax.fori_loop(0, NBANDS + 1, spread, 0)
    pairs = [(i, j) for i in range(NBANDS + 1) for j in range(i, NBANDS + 1)]
    own = slice(HALO, HALO + QROWS)

    def quarter(q, sums):
        rows = pl.ds(pl.multiple_of(QROWS * q, QROWS), RQ)

        def cells(plane):
            return jnp.concatenate([window[plane, rows, :], beside[plane, rows, :]], axis=1)

        land = cells(NBANDS).astype(f32)
        for band in range(NBANDS):
            x = cells(band)
            down = split(dot(row_h[...], x) + dot(row_l[...], x))
            bands[band] = dot3(down, (col_h[...], col_l[...]))
        for i in range(NBANDS + 1):
            value = split(land if i == 0 else land * bands[i - 1])
            down = split(dot3((row_h[own, :], row_l[own, :]), value))
            adjoint[i, pl.ds(pl.multiple_of(QROWS * q, QROWS), QROWS), :] = dot3(
                down, (col_h[:, 0:LANES], col_l[:, 0:LANES])
            )

        def step(g, sums):
            at = pl.multiple_of(HALO + 16 * g, 16)
            part = pl.ds(at, 16)
            mask = window[NBANDS, pl.ds(pl.multiple_of(QROWS * q + at, 16), 16), :].astype(f32)
            x = [None] + [bands[band, part, 0:LANES] for band in range(NBANDS)]
            mx = [mask] + [mask * x[i] for i in range(1, NBANDS + 1)]
            new = []
            for (i, j), total in zip(pairs, sums):
                v = mx[j] if i == 0 else mx[i] * x[j]
                new.append(total + (v[0:8] + v[8:16]))
            return tuple(new)

        return lax.fori_loop(0, QROWS // 16, step, sums)

    sums = lax.fori_loop(0, NY, quarter, tuple(jnp.zeros((8, LANES), f32) for _ in pairs))
    row = lax.broadcasted_iota(jnp.int32, (8, LANES), 0)
    lane = lax.broadcasted_iota(jnp.int32, (8, LANES), 1)
    result = jnp.zeros((8, LANES), f32)
    for (i, j), total in zip(pairs, sums):
        here = ((row == i) & (lane == j)) | ((row == j) & (lane == i))
        result = jnp.where(here, jnp.sum(total), result)
    normal[...] = result


def cut_kernel(window, after, out):
    for k in range(NY):
        out[k] = window[:, QROWS * k : QROWS * k + RQ, :]


def blend_kernel(info, *refs):
    nums, dens = refs[0:4], refs[4:8]
    background, above, below = refs[8:11]
    adjoint, normal = refs[11], refs[12]
    outs, field = refs[13:17], refs[17]
    first, last, s = info[4], info[5], info[3]
    num = nums[0][...].astype(f32)
    den = dens[0][...].astype(f32)
    for n in nums[1:]:
        num = num + n[...].astype(f32)
    for d in dens[1:]:
        den = den + d[...].astype(f32)
    ends = [
        edge[NBANDS + 1, :, 0:LANES].astype(f32) + edge[NBANDS + 2, :, 0:LANES].astype(f32) for edge in (above, below)
    ]
    prior = jnp.concatenate([ends[0], background[...], ends[1]], axis=0)
    row = lax.broadcasted_iota(jnp.int32, (WIN, LANES), 0)
    inside = (row >= HALO * first) & (row < WIN - HALO * last)
    blended = (prior_weight * prior + num) / (prior_weight + den)
    field[...] = jnp.where(inside, blended, 0.0)
    totals = [jnp.zeros((8, LANES), f32) for _ in range(NBANDS + 1)]

    def step(g, totals):
        cells = field[pl.ds(pl.multiple_of(HALO + 16 * g, 16), 16), :]
        rows = pl.ds(pl.multiple_of(16 * g, 16), 16)
        new = []
        for i, total in enumerate(totals):
            v = cells * adjoint[i, rows, :]
            new.append(total + (v[0:8] + v[8:16]))
        return tuple(new)

    totals = lax.fori_loop(0, TR // 16, step, tuple(totals))
    row = lax.broadcasted_iota(jnp.int32, (8, LANES), 0)
    lane = lax.broadcasted_iota(jnp.int32, (8, LANES), 1)
    sums = normal[...]
    for i, total in enumerate(totals):
        sums = jnp.where((row == i) & (lane == NBANDS + 1), jnp.sum(total), sums)
    for k, out in enumerate(outs):
        start = pl.multiple_of(lax.rem(s + k, NY) * QROWS, QROWS)
        out[0:RQ, :] = field[pl.ds(start, RQ), :]
        out[RQ:, :] = sums


def merge_kernel(b0, b1, b2, b3, out):
    total = (b0[...] + b2[...]) + (b1[...] + b3[...])
    out[...] = jnp.broadcast_to(total[None], out.shape)


def lane_place(s, k):
    return pl.ds(pl.multiple_of(lax.rem(s + NY - k, NY) * LANES, LANES), LANES)


def split(v):
    high = v.astype(bf16)
    return high, (v - high.astype(f32)).astype(bf16)


def dot(a, b):
    return jnp.dot(a, b, preferred_element_type=f32)


def dot3(a, b):
    return dot(a[0], b[0]) + (dot(a[0], b[1]) + dot(a[1], b[0]))


def row_inside(info, rows):
    row = lax.broadcasted_iota(jnp.int32, (rows, 1), 0)
    return (row >= HALO * info[6]) & (row < rows - HALO * info[7])


def bands_kernel(info, pieces, row_h, row_l, col_h, col_l, turn, fields, coarse, raw):
    for k in range(NY):
        raw[:, :, LANES * k : LANES * (k + 1)] = pieces[k]
    inside = row_inside(info, RQ)
    for band in range(NBANDS + 1):
        cells = raw[band]
        fields[band] = dot(cells, turn[...]).astype(bf16)
        if band < NBANDS:
            down = split(dot(row_h[...], cells) + dot(row_l[...], cells))
            coarse[band] = jnp.where(inside, dot3(down, (col_h[...], col_l[...])), 0.0)


def write(slot, start, value):
    rows = slice(start, start + value.shape[0])
    lane = lax.broadcasted_iota(jnp.int32, (value.shape[0], LANES), 1)
    for t in range(NY):
        slot[t + 1, rows, :] = value[:, LANES * t : LANES * (t + 1)]
    before = pltpu.roll(value[:, 3 * LANES :], 1, 1)
    after = pltpu.roll(value[:, :LANES], LANES - 1, 1)
    slot[0, rows, :] = jnp.where(lane > 0, before, 0.0)
    slot[5, rows, :] = jnp.where(lane < LANES - 1, after, 0.0)


def put(slot, g, hidden):
    for t in range(6):
        part = slice(LANES * t, LANES * (t + 1))
        hidden[g, 0:128, part] = slot[t].astype(bf16)
        hidden[g + 1, 128:144, part] = slot[t, pl.ds(7, CH, stride=8), :].astype(bf16)
        hidden[g - 1, 144:160, part] = slot[t, pl.ds(0, CH, stride=8), :].astype(bf16)


def clear_ends(hidden):
    zero_rows = jnp.zeros((CH, 6 * LANES), bf16)
    hidden[1, 128:144, :] = zero_rows
    hidden[GROUPS - 2, 144:160, :] = zero_rows


def assemble_kernel(
    info, b0, b1, b2, b3, row_h, row_l, col_h, col_l, turn, fields_in, bands_in,
    coarse, hidden_out, natural, blended, group, fields, bands, hidden, in_sems, out_sems,
):
    s = info[3]
    arrays = ((fields_in, fields), (bands_in, bands))
    copies = [pltpu.make_async_copy(a, b, in_sems.at[i]) for i, (a, b) in enumerate(arrays)]
    for copy in copies:
        copy.start()
    for k, piece in enumerate((b0, b1, b2, b3)):
        natural[:, lane_place(s, k)] = piece[0:RQ, :]
    high, low = split(natural[...])
    down = split(dot3((row_h[...], row_l[...]), (high, low)))
    coarse[...] = jnp.where(
        row_inside(info, RQ), dot3(down, (col_h[...], col_l[...])), 0.0
    )
    blended[...] = dot(high, turn[...])
    clear_ends(hidden)
    for copy in copies:
        copy.wait()

    def leave(m):
        part = pl.ds(2 * m - 1, 2)
        return pltpu.make_async_copy(hidden.at[part], hidden_out.at[part], out_sems.at[m])

    def step(m, carry):
        rows = pl.ds(pl.multiple_of(16 * m, 16), 16)
        values = [jnp.zeros((16, COLS), f32), blended[rows, :], coarse[rows, :]]
        values.append(fields[NBANDS, rows, :].astype(f32))
        values += [fields[band, rows, :].astype(f32) for band in range(NBANDS)]
        values += [bands[band, rows, :] for band in range(NBANDS)]
        for half in range(2):
            g = 2 * m + half
            for channel, value in enumerate(values):
                write(group.at[half], 8 * channel, value[8 * half : 8 * half + 8])

            @pl.when((g >= 1) & (g <= GROUPS - 2))
            def _():
                put(group.at[half], g, hidden)

        @pl.when(m >= 1)
        def _():
            leave(m).start()

        return carry

    lax.fori_loop(0, GROUPS // 2, step, 0)
    for m in range(1, GROUPS // 2):
        leave(m).wait()


def assemble_scratch():
    return [
        pltpu.VMEM((RQ, COLS), f32),
        pltpu.VMEM((RQ, COLS), f32),
        pltpu.VMEM((2, 6, CH * 8, LANES), f32),
        pltpu.VMEM((NBANDS + 1, RQ, COLS), bf16),
        pltpu.VMEM((NBANDS, RQ, COLS), f32),
        pltpu.VMEM((GROUPS, KROWS, 6 * LANES), bf16),
        pltpu.SemaphoreType.DMA((2,)),
        pltpu.SemaphoreType.DMA((GROUPS // 2,)),
    ]


def solve(sums):
    row = lax.broadcasted_iota(jnp.int32, (8, LANES), 0)
    lane = lax.broadcasted_iota(jnp.int32, (8, LANES), 1)
    work = sums + jnp.where((row == lane) & (row <= NBANDS), ridge_term, 0.0)
    for pivot in range(NBANDS + 1):
        pivot_row = work[pivot : pivot + 1, :]
        pivot_value = jnp.sum(jnp.where(lane[0:1] == pivot, pivot_row, 0.0), axis=1, keepdims=True)
        scaled = pivot_row / pivot_value
        factor = jnp.sum(jnp.where(lane == pivot, work, 0.0), axis=1, keepdims=True)
        work = jnp.where(row == pivot, scaled, work - factor * scaled)
    picked = jnp.where(lane == NBANDS + 1, work, 0.0)
    return [jnp.sum(picked[i : i + 1, :]) for i in range(NBANDS + 1)]


def main_kernel(
    info, head, sums, coarse_in, fields_in, bands_in, kernels, biases, turn_back_in, stacked_in,
    o0, o1, o2, o3, fit_out, first_h, second_h, group, base, result,
    coarse, fields, bands, turn_back, stacked, sems, stack_sems,
):
    s = info[3]
    arrays = ((coarse_in, coarse), (fields_in, fields), (bands_in, bands))
    copies = [pltpu.make_async_copy(a, b, sems.at[i]) for i, (a, b) in enumerate(arrays)]
    for copy in copies:
        copy.start()
    steps = STEPS

    def stack_copy(i):
        part = pl.ds(1 + steps * i, steps)
        return pltpu.make_async_copy(stacked_in.at[part], stacked.at[part], stack_sems.at[i])

    for i in range((GROUPS - 2) // steps):
        stack_copy(i).start()
    turn_copy = pltpu.make_async_copy(turn_back_in, turn_back, sems.at[3])
    turn_copy.start()
    coefs = solve(jnp.sum(sums[...], axis=0))
    for i in range(NBANDS + 1):
        fit_out[i] = coefs[i]
    for copy in copies:
        copy.wait()
    clear_ends(first_h)
    clear_ends(second_h)

    def start(m, carry):
        rows = pl.ds(pl.multiple_of(16 * m, 16), 16)
        value = coarse[rows, :]
        for band in range(NBANDS):
            value = value + coefs[band + 1] * (
                fields[band, rows, :].astype(f32) - bands[band, rows, :]
            )
        lane = lax.broadcasted_iota(jnp.int32, (16, LANES), 1)
        base[rows, LANES : 5 * LANES] = value
        base[rows, 0:LANES] = jnp.where(lane > 0, pltpu.roll(value[:, 3 * LANES :], 1, 1), 0.0)
        base[rows, 5 * LANES :] = jnp.where(
            lane < LANES - 1, pltpu.roll(value[:, :LANES], LANES - 1, 1), 0.0
        )
        return carry

    lax.fori_loop(0, GROUPS // 2, start, 0)
    edge_row = lax.broadcasted_iota(jnp.int32, (CH, 6 * LANES), 0) == 0

    def with_base(g):
        own = stacked[g, 0:16, :].astype(f32)
        at = pl.multiple_of(8 * g, 8)
        own = jnp.concatenate([base[pl.ds(at, 8), :], own[8:16]], axis=0).astype(bf16)
        above = jnp.where(
            edge_row, base[pl.ds(8 * g - 1, 1), :], stacked[g, 128:144, :].astype(f32)
        )
        below = jnp.where(
            edge_row, base[pl.ds(8 * g + 8, 1), :], stacked[g, 144:160, :].astype(f32)
        )
        return jnp.concatenate(
            [own, stacked[g, 16:128, :], above.astype(bf16), below.astype(bf16)], axis=0
        )

    def convolved(layer, cells):
        spans = [slice(LANES * b, LANES * (b + 4)) for b in range(3)]
        taps = jnp.concatenate(
            [cells[0:128, span] for span in spans] + [cells[128:160, span] for span in spans],
            axis=0,
        )
        bias = jnp.concatenate([biases[layer]] * NY, axis=1)
        return jnp.maximum(dot(kernels[layer], taps) + bias, 0.0)

    for layer, following in enumerate((first_h, second_h)):

        def body(i, carry, layer=layer, following=following):
            if layer == 0:
                stack_copy(i).wait()
            for u in range(steps):
                g = 1 + steps * i + u
                cells = with_base(g) if layer == 0 else first_h[g]
                outside = ((g == 1) & (info[6] == 1)) | ((g == GROUPS - 2) & (info[7] == 1))
                keep = jnp.where(outside, 0.0, 1.0)
                write(group.at[u], 0, convolved(layer, cells) * keep)
                put(group.at[u], g, following)
            return carry

        lax.fori_loop(0, (GROUPS - 2) // steps, body, 0)

    def last(i, carry):
        mask = fields[NBANDS, pl.ds(pl.multiple_of(HALO + 32 * i, 32), 32), :].astype(f32)
        for u in range(4):
            g = 2 + 4 * i + u
            third = convolved(2, second_h[g]).astype(bf16).astype(f32)
            total = head[0] * third[0:8]
            for channel in range(1, CH):
                total = total + head[channel] * third[8 * channel : 8 * channel + 8]
            rows = pl.ds(pl.multiple_of(8 * g, 8), 8)
            out_rows = pl.ds(pl.multiple_of(8 * g - HALO, 8), 8)
            result[out_rows, :] = (
                base[rows, LANES : 5 * LANES] + mask[8 * u : 8 * u + 8] * total
            )
        return carry

    lax.fori_loop(0, QROWS // 32, last, 0)
    turn_copy.wait()
    high, low = split(result[...])
    result[...] = dot(high, turn_back[...]) + dot(low, turn_back[...])
    for k, out in enumerate((o0, o1, o2, o3)):
        out[...] = result[:, pl.ds(pl.multiple_of(lax.rem(s + k, NY) * LANES, LANES), LANES)]


def main_scratch():
    hidden = pltpu.VMEM((GROUPS, KROWS, 6 * LANES), bf16)
    return [
        hidden,
        hidden,
        pltpu.VMEM((STEPS, 6, CH * 8, LANES), f32),
        pltpu.VMEM((RQ, 6 * LANES), f32),
        pltpu.VMEM((QROWS, COLS), f32),
        pltpu.VMEM((RQ, COLS), f32),
        pltpu.VMEM((NBANDS + 1, RQ, COLS), bf16),
        pltpu.VMEM((NBANDS, RQ, COLS), f32),
        pltpu.VMEM((COLS, COLS), bf16),
        hidden,
        pltpu.SemaphoreType.DMA((4,)),
        pltpu.SemaphoreType.DMA(((GROUPS - 2) // STEPS,)),
    ]


def join_kernel(info, o0, o1, o2, o3, out):
    s = info[3]
    for k, piece in enumerate((o0, o1, o2, o3)):
        start = pl.multiple_of(lax.rem(s + NY - k, NY) * QROWS, QROWS)
        out[pl.ds(start, QROWS), :] = piece[...]


def band_matrix(rows, columns):
    offsets = np.arange(2 * RADIUS + 1) - RADIUS
    norm = np.sum(np.exp(-0.125 * offsets**2))
    apart = rows[:, None] - columns[None, :]
    weights = np.where(np.abs(apart) <= RADIUS, np.exp(-0.125 * apart**2) / norm, 0.0)
    high = weights.astype(bf16)
    return jnp.asarray(high), jnp.asarray((weights - high.astype(np.float64)).astype(bf16))


def matrices_kernel(taps, bias, kernels, biases):
    def iota(size, axis):
        return lax.broadcasted_iota(jnp.int32, (size, size), axis)

    tall = (CH * 8, CH)
    spread_rows = (
        lax.broadcasted_iota(jnp.int32, tall, 0) >> 3 == lax.broadcasted_iota(jnp.int32, tall, 1)
    )
    spread_rows = jnp.where(spread_rows, 1.0, 0.0).astype(bf16)
    wide = (CH, CH * 8)
    channel, lane = (lax.broadcasted_iota(jnp.int32, wide, a) for a in range(2))
    spread_lanes = jnp.where(lane >> 3 == channel, 1.0, 0.0).astype(bf16)
    r, l = iota(CH * 8, 0), iota(CH * 8, 1)
    up = (l & 7) - (r & 7)
    for layer in range(3):
        halo = jnp.zeros((CH * 8, CH * 8), f32)
        for b in range(3):
            own = jnp.zeros((CH * 8, CH * 8), f32)
            for a in range(3):
                column = dot(spread_rows, taps[layer, a, b]).astype(bf16)
                own = jnp.where(up == a - 1, dot(column, spread_lanes), own)
                if a == 1:
                    continue
                at = 32 * b + (0 if a == 0 else CH)
                placed = jnp.where(lane == channel + at, 1.0, 0.0).astype(bf16)
                halo = halo + jnp.where((r & 7) == (0 if a == 0 else 7), dot(column, placed), 0.0)
            kernels[layer, :, 128 * b : 128 * b + 128] = own.astype(bf16)
        kernels[layer, :, 384:480] = halo[:, 0:96].astype(bf16)
        for o in range(CH):
            biases[layer, 8 * o : 8 * o + 8, :] = jnp.broadcast_to(
                bias[CH * layer + o : CH * layer + o + 1, :], (8, LANES)
            )


def exchange(pieces, axis, route):
    return [pieces[0]] + [lax.ppermute(pieces[k], axis, route(k)) for k in range(1, 4)]


def shards(
    blk_temp, blk_qual, dest_tile, blk_offset, background, reflect, land,
    conv_first, bias_first, conv_second, bias_second, conv_third, bias_third, head,
):
    tile = lax.axis_index("tiles")
    s = lax.axis_index("swath")
    tiles = lax.axis_size("tiles")
    x, z, c = tile // (2 * NZ), (tile // 2) % NZ, tile % 2
    first = tile == 0
    last = tile == tiles - 1
    info = jnp.stack(
        [x, z, c, s, first, last, first & (s == 0), last & (s == NY - 1)]
    ).astype(jnp.int32)

    count = blk_temp.shape[0]
    down = [(i, i + 1) for i in range(tiles - 1)]
    up = [(i + 1, i) for i in range(tiles - 1)]

    def edge(last_rows):
        at = TR // HALO - 1 if last_rows else 0
        return [
            pl.BlockSpec((NBANDS, HALO, LANES), lambda i: (0, at, 0)),
            pl.BlockSpec((HALO, LANES), lambda i: (at, 0)),
            pl.BlockSpec((HALO, LANES), lambda i: (at, 0)),
        ]

    edges = [spec for pair in zip(edge(False), edge(True)) for spec in pair]
    row_h, row_l = band_matrix(np.arange(RQ), np.arange(RQ))
    natural = np.arange(COLS)
    place = NY * (natural % LANES) + natural // LANES
    col_h, col_l = band_matrix(natural, place)
    turn = jnp.asarray((natural[:, None] == place[None, :]).astype(bf16))
    turn_back = jnp.asarray((place[:, None] == natural[None, :]).astype(bf16))
    lanes = np.arange(2 * LANES)
    spot = np.where(lanes < LANES + HALO, lanes, lanes - LANES - 2 * HALO)
    spot = np.where(lanes < LANES + 2 * HALO, spot, 1000 * lanes)
    near_h, near_l = band_matrix(spot, spot)

    strip = sds((NBANDS + 1, STRIP, LANES), bf16)
    first_columns, last_columns = call(slab_kernel, (strip, strip), [VMEM] * 2, name="slab")(
        reflect, land
    )
    from_left = lax.ppermute(last_columns, "swath", [(i, i + 1) for i in range(NY - 1)])
    from_right = lax.ppermute(first_columns, "swath", [(i + 1, i) for i in range(NY - 1)])
    packed = call(
        pack_kernel,
        (sds((2 * count * BR + HALO, LANES), bf16),) * 4,
        [SMEM] * 3 + [VMEM] * 2,
        name="pack",
    )(info, dest_tile, blk_offset, blk_temp, blk_qual)
    block = sds(packed[0].shape, bf16)
    packed = tuple(packed[0:1]) + tuple(call(
        order_kernel, (block,) * 3, [ANY] * 5, place=ANY, alias={0: 0, 1: 1, 2: 2}, name="order"
    )(*packed[1:], from_left, from_right))
    edge_rows = sds((NBANDS + 3, HALO, 2 * LANES), bf16)
    top, bottom = call(
        edges_kernel, (edge_rows,) * 2, edges + [VMEM] * 2, grid=(1,), name="edges"
    )(reflect, reflect, land, land, background, background, from_left, from_right)
    above = lax.ppermute(bottom, "tiles", down)
    below = lax.ppermute(top, "tiles", up)

    adjoint, normal, window = call(
        adjoint_kernel,
        (
            sds((NBANDS + 1, TR, LANES), f32),
            sds((8, LANES), f32),
            sds((NBANDS + 1, WIN, LANES), bf16),
        ),
        [VMEM] * 10,
        scratch=[
            pltpu.VMEM((NBANDS + 1, WIN, LANES), bf16),
            pltpu.VMEM((NBANDS, RQ, 2 * LANES), f32),
        ],
        name="adjoint",
    )(reflect, land, above, below, from_left, from_right, row_h, row_l, near_h, near_l)
    taps = jnp.transpose(jnp.stack([conv_first, conv_second, conv_third]), (0, 3, 4, 1, 2))
    bias = jnp.concatenate([bias_first, bias_second, bias_third])
    kernels, biases = call(
        matrices_kernel,
        (sds((3, CH * 8, 3 * KROWS), bf16), sds((3, CH * 8, LANES), f32)),
        [VMEM] * 2,
        name="matrices",
    )(taps, jnp.broadcast_to(bias[:, None], (3 * CH, LANES)))
    weights = head.astype(f32)

    chip = exchange(packed, "swath", along_y)
    chip[1] = call(
        order_kernel, (block,), [ANY] * 3, place=ANY, alias={0: 0}, name="order"
    )(chip[1], adjoint, kernels)[0]
    chip = chip + [lax.ppermute(p, "tiles", core_pair) for p in chip]

    cut = call(
        cut_kernel,
        sds((NY, NBANDS + 1, RQ, LANES), bf16),
        [VMEM] + [ANY],
        name="cut",
    )(window, chip[2])
    pieces = lax.all_to_all(cut, "swath", split_axis=0, concat_axis=0, tiled=True)
    fields, bands = call(
        bands_kernel,
        (sds((NBANDS + 1, RQ, COLS), bf16), sds((NBANDS, RQ, COLS), f32)),
        [SMEM] + [VMEM] * 6,
        scratch=[pltpu.VMEM((NBANDS + 1, RQ, COLS), bf16)],
        flops=2 * 6 * 160 * 512 * (320 + 1536),
        nbytes=10 << 20,
        name="bands",
    )(info, pieces, row_h, row_l, col_h, col_l, turn)
    part = sds((4, WIN, LANES), bf16)
    routed = call(
        scatter_kernel,
        (part,) * 8,
        [SMEM] + [ANY] * 9,
        scratch=scatter_scratch(2 * count * BR),
        place=ANY,
        flops=96 * 128 * 128 * 8,
        nbytes=12 << 20,
        name="scatter",
    )(info, *chip, cut)
    nums = exchange(routed[0:4], "tiles", along_x)
    dens = exchange(routed[4:8], "tiles", along_z)

    one = sds((WIN, LANES), f32)
    summed = call(sum_kernel, (one,) * 4, [VMEM] * 4 + [ANY], nbytes=3 << 20, name="add")
    nums = summed(*nums, fields)
    dens = summed(*dens, fields)
    nums = exchange(nums, "tiles", along_z)
    dens = exchange(dens, "tiles", along_x)
    rows = call(
        blend_kernel,
        (sds((RQ + 8, LANES), f32),) * 4,
        [SMEM] + [VMEM] * 13,
        scratch=[pltpu.VMEM((WIN, LANES), f32)],
        nbytes=3 << 20,
        name="blend",
    )(info, *nums, *dens, background, above, below, adjoint, normal)
    rows = exchange(rows, "swath", along_y)
    sums = call(
        merge_kernel,
        sds((tiles, 8, LANES), f32),
        [pl.BlockSpec((8, LANES), lambda i: (RQ // 8, 0))] * 4,
        grid=(1,),
        name="merge",
    )(*rows)
    sums = lax.all_to_all(sums, "tiles", split_axis=0, concat_axis=0, tiled=True)
    coarse, stacked = call(
        assemble_kernel,
        (sds((RQ, COLS), f32), sds((GROUPS, KROWS, 6 * LANES), bf16)),
        [SMEM] + [VMEM] * 9 + [ANY] * 2,
        scratch=assemble_scratch(),
        place=(VMEM, ANY),
        flops=2 * 160 * 512 * (480 + 1536),
        nbytes=8 << 20,
        name="assemble",
    )(info, *rows, row_h, row_l, col_h, col_l, turn, fields, bands)
    *sharp, fit_coefs = call(
        main_kernel,
        (sds((QROWS, LANES), f32),) * 4 + (sds((NBANDS + 1,), f32),),
        [SMEM, SMEM, VMEM] + [ANY] * 3 + [VMEM] * 2 + [ANY] * 2,
        scratch=main_scratch(),
        flops=3 * 18 * 2 * 384 * 160 * 512,
        nbytes=8 << 20,
        name="convolve",
    )(info, weights, sums, coarse, fields, bands, kernels, biases, turn_back, stacked)
    sharp = exchange(sharp, "swath", along_y)
    out = call(join_kernel, sds((TR, LANES), f32), [SMEM] + [VMEM] * 4, name="join")(info, *sharp)
    return out, fit_coefs


def solution(mesh):
    placed = (
        P(("tiles", "swath"), None, None),
        P(("tiles", "swath"), None, None),
        P(("tiles", "swath")),
        P(("tiles", "swath")),
        P("tiles", "swath"),
        P(None, "tiles", "swath"),
        P("tiles", "swath"),
        P(),
        P(),
        P(),
        P(),
        P(),
        P(),
        P(),
    )
    return jax.shard_map(
        shards, mesh=mesh, in_specs=placed, out_specs=(P("tiles", "swath"), P()), check_vma=False
    )
```

time: 1140 us -> 185 us (0.16); the launches traced: 1120 us -> 184 us
  other arithmetic: 455 us -> 1.26 us
  local copies, waits for them, and re-layouts: 236 us -> 10.5 us
  blocking collectives: 225 us -> 0 us
  matrix products: 103 us -> 0 us
  Pallas kernels: 0 us -> 75.6 us
    scatter-add x2 -> x0, other arithmetic: 334 us -> none  [the longest x1 175 us: shards(): jnp.full(background.shape, prior_weight, jnp.float32).at[row_list]]
    unnamed x1 -> x0, blocking collectives: 158 us -> none
    conv_general_dilated x9 -> x0, local copies, waits for them, and re-layouts: 126 us -> none  [convolve(): lax.conv_general_dilated(field[None], kernel, (1, 1), 'VALID', dimension_...]
    conv_general_dilated x3 -> x0, matrix products: 86.3 us -> none  [convolve(): lax.conv_general_dilated(field[None], kernel, (1, 1), 'VALID', dimension_...]
    pallas_call x0 -> x17, Pallas kernels: none -> 75.6 us  [the longest x1 12.8 us: shards(): call(adjoint_kernel, (sds((NBANDS + 1, TR, LANES), f32), sds((8, LANES),...]
    add x7 -> x0, other arithmetic: 73.3 us -> none  [the longest x1 35.7 us: blur(): across + weights[tap_index] * field[:, tap_index:tap_index + height, :]]
    psum x1 -> x0, blocking collectives: 67.3 us -> none  [shards(): normal, right_side = lax.psum((normal, right_side), ('tiles', 'swath'))]
    transpose x2 -> x0, local copies, waits for them, and re-layouts: 23.9 us -> none  [pack(): jnp.transpose(chosen, (0, 3, 1, 2, 4)).reshape(devices, capacity, BR, width)]
  transfers between devices with their start and end apart: 18 -> 31, of which waited for: 11 -> 11; matrix products, arithmetic and copies ran while one was open for 19% -> 1% of each run, Pallas kernels for 0% -> 30%
where the time goes in v1:
time: 185 us; the launch traced here: 184 us
  Pallas kernels  75.6 us (41%)
  starting transfers between devices  68 us (37%)
  waiting for transfers between devices  27.5 us (15%)
  local copies, waits for them, and re-layouts  10.5 us (6%)
    ppermute x21, starting transfers between devices, exchange(): lax.ppermute(pieces[k], axis, route(k))  43.1 us
    ppermute x21, waiting for transfers between devices, exchange(): lax.ppermute(pieces[k], axis, route(k))  26.8 us
    pallas_call x1, Pallas kernels, shards(): call(adjoint_kernel, (sds((NBANDS + 1, TR, LANES), f32), sds((8, LANES),...  12.8 us
    pallas_call x1, Pallas kernels, shards(): call(main_kernel, (sds((QROWS, LANES), f32),) * 4 + (sds((NBANDS + 1,), f...  12.1 us
    unnamed x66, local copies, waits for them, and re-layouts  9.1 us
    pallas_call x1, Pallas kernels, shards(): call(scatter_kernel, (part,) * 8, [SMEM] + [ANY] * 9, scratch=scatter_scr...  9.02 us
    all_to_all x1, starting transfers between devices, shards(): lax.all_to_all(sums, 'tiles', split_axis=0, concat_axis=0, tiled=True)  8.88 us
    pallas_call x1, Pallas kernels, shards(): call(assemble_kernel, (sds((RQ, COLS), f32), sds((GROUPS, KROWS, 6 * LANE...  7.97 us
  transfers between devices with their start and end apart: 31, of which 11 were waited for; matrix products, arithmetic and copies ran while one was open for 1% of the time, Pallas kernels for 30%

profile of v1, /device:TPU:2, one launch (start us, length us, event | category | flops | bytes accessed | tf_op | source)
XLA Modules:
  0.0 183.9 jit_solution(12190078892677734968)
XLA Ops:
  0.6 2.4 %slab.1 = (bf16[7,64,128]{2,1,0:T(8,128)(2,1)}, bf16[7,64,128]{2,1,0:T(8,128)(2,1)}) custom-call(bf16[6,512,128]{2,1,0:T(8,128)(2,1)} %reflect.3, s32[512,128]{1,0:T(8,128)} %land.3), custom_call_target="tpu_custom_call" | custom-call | tf_op jit(solution)/shard_map/slab/pallas_call | solution.py:725
  3.0 3.5 %collective-permute-start = (bf16[7,64,128]{2,1,0:T(8,128)(2,1)}, bf16[7,64,128]{2,1,0:T(8,128)(2,1)S(1)}, u32[]{:S(2)}, u32[]{:S(2)}) collective-permute-start(bf16[7,64,128]{2,1,0:T(8,128)(2,1)} %get-tuple-element.51), channel_id=1, source_target_pairs={{0,1},{1,2},{2,3},{4,5},{5,6},{6,7},{8,9},{9,10},{10,11},{12,13},{... | collective-permute-start | bytes 344072 | tf_op jit(solution)/shard_map/ppermute | solution.py:728
  6.5 1.3 collective-permute-start.1
  7.8 0.7 stack.63.info
  8.5 4.1 %pack.1 = (bf16[3088,128]{1,0:T(8,128)(2,1)}, bf16[3088,128]{1,0:T(8,128)(2,1)}, bf16[3088,128]{1,0:T(8,128)(2,1)}, bf16[3088,128]{1,0:T(8,128)(2,1)}) custom-call(s32[8]{0:T(128)} %stack.63.info, s32[12]{0:T(128)} %dest.1, s32[12]{0:T(128)} %offset.1, bf16[12,128,512]{2,1,0:T(8,128)(2,1)} %temp.1, bf16[12,128,512]{2,1,0:T(8,128)(2,1)} %qual.1), custom_call_target="tpu_custom_call" | custom-call | tf_op jit(solution)/shard_map/pack/pallas_call | solution.py:730
  12.7 0.7 collective-permute-done.1.refs_4_.right
  13.4 0.6 copy-done.4
  14.0 2.0 %collective-permute-start.2 = (bf16[3088,128]{1,0:T(8,128)(2,1)}, bf16[3088,128]{1,0:T(8,128)(2,1)S(1)}, u32[]{:S(2)}, u32[]{:S(2)}) collective-permute-start(bf16[3088,128]{1,0:T(8,128)(2,1)} %get-tuple-element.53), channel_id=1, source_target_pairs={{0,1},{1,2},{2,3},{3,0},{4,5},{5,6},{6,7},{7,4},{8,9},{9,10},{10,1... | collective-permute-start | bytes 2371592 | tf_op jit(solution)/shard_map/ppermute | solution.py:683
  16.1 1.5 collective-permute-start.6
  17.6 2.1 %collective-permute-start.5 = (bf16[3088,128]{1,0:T(8,128)(2,1)}, bf16[3088,128]{1,0:T(8,128)(2,1)S(1)}, u32[]{:S(2)}, u32[]{:S(2)}) collective-permute-start(bf16[3088,128]{1,0:T(8,128)(2,1)} %get-tuple-element.58), channel_id=1, source_target_pairs={{0,2},{1,3},{2,0},{3,1},{4,6},{5,7},{6,4},{7,5},{8,10},{9,11},{10,... | collective-permute-start | bytes 2371592 | tf_op jit(solution)/shard_map/ppermute | solution.py:683
  19.7 0.7 maximum_bitcast_fusion.taps
  20.4 1.8 edges.1
  22.2 1.9 %collective-permute-start.3 = (bf16[9,16,256]{2,1,0:T(8,128)(2,1)}, bf16[9,16,256]{2,1,0:T(8,128)(2,1)S(1)}, u32[]{:S(2)}, u32[]{:S(2)}) collective-permute-start(bf16[9,16,256]{2,1,0:T(8,128)(2,1)} %get-tuple-element.54), channel_id=1, source_target_pairs={{0,4},{4,8},{8,12},{12,16},{16,20},{20,24},{24,28},{28,32},{32,36}... | collective-permute-start | bytes 221192 | tf_op jit(solution)/shard_map/ppermute | solution.py:744
  24.1 5.8 %collective-permute-start.4 = (bf16[9,16,256]{2,1,0:T(8,128)(2,1)}, bf16[9,16,256]{2,1,0:T(8,128)(2,1)S(1)}, u32[]{:S(2)}, u32[]{:S(2)}) collective-permute-start(bf16[9,16,256]{2,1,0:T(8,128)(2,1)} %get-tuple-element.55), channel_id=1, source_target_pairs={{4,0},{8,4},{12,8},{16,12},{20,16},{24,20},{28,24},{32,28},{36,32}... | collective-permute-start | bytes 221192 | tf_op jit(solution)/shard_map/ppermute | solution.py:745
  30.0 0.7 broadcast_in_dim.2.bias
  30.7 4.5 %matrices.1 = (bf16[3,128,480]{2,1,0:T(8,128)(2,1)}, f32[3,128,128]{2,1,0:T(8,128)}) custom-call(bf16[3,3,3,16,16]{4,3,2,1,0:T(8,128)(2,1)} %maximum_bitcast_fusion.taps, f32[48,128]{1,0:T(8,128)} %broadcast_in_dim.2.bias), custom_call_target="tpu_custom_call" | custom-call | tf_op jit(solution)/shard_map/matrices/pallas_call | solution.py:763
  35.8 0.6 copy-done.15
  36.4 12.8 %adjoint.1 = (f32[7,512,128]{2,1,0:T(8,128)}, f32[8,128]{1,0:T(8,128)}, bf16[7,544,128]{2,1,0:T(8,128)(2,1)}) custom-call(bf16[6,512,128]{2,1,0:T(8,128)(2,1)} %reflect.3, s32[512,128]{1,0:T(8,128)} %land.3, bf16[9,16,256]{2,1,0:T(8,128)(2,1)} %copy-done.14, bf16[9,16,256]{2,1,0:T(8,128)(2,1)} %copy-done.15, bf16[7,64,128]{2,1,0:T(8,128)(2,1)} %copy-done.3, ...), custom_call_target="tpu_custom_call" | custom-call | tf_op jit(solution)/shard_map/adjoint/pallas_call | solution.py:747
  49.2 0.9 copy-done.1
  50.1 1.1 collective-permute-done.6.refs_3_
  51.2 1.7 collective-permute-done.5.after.refs_2_
  52.9 0.9 copy-done
  53.8 2.3 %cut.1.refs_8_ = bf16[4,7,160,128]{3,2,1,0:T(8,128)(2,1)} custom-call(bf16[7,544,128]{2,1,0:T(8,128)(2,1)} %get-tuple-element.60.window, bf16[3088,128]{1,0:T(8,128)(2,1)} %copy-done), custom_call_target="tpu_custom_call" | custom-call | tf_op jit(solution)/shard_map/cut/pallas_call | solution.py:777
  56.1 3.5 %all-to-all-start = ((bf16[4,7,160,128]{3,2,1,0:T(8,128)(2,1)}), bf16[4,7,160,128]{3,2,1,0:T(8,128)(2,1)S(1)}, u32[]{:S(2)}, u32[]{:S(2)}) async-start(bf16[4,7,160,128]{3,2,1,0:T(8,128)(2,1)} %cut.1.refs_8_), calls=%async_computation | async-start | bytes 2293760 | tf_op jit(solution)/shard_map/all_to_all | solution.py:783
  59.7 9.0 %scatter.1 = (bf16[4,544,128]{2,1,0:T(8,128)(2,1)}, bf16[4,544,128]{2,1,0:T(8,128)(2,1)}, bf16[4,544,128]{2,1,0:T(8,128)(2,1)}, bf16[4,544,128]{2,1,0:T(8,128)(2...) custom-call(s32[8]{0:T(128)} %stack.63.info, ...), custom_call_target="tpu_custom_call" | custom-call | flops 12582912 | bytes 12582912 | tf_op jit(solution)/shard_map/scatter/pallas_call | solution.py:794
  68.7 2.0 %collective-permute-start.17 = (bf16[4,544,128]{2,1,0:T(8,128)(2,1)}, bf16[4,544,128]{2,1,0:T(8,128)(2,1)S(1)}, u32[]{:S(2)}, u32[]{:S(2)}) collective-permute-start(bf16[4,544,128]{2,1,0:T(8,128)(2,1)} %get-tuple-element.71), channel_id=1, source_target_pairs={{0,8},{4,12},{8,16},{12,20},{16,24},{20,28},{24,0},{28,4},{32,40},... | collective-permute-start | bytes 1671176 | tf_op jit(solution)/shard_map/ppermute | solution.py:683
  70.7 3.6 %collective-permute-start.18 = (bf16[4,544,128]{2,1,0:T(8,128)(2,1)}, bf16[4,544,128]{2,1,0:T(8,128)(2,1)}, u32[]{:S(2)}, u32[]{:S(2)}) collective-permute-start(bf16[4,544,128]{2,1,0:T(8,128)(2,1)} %get-tuple-element.72), channel_id=1, source_target_pairs={{0,16},{4,20},{8,24},{12,28},{16,0},{20,4},{24,8},{28,12},{32,48},... | collective-permute-start | bytes 1671176 | tf_op jit(solution)/shard_map/ppermute | solution.py:683
  74.3 1.1 collective-permute-start.19
  75.4 1.5 collective-permute-start.11
  76.9 1.1 collective-permute-start.12
  77.9 7.7 %collective-permute-done.17.b = bf16[4,544,128]{2,1,0:T(8,128)(2,1)S(1)} collective-permute-done((bf16[4,544,128]{2,1,0:T(8,128)(2,1)}, bf16[4,544,128]{2,1,0:T(8,128)(2,1)S(1)}, u32[]{:S(2)}, u32[]{:S(2)}) %collective-permute-start.17) | collective-permute-done | bytes 557088 | tf_op jit(solution)/shard_map/ppermute | solution.py:683
  85.6 0.8 copy-done.10
  87.1 1.0 copy-done.2
  88.1 6.8 %bands.1 = (bf16[7,160,512]{2,1,0:T(8,128)(2,1)}, f32[6,160,512]{2,1,0:T(8,128)}) custom-call(s32[8]{0:T(128)} %stack.63.info, bf16[4,7,160,128]{3,2,1,0:T(8,128)(2,1)} %copy-done.2, bf16[160,160]{1,0:T(8,128)(2,1)} %constant.73.clone.row_h, bf16[160,160]{1,0:T(8,128)(2,1)} %constant.74.clone.row_l, bf16[512,512]{1,0:T(8,128)(2,1)} %constant.75.clone.col_h, ...), custom_call_target="tpu_custom_call" | custom-call | flops 1824522240 | bytes 10485760 | tf_op jit(solution)/shard_map/bands/pallas_call | solution.py:784
  94.9 3.8 %collective-permute-done.18.c = bf16[4,544,128]{2,1,0:T(8,128)(2,1)} collective-permute-done((bf16[4,544,128]{2,1,0:T(8,128)(2,1)}, bf16[4,544,128]{2,1,0:T(8,128)(2,1)}, u32[]{:S(2)}, u32[]{:S(2)}) %collective-permute-start.18) | collective-permute-done | bytes 557088 | tf_op jit(solution)/shard_map/ppermute | solution.py:683
  98.7 2.6 %add.14 = (f32[544,128]{1,0:T(8,128)}, f32[544,128]{1,0:T(8,128)}, f32[544,128]{1,0:T(8,128)}, f32[544,128]{1,0:T(8,128)}) custom-call(bf16[4,544,128]{2,1,0:T(8,128)(2,1)} %get-tuple-element.70.a, bf16[4,544,128]{2,1,0:T(8,128)(2,1)} %copy-done.10, bf16[4,544,128]{2,1,0:T(8,128)(2,1)} %collective-permute-done.18.c, ...), custom_call_target="tpu_custom_call" | custom-call | bytes 3145728 | tf_op jit(solution)/shard_map/add/pallas_call | solution.py:810
  101.4 1.4 collective-permute-start.20
  102.8 1.1 collective-permute-start.21
  103.9 2.2 %collective-permute-start.22 = (f32[544,128]{1,0:T(8,128)}, f32[544,128]{1,0:T(8,128)S(1)}, u32[]{:S(2)}, u32[]{:S(2)}) collective-permute-start(f32[544,128]{1,0:T(8,128)} %get-tuple-element.77), channel_id=1, source_target_pairs={{0,96},{4,100},{8,104},{12,108},{16,112},{20,116},{24,120},{28,124... | collective-permute-start | bytes 835592 | tf_op jit(solution)/shard_map/ppermute | solution.py:683
  106.1 0.8 copy-done.8
  107.1 2.6 %add.13 = (f32[544,128]{1,0:T(8,128)}, f32[544,128]{1,0:T(8,128)}, f32[544,128]{1,0:T(8,128)}, f32[544,128]{1,0:T(8,128)}) custom-call(bf16[4,544,128]{2,1,0:T(8,128)(2,1)} %get-tuple-element.61.a, bf16[4,544,128]{2,1,0:T(8,128)(2,1)} %copy-done.7, bf16[4,544,128]{2,1,0:T(8,128)(2,1)} %copy-done.8, bf16[4,544,128]{2,1,0:T(8,128)(2,1)} %copy-done.9, ...), custom_call_target="tpu_custom_call" | custom-call | bytes 3145728 | tf_op jit(solution)/shard_map/add/pallas_call | solution.py:809
  109.7 7.4 %collective-permute-start.14 = (f32[544,128]{1,0:T(8,128)}, f32[544,128]{1,0:T(8,128)S(1)}, u32[]{:S(2)}, u32[]{:S(2)}) collective-permute-start(f32[544,128]{1,0:T(8,128)} %get-tuple-element.67), channel_id=1, source_target_pairs={{0,8},{4,12},{8,16},{12,20},{16,24},{20,28},{24,0},{28,4},{32,40},... | collective-permute-start | bytes 835592 | tf_op jit(solution)/shard_map/ppermute | solution.py:683
  117.2 2.4 %collective-permute-start.15 = (f32[544,128]{1,0:T(8,128)}, f32[544,128]{1,0:T(8,128)S(1)}, u32[]{:S(2)}, u32[]{:S(2)}) collective-permute-start(f32[544,128]{1,0:T(8,128)} %get-tuple-element.68), channel_id=1, source_target_pairs={{0,16},{4,20},{8,24},{12,28},{16,0},{20,4},{24,8},{28,12},{32,48},... | collective-permute-start | bytes 835592 | tf_op jit(solution)/shard_map/ppermute | solution.py:683
  119.5 2.6 %collective-permute-start.16 = (f32[544,128]{1,0:T(8,128)}, f32[544,128]{1,0:T(8,128)S(1)}, u32[]{:S(2)}, u32[]{:S(2)}) collective-permute-start(f32[544,128]{1,0:T(8,128)} %get-tuple-element.69), channel_id=1, source_target_pairs={{0,24},{4,28},{8,0},{12,4},{16,8},{20,12},{24,16},{28,20},{32,56},... | collective-permute-start | bytes 835592 | tf_op jit(solution)/shard_map/ppermute | solution.py:683
  122.2 5.0 %collective-permute-done.15.refs_2_ = f32[544,128]{1,0:T(8,128)S(1)} collective-permute-done((f32[544,128]{1,0:T(8,128)}, f32[544,128]{1,0:T(8,128)S(1)}, u32[]{:S(2)}, u32[]{:S(2)}) %collective-permute-start.15) | collective-permute-done | bytes 278560 | tf_op jit(solution)/shard_map/ppermute | solution.py:683
  127.3 0.7 copy-done.20
  128.1 3.6 %blend.1 = (f32[168,128]{1,0:T(8,128)}, f32[168,128]{1,0:T(8,128)}, f32[168,128]{1,0:T(8,128)}, f32[168,128]{1,0:T(8,128)}) custom-call(s32[8]{0:T(128)} %stack.63.info, f32[544,128]{1,0:T(8,128)} %get-tuple-element.66.refs_0_, f32[544,128]{1,0:T(8,128)} %copy-done.19, f32[544,128]{1,0:T(8,128)} %copy-done.20, f32[544,128]{1,0:T(8,128)} %copy-done.21, ...), custom_call_target="tpu_custom_call" | custom-call | bytes 3145728 | tf_op jit(solution)/shard_map/blend/pallas_call | solution.py:813
  131.6 1.7 collective-permute-start.23
  133.4 2.7 %collective-permute-start.24 = (f32[168,128]{1,0:T(8,128)}, f32[168,128]{1,0:T(8,128)S(1)}, u32[]{:S(2)}, u32[]{:S(2)}) collective-permute-start(f32[168,128]{1,0:T(8,128)} %get-tuple-element.81), channel_id=1, source_target_pairs={{0,2},{1,3},{2,0},{3,1},{4,6},{5,7},{6,4},{7,5},{8,10},{9,11},{10,... | collective-permute-start | bytes 258056 | tf_op jit(solution)/shard_map/ppermute | solution.py:683
  136.0 1.5 collective-permute-start.25
  137.5 2.1 %collective-permute-done.24.b2 = f32[168,128]{1,0:T(8,128)S(1)} collective-permute-done((f32[168,128]{1,0:T(8,128)}, f32[168,128]{1,0:T(8,128)S(1)}, u32[]{:S(2)}, u32[]{:S(2)}) %collective-permute-start.24) | collective-permute-done | bytes 86048 | tf_op jit(solution)/shard_map/ppermute | solution.py:683
  139.6 1.1 collective-permute-done.25.b3
  140.8 0.6 copy-done.13
  141.4 1.4 merge.1
  142.7 8.9 %all-to-all-start.1 = ((f32[32,8,128]{2,1,0:T(8,128)}), f32[32,8,128]{2,1,0:T(8,128)S(1)}, u32[]{:S(2)}, u32[]{:S(2)}) async-start(f32[32,8,128]{2,1,0:T(8,128)} %merge.1), calls=%async_computation.1 | async-start | bytes 262144 | tf_op jit(solution)/shard_map/all_to_all | solution.py:829
  152.2 8.0 %assemble.1 = (f32[160,512]{1,0:T(8,128)}, bf16[20,160,768]{2,1,0:T(8,128)(2,1)}) custom-call(s32[8]{0:T(128)} %stack.63.info, f32[168,128]{1,0:T(8,128)} %get-tuple-element.79.b0, f32[168,128]{1,0:T(8,128)} %copy-done.11, f32[168,128]{1,0:T(8,128)} %copy-done.12, f32[168,128]{1,0:T(8,128)} %copy-done.13, bf16[160,160]{1,0:T(8,128)(2,1)} %constant.73.clone.row_h, ...), custom_call_target="tpu_custom_call" | custom-call | flops 330301440 | bytes 8388608 | tf_op jit(solution)/shard_map/assemble/pallas_call | solution.py:830
  160.2 0.6 copy-done.22
  160.8 12.1 %convolve.1 = (f32[128,128]{1,0:T(8,128)}, f32[128,128]{1,0:T(8,128)}, f32[128,128]{1,0:T(8,128)}, f32[128,128]{1,0:T(8,128)}, f32[7]{0:T(128)}) custom-call(s32[8]{0:T(128)} %stack.63.info, f32[16]{0:T(128)} %convert_element_type.2.head, f32[32,8,128]{2,1,0:T(8,128)} %copy-done.22, f32[160,512]{1,0:T(8,128)} %get-tuple-element.84.coarse_in, ...), custom_call_target="tpu_custom_call" | custom-call | flops 3397386240 | bytes 8388608 | tf_op jit(solution)/shard_map/convolve/pallas_call | solution.py:840
  172.9 0.7 collective-permute-start.26
  173.6 3.5 %collective-permute-start.27 = (f32[128,128]{1,0:T(8,128)}, f32[128,128]{1,0:T(8,128)S(1)}, u32[]{:S(2)}, u32[]{:S(2)}) collective-permute-start(f32[128,128]{1,0:T(8,128)} %get-tuple-element.89), channel_id=1, source_target_pairs={{0,2},{1,3},{2,0},{3,1},{4,6},{5,7},{6,4},{7,5},{8,10},{9,11},{10,... | collective-permute-start | bytes 196616 | tf_op jit(solution)/shard_map/ppermute | solution.py:683
  177.4 1.2 collective-permute-done.26.o1
  178.7 2.2 %collective-permute-done.27.o2 = f32[128,128]{1,0:T(8,128)S(1)} collective-permute-done((f32[128,128]{1,0:T(8,128)}, f32[128,128]{1,0:T(8,128)S(1)}, u32[]{:S(2)}, u32[]{:S(2)}) %collective-permute-start.27) | collective-permute-done | bytes 65568 | tf_op jit(solution)/shard_map/ppermute | solution.py:683
  180.9 0.7 collective-permute-done.28.o3
  182.2 1.7 join.1
  (86 shorter events, 3.2 us)
Async XLA Ops:
  3.0 9.7 %collective-permute-start = (bf16[7,64,128]{2,1,0:T(8,128)(2,1)}, bf16[7,64,128]{2,1,0:T(8,128)(2,1)S(1)}, u32[]{:S(2)}, u32[]{:S(2)}) collective-permute-start(bf16[7,64,128]{2,1,0:T(8,128)(2,1)} %get-tuple-element.51), channel_id=1, source_target_pairs={{0,1},{1,2},{2,3},{4,5},{5,6},{6,7},{8,9},{9,10},{10,11},{12,13},{... | collective-permute-start | bytes 344072 | tf_op jit(solution)/shard_map/ppermute | solution.py:728
  6.5 6.9 %collective-permute-start.1 = (bf16[7,64,128]{2,1,0:T(8,128)(2,1)}, bf16[7,64,128]{2,1,0:T(8,128)(2,1)S(1)}, u32[]{:S(2)}, u32[]{:S(2)}) collective-permute-start(bf16[7,64,128]{2,1,0:T(8,128)(2,1)} %get-tuple-element.52), channel_id=1, source_target_pairs={{1,0},{2,1},{3,2},{5,4},{6,5},{7,6},{9,8},{10,9},{11,10},{13,12},{... | collective-permute-start | bytes 344072 | tf_op jit(solution)/shard_map/ppermute | solution.py:729
  12.7 7.1 %copy-start.26 = (bf16[16,16,3,3]{1,0,3,2:T(8,128)(2,1)S(1)}, bf16[16,16,3,3]{1,0,3,2:T(8,128)(2,1)}, u32[]{:S(2)}) copy-start(bf16[16,16,3,3]{1,0,3,2:T(8,128)(2,1)} %param.33) | copy-start | bytes 13828
  12.7 7.1 %copy-start.27 = (bf16[16,16,3,3]{1,0,3,2:T(8,128)(2,1)S(1)}, bf16[16,16,3,3]{1,0,3,2:T(8,128)(2,1)}, u32[]{:S(2)}) copy-start(bf16[16,16,3,3]{1,0,3,2:T(8,128)(2,1)} %param.31) | copy-start | bytes 13828
  12.7 7.1 %copy-start.28 = (bf16[16,16,3,3]{1,0,3,2:T(8,128)(2,1)S(1)}, bf16[16,16,3,3]{1,0,3,2:T(8,128)(2,1)}, u32[]{:S(2)}) copy-start(bf16[16,16,3,3]{1,0,3,2:T(8,128)(2,1)} %param.29) | copy-start | bytes 13828
  12.7 0.7 copy-start.3
  13.4 0.7 copy-start.4
  14.0 15.8 %copy-start.29 = (f32[16]{0:T(128)S(1)}, f32[16]{0:T(128)}, u32[]{:S(2)}) copy-start(f32[16]{0:T(128)} %param.34) | copy-start | bytes 196
  14.0 15.9 %copy-start.30 = (f32[16]{0:T(128)S(1)}, f32[16]{0:T(128)}, u32[]{:S(2)}) copy-start(f32[16]{0:T(128)} %param.32) | copy-start | bytes 196
  14.0 15.9 %copy-start.31 = (f32[16]{0:T(128)S(1)}, f32[16]{0:T(128)}, u32[]{:S(2)}) copy-start(f32[16]{0:T(128)} %param.30) | copy-start | bytes 196
  14.0 35.2 %collective-permute-start.2 = (bf16[3088,128]{1,0:T(8,128)(2,1)}, bf16[3088,128]{1,0:T(8,128)(2,1)S(1)}, u32[]{:S(2)}, u32[]{:S(2)}) collective-permute-start(bf16[3088,128]{1,0:T(8,128)(2,1)} %get-tuple-element.53), channel_id=1, source_target_pairs={{0,1},{1,2},{2,3},{3,0},{4,5},{5,6},{6,7},{7,4},{8,9},{9,10},{10,1... | collective-permute-start | bytes 2371592 | tf_op jit(solution)/shard_map/ppermute | solution.py:683
  16.1 35.1 %collective-permute-start.6 = (bf16[3088,128]{1,0:T(8,128)(2,1)}, bf16[3088,128]{1,0:T(8,128)(2,1)S(1)}, u32[]{:S(2)}, u32[]{:S(2)}) collective-permute-start(bf16[3088,128]{1,0:T(8,128)(2,1)} %get-tuple-element.59), channel_id=1, source_target_pairs={{0,3},{1,0},{2,1},{3,2},{4,7},{5,4},{6,5},{7,6},{8,11},{9,8},{10,9... | collective-permute-start | bytes 2371592 | tf_op jit(solution)/shard_map/ppermute | solution.py:683
  17.6 35.3 %collective-permute-start.5 = (bf16[3088,128]{1,0:T(8,128)(2,1)}, bf16[3088,128]{1,0:T(8,128)(2,1)S(1)}, u32[]{:S(2)}, u32[]{:S(2)}) collective-permute-start(bf16[3088,128]{1,0:T(8,128)(2,1)} %get-tuple-element.58), channel_id=1, source_target_pairs={{0,2},{1,3},{2,0},{3,1},{4,6},{5,7},{6,4},{7,5},{8,10},{9,11},{10,... | collective-permute-start | bytes 2371592 | tf_op jit(solution)/shard_map/ppermute | solution.py:683
  19.7 15.5 %copy-start.5 = (bf16[3088,128]{1,0:T(8,128)(2,1)S(1)}, bf16[3088,128]{1,0:T(8,128)(2,1)}, u32[]{:S(2)}) copy-start(bf16[3088,128]{1,0:T(8,128)(2,1)} %get-tuple-element.47.refs_0_) | copy-start | bytes 2371588
  22.2 13.0 %collective-permute-start.3 = (bf16[9,16,256]{2,1,0:T(8,128)(2,1)}, bf16[9,16,256]{2,1,0:T(8,128)(2,1)S(1)}, u32[]{:S(2)}, u32[]{:S(2)}) collective-permute-start(bf16[9,16,256]{2,1,0:T(8,128)(2,1)} %get-tuple-element.54), channel_id=1, source_target_pairs={{0,4},{4,8},{8,12},{12,16},{16,20},{20,24},{24,28},{28,32},{32,36}... | collective-permute-start | bytes 221192 | tf_op jit(solution)/shard_map/ppermute | solution.py:744
  24.1 11.2 %collective-permute-start.4 = (bf16[9,16,256]{2,1,0:T(8,128)(2,1)}, bf16[9,16,256]{2,1,0:T(8,128)(2,1)S(1)}, u32[]{:S(2)}, u32[]{:S(2)}) collective-permute-start(bf16[9,16,256]{2,1,0:T(8,128)(2,1)} %get-tuple-element.55), channel_id=1, source_target_pairs={{4,0},{8,4},{12,8},{16,12},{20,16},{24,20},{28,24},{32,28},{36,32}... | collective-permute-start | bytes 221192 | tf_op jit(solution)/shard_map/ppermute | solution.py:745
  35.2 0.6 copy-start.14
  35.2 24.4 %collective-permute-start.7 = (bf16[3088,128]{1,0:T(8,128)(2,1)S(1)}, bf16[3088,128]{1,0:T(8,128)(2,1)}, u32[]{:S(2)}, u32[]{:S(2)}) collective-permute-start(bf16[3088,128]{1,0:T(8,128)(2,1)S(1)} %copy-done.5), channel_id=1, source_target_pairs={{0,4},{4,0},{8,12},{12,8},{16,20},{20,16},{24,28},{28,24},{32,36},... | collective-permute-start | bytes 2371592 | tf_op jit(solution)/shard_map/ppermute | solution.py:775
  35.8 0.6 copy-start.15
  49.2 0.9 copy-start.1
  50.1 9.5 %collective-permute-start.8 = (bf16[3088,128]{1,0:T(8,128)(2,1)}, bf16[3088,128]{1,0:T(8,128)(2,1)}, u32[]{:S(2)}, u32[]{:S(2)}) collective-permute-start(bf16[3088,128]{1,0:T(8,128)(2,1)} %order.3.refs_1_), channel_id=1, source_target_pairs={{0,4},{4,0},{8,12},{12,8},{16,20},{20,16},{24,28},{28,24},{32,36},... | collective-permute-start | bytes 2371592 | tf_op jit(solution)/shard_map/ppermute | solution.py:775
  51.2 8.5 %copy-start.6 = (bf16[3088,128]{1,0:T(8,128)(2,1)}, bf16[3088,128]{1,0:T(8,128)(2,1)S(1)}, u32[]{:S(2)}) copy-start(bf16[3088,128]{1,0:T(8,128)(2,1)S(1)} %collective-permute-done.6.refs_3_) | copy-start | bytes 2371588
  51.2 8.4 %collective-permute-start.10 = (bf16[3088,128]{1,0:T(8,128)(2,1)S(1)}, bf16[3088,128]{1,0:T(8,128)(2,1)}, u32[]{:S(2)}, u32[]{:S(2)}) collective-permute-start(bf16[3088,128]{1,0:T(8,128)(2,1)S(1)} %collective-permute-done.6.refs_3_), channel_id=1, source_target_pairs={{0,4},{4,0},{8,12},{12,8},{16,20},{20,16},{24,28},{28,24},{32,36},... | collective-permute-start | bytes 2371592 | tf_op jit(solution)/shard_map/ppermute | solution.py:775
  52.9 0.9 copy-start
  52.9 6.7 %collective-permute-start.9 = (bf16[3088,128]{1,0:T(8,128)(2,1)S(1)}, bf16[3088,128]{1,0:T(8,128)(2,1)}, u32[]{:S(2)}, u32[]{:S(2)}) collective-permute-start(bf16[3088,128]{1,0:T(8,128)(2,1)S(1)} %collective-permute-done.5.after.refs_2_), channel_id=1, source_target_pairs={{0,4},{4,0},{8,12},{12,8},{16,20},{20,16},{24,28},{28,24},{32,36},... | collective-permute-start | bytes 2371592 | tf_op jit(solution)/shard_map/ppermute | solution.py:775
  56.1 31.0 %all-to-all-start = ((bf16[4,7,160,128]{3,2,1,0:T(8,128)(2,1)}), bf16[4,7,160,128]{3,2,1,0:T(8,128)(2,1)S(1)}, u32[]{:S(2)}, u32[]{:S(2)}) async-start(bf16[4,7,160,128]{3,2,1,0:T(8,128)(2,1)} %cut.1.refs_8_), calls=%async_computation | async-start | bytes 2293760 | tf_op jit(solution)/shard_map/all_to_all | solution.py:783
  68.7 16.9 %collective-permute-start.17 = (bf16[4,544,128]{2,1,0:T(8,128)(2,1)}, bf16[4,544,128]{2,1,0:T(8,128)(2,1)S(1)}, u32[]{:S(2)}, u32[]{:S(2)}) collective-permute-start(bf16[4,544,128]{2,1,0:T(8,128)(2,1)} %get-tuple-element.71), channel_id=1, source_target_pairs={{0,8},{4,12},{8,16},{12,20},{16,24},{20,28},{24,0},{28,4},{32,40},... | collective-permute-start | bytes 1671176 | tf_op jit(solution)/shard_map/ppermute | solution.py:683
  70.7 28.0 %collective-permute-start.18 = (bf16[4,544,128]{2,1,0:T(8,128)(2,1)}, bf16[4,544,128]{2,1,0:T(8,128)(2,1)}, u32[]{:S(2)}, u32[]{:S(2)}) collective-permute-start(bf16[4,544,128]{2,1,0:T(8,128)(2,1)} %get-tuple-element.72), channel_id=1, source_target_pairs={{0,16},{4,20},{8,24},{12,28},{16,0},{20,4},{24,8},{28,12},{32,48},... | collective-permute-start | bytes 1671176 | tf_op jit(solution)/shard_map/ppermute | solution.py:683
  74.3 24.4 %collective-permute-start.19 = (bf16[4,544,128]{2,1,0:T(8,128)(2,1)}, bf16[4,544,128]{2,1,0:T(8,128)(2,1)}, u32[]{:S(2)}, u32[]{:S(2)}) collective-permute-start(bf16[4,544,128]{2,1,0:T(8,128)(2,1)} %get-tuple-element.73), channel_id=1, source_target_pairs={{0,24},{4,28},{8,0},{12,4},{16,8},{20,12},{24,16},{28,20},{32,56},... | collective-permute-start | bytes 1671176 | tf_op jit(solution)/shard_map/ppermute | solution.py:683
  75.4 28.5 %collective-permute-start.11 = (bf16[4,544,128]{2,1,0:T(8,128)(2,1)}, bf16[4,544,128]{2,1,0:T(8,128)(2,1)S(1)}, u32[]{:S(2)}, u32[]{:S(2)}) collective-permute-start(bf16[4,544,128]{2,1,0:T(8,128)(2,1)} %get-tuple-element.62), channel_id=1, source_target_pairs={{0,32},{4,36},{8,40},{12,44},{16,48},{20,52},{24,56},{28,60},{32,6... | collective-permute-start | bytes 1671176 | tf_op jit(solution)/shard_map/ppermute | solution.py:683
  76.9 29.2 %collective-permute-start.12 = (bf16[4,544,128]{2,1,0:T(8,128)(2,1)}, bf16[4,544,128]{2,1,0:T(8,128)(2,1)S(1)}, u32[]{:S(2)}, u32[]{:S(2)}) collective-permute-start(bf16[4,544,128]{2,1,0:T(8,128)(2,1)} %get-tuple-element.63), channel_id=1, source_target_pairs={{0,64},{4,68},{8,72},{12,76},{16,80},{20,84},{24,88},{28,92},{32,9... | collective-permute-start | bytes 1671176 | tf_op jit(solution)/shard_map/ppermute | solution.py:683
  85.6 0.8 copy-start.10
  86.4 19.6 %collective-permute-start.13 = (bf16[4,544,128]{2,1,0:T(8,128)(2,1)}, bf16[4,544,128]{2,1,0:T(8,128)(2,1)S(1)}, u32[]{:S(2)}, u32[]{:S(2)}) collective-permute-start(bf16[4,544,128]{2,1,0:T(8,128)(2,1)} %get-tuple-element.64), channel_id=1, source_target_pairs={{0,96},{4,100},{8,104},{12,108},{16,112},{20,116},{24,120},{28,124... | collective-permute-start | bytes 1671176 | tf_op jit(solution)/shard_map/ppermute | solution.py:683
  87.1 1.0 copy-start.2
  101.4 18.2 %collective-permute-start.20 = (f32[544,128]{1,0:T(8,128)}, f32[544,128]{1,0:T(8,128)S(1)}, u32[]{:S(2)}, u32[]{:S(2)}) collective-permute-start(f32[544,128]{1,0:T(8,128)} %get-tuple-element.75), channel_id=1, source_target_pairs={{0,32},{4,36},{8,40},{12,44},{16,48},{20,52},{24,56},{28,60},{32,6... | collective-permute-start | bytes 835592 | tf_op jit(solution)/shard_map/ppermute | solution.py:683
  102.8 19.4 %collective-permute-start.21 = (f32[544,128]{1,0:T(8,128)}, f32[544,128]{1,0:T(8,128)S(1)}, u32[]{:S(2)}, u32[]{:S(2)}) collective-permute-start(f32[544,128]{1,0:T(8,128)} %get-tuple-element.76), channel_id=1, source_target_pairs={{0,64},{4,68},{8,72},{12,76},{16,80},{20,84},{24,88},{28,92},{32,9... | collective-permute-start | bytes 835592 | tf_op jit(solution)/shard_map/ppermute | solution.py:683
  103.9 2.2 %copy-start.7 = (bf16[4,544,128]{2,1,0:T(8,128)(2,1)}, bf16[4,544,128]{2,1,0:T(8,128)(2,1)S(1)}, u32[]{:S(2)}) copy-start(bf16[4,544,128]{2,1,0:T(8,128)(2,1)S(1)} %collective-permute-done.11.b) | copy-start | bytes 1671172
  103.9 18.3 %collective-permute-start.22 = (f32[544,128]{1,0:T(8,128)}, f32[544,128]{1,0:T(8,128)S(1)}, u32[]{:S(2)}, u32[]{:S(2)}) collective-permute-start(f32[544,128]{1,0:T(8,128)} %get-tuple-element.77), channel_id=1, source_target_pairs={{0,96},{4,100},{8,104},{12,108},{16,112},{20,116},{24,120},{28,124... | collective-permute-start | bytes 835592 | tf_op jit(solution)/shard_map/ppermute | solution.py:683
  106.1 0.8 copy-start.8
  106.1 1.0 copy-start.9
  109.7 12.5 %collective-permute-start.14 = (f32[544,128]{1,0:T(8,128)}, f32[544,128]{1,0:T(8,128)S(1)}, u32[]{:S(2)}, u32[]{:S(2)}) collective-permute-start(f32[544,128]{1,0:T(8,128)} %get-tuple-element.67), channel_id=1, source_target_pairs={{0,8},{4,12},{8,16},{12,20},{16,24},{20,28},{24,0},{28,4},{32,40},... | collective-permute-start | bytes 835592 | tf_op jit(solution)/shard_map/ppermute | solution.py:683
  117.2 10.1 %collective-permute-start.15 = (f32[544,128]{1,0:T(8,128)}, f32[544,128]{1,0:T(8,128)S(1)}, u32[]{:S(2)}, u32[]{:S(2)}) collective-permute-start(f32[544,128]{1,0:T(8,128)} %get-tuple-element.68), channel_id=1, source_target_pairs={{0,16},{4,20},{8,24},{12,28},{16,0},{20,4},{24,8},{28,12},{32,48},... | collective-permute-start | bytes 835592 | tf_op jit(solution)/shard_map/ppermute | solution.py:683
  119.5 7.7 %copy-start.16 = (f32[544,128]{1,0:T(8,128)}, f32[544,128]{1,0:T(8,128)S(1)}, u32[]{:S(2)}) copy-start(f32[544,128]{1,0:T(8,128)S(1)} %collective-permute-done.20.refs_5_) | copy-start | bytes 835588
  119.5 7.7 %collective-permute-start.16 = (f32[544,128]{1,0:T(8,128)}, f32[544,128]{1,0:T(8,128)S(1)}, u32[]{:S(2)}, u32[]{:S(2)}) collective-permute-start(f32[544,128]{1,0:T(8,128)} %get-tuple-element.69), channel_id=1, source_target_pairs={{0,24},{4,28},{8,0},{12,4},{16,8},{20,12},{24,16},{28,20},{32,56},... | collective-permute-start | bytes 835592 | tf_op jit(solution)/shard_map/ppermute | solution.py:683
  122.2 5.1 %copy-start.17 = (f32[544,128]{1,0:T(8,128)}, f32[544,128]{1,0:T(8,128)S(1)}, u32[]{:S(2)}) copy-start(f32[544,128]{1,0:T(8,128)S(1)} %collective-permute-done.21.refs_6_) | copy-start | bytes 835588
  122.2 5.1 %copy-start.18 = (f32[544,128]{1,0:T(8,128)}, f32[544,128]{1,0:T(8,128)S(1)}, u32[]{:S(2)}) copy-start(f32[544,128]{1,0:T(8,128)S(1)} %collective-permute-done.22.refs_7_) | copy-start | bytes 835588
  122.2 5.1 %copy-start.19 = (f32[544,128]{1,0:T(8,128)}, f32[544,128]{1,0:T(8,128)S(1)}, u32[]{:S(2)}) copy-start(f32[544,128]{1,0:T(8,128)S(1)} %collective-permute-done.14.refs_1_) | copy-start | bytes 835588
  127.3 0.7 copy-start.20
  127.3 0.8 copy-start.21
  128.1 23.6 %copy-start.32 = (bf16[16]{0:T(256)(128)(2,1)S(1)}, bf16[16]{0:T(256)(128)(2,1)}, u32[]{:S(2)}) copy-start(bf16[16]{0:T(256)(128)(2,1)} %param.35) | copy-start | bytes 100
  131.6 5.9 %collective-permute-start.23 = (f32[168,128]{1,0:T(8,128)}, f32[168,128]{1,0:T(8,128)S(1)}, u32[]{:S(2)}, u32[]{:S(2)}) collective-permute-start(f32[168,128]{1,0:T(8,128)} %get-tuple-element.80), channel_id=1, source_target_pairs={{0,1},{1,2},{2,3},{3,0},{4,5},{5,6},{6,7},{7,4},{8,9},{9,10},{10,1... | collective-permute-start | bytes 258056 | tf_op jit(solution)/shard_map/ppermute | solution.py:683
  133.4 6.3 %collective-permute-start.24 = (f32[168,128]{1,0:T(8,128)}, f32[168,128]{1,0:T(8,128)S(1)}, u32[]{:S(2)}, u32[]{:S(2)}) collective-permute-start(f32[168,128]{1,0:T(8,128)} %get-tuple-element.81), channel_id=1, source_target_pairs={{0,2},{1,3},{2,0},{3,1},{4,6},{5,7},{6,4},{7,5},{8,10},{9,11},{10,... | collective-permute-start | bytes 258056 | tf_op jit(solution)/shard_map/ppermute | solution.py:683
  136.0 4.7 %collective-permute-start.25 = (f32[168,128]{1,0:T(8,128)}, f32[168,128]{1,0:T(8,128)S(1)}, u32[]{:S(2)}, u32[]{:S(2)}) collective-permute-start(f32[168,128]{1,0:T(8,128)} %get-tuple-element.82), channel_id=1, source_target_pairs={{0,3},{1,0},{2,1},{3,2},{4,7},{5,4},{6,5},{7,6},{8,11},{9,8},{10,9... | collective-permute-start | bytes 258056 | tf_op jit(solution)/shard_map/ppermute | solution.py:683
  137.5 3.2 %copy-start.11 = (f32[168,128]{1,0:T(8,128)}, f32[168,128]{1,0:T(8,128)S(1)}, u32[]{:S(2)}) copy-start(f32[168,128]{1,0:T(8,128)S(1)} %collective-permute-done.23.b1) | copy-start | bytes 258052
  139.6 1.1 copy-start.12
  140.7 0.6 copy-start.13
  142.7 17.4 %all-to-all-start.1 = ((f32[32,8,128]{2,1,0:T(8,128)}), f32[32,8,128]{2,1,0:T(8,128)S(1)}, u32[]{:S(2)}, u32[]{:S(2)}) async-start(f32[32,8,128]{2,1,0:T(8,128)} %merge.1), calls=%async_computation.1 | async-start | bytes 262144 | tf_op jit(solution)/shard_map/all_to_all | solution.py:829
  160.2 0.7 copy-start.22
  172.9 5.8 %collective-permute-start.26 = (f32[128,128]{1,0:T(8,128)}, f32[128,128]{1,0:T(8,128)S(1)}, u32[]{:S(2)}, u32[]{:S(2)}) collective-permute-start(f32[128,128]{1,0:T(8,128)} %get-tuple-element.88), channel_id=1, source_target_pairs={{0,1},{1,2},{2,3},{3,0},{4,5},{5,6},{6,7},{7,4},{8,9},{9,10},{10,1... | collective-permute-start | bytes 196616 | tf_op jit(solution)/shard_map/ppermute | solution.py:683
  173.6 7.3 %collective-permute-start.27 = (f32[128,128]{1,0:T(8,128)}, f32[128,128]{1,0:T(8,128)S(1)}, u32[]{:S(2)}, u32[]{:S(2)}) collective-permute-start(f32[128,128]{1,0:T(8,128)} %get-tuple-element.89), channel_id=1, source_target_pairs={{0,2},{1,3},{2,0},{3,1},{4,6},{5,7},{6,4},{7,5},{8,10},{9,11},{10,... | collective-permute-start | bytes 196616 | tf_op jit(solution)/shard_map/ppermute | solution.py:683
  177.1 4.5 %collective-permute-start.28 = (f32[128,128]{1,0:T(8,128)}, f32[128,128]{1,0:T(8,128)S(1)}, u32[]{:S(2)}, u32[]{:S(2)}) collective-permute-start(f32[128,128]{1,0:T(8,128)} %get-tuple-element.90), channel_id=1, source_target_pairs={{0,3},{1,0},{2,1},{3,2},{4,7},{5,4},{6,5},{7,6},{8,11},{9,8},{10,9... | collective-permute-start | bytes 196616 | tf_op jit(solution)/shard_map/ppermute | solution.py:683
  178.6 3.0 %copy-start.23 = (f32[128,128]{1,0:T(8,128)}, f32[128,128]{1,0:T(8,128)S(1)}, u32[]{:S(2)}) copy-start(f32[128,128]{1,0:T(8,128)S(1)} %collective-permute-done.26.o1) | copy-start | bytes 196612
  180.9 0.7 copy-start.24
  181.6 0.6 copy-start.25

commit v2 on v1

--- a/solution.py
+++ b/solution.py
@@ -772,8 +772,6 @@
     chip[1] = call(
         order_kernel, (block,), [ANY] * 3, place=ANY, alias={0: 0}, name="order"
     )(chip[1], adjoint, kernels)[0]
-    chip = chip + [lax.ppermute(p, "tiles", core_pair) for p in chip]
-
     cut = call(
         cut_kernel,
         sds((NY, NBANDS + 1, RQ, LANES), bf16),
@@ -790,6 +788,11 @@
         nbytes=10 << 20,
         name="bands",
     )(info, pieces, row_h, row_l, col_h, col_l, turn)
+    chip[2] = call(
+        order_kernel, (block,), [ANY] * 2, place=ANY, alias={0: 0}, name="order"
+    )(chip[2], cut)[0]
+    chip = chip + [lax.ppermute(p, "tiles", core_pair) for p in chip]
+
     part = sds((4, WIN, LANES), bf16)
     routed = call(
         scatter_kernel,

time: 185 us -> 180 us (0.973)
  starting transfers between devices: 68 us -> 60.9 us
    ppermute x21, starting transfers between devices: 43.1 us -> 37.9 us  [exchange(): lax.ppermute(pieces[k], axis, route(k))]
    all_to_all x1, starting transfers between devices: 8.88 us -> 6.34 us  [shards(): lax.all_to_all(sums, 'tiles', split_axis=0, concat_axis=0, tiled=True)]
    unnamed x66 -> x68, local copies, waits for them, and re-layouts: 9.1 us -> 9.17 us
  transfers between devices with their start and end apart: 31 -> 31, of which waited for: 11 -> 12; matrix products, arithmetic and copies ran while one was open for 1% -> 1% of each run, Pallas kernels for 30% -> 31%
where the time goes in v2:
time: 180 us; the launch traced here: 179 us
  Pallas kernels  75.7 us (42%)
  starting transfers between devices  60.9 us (34%)
  waiting for transfers between devices  29.2 us (16%)
  local copies, waits for them, and re-layouts  10.5 us (6%)
    ppermute x21, starting transfers between devices, exchange(): lax.ppermute(pieces[k], axis, route(k))  37.9 us
    ppermute x21, waiting for transfers between devices, exchange(): lax.ppermute(pieces[k], axis, route(k))  28.4 us
    pallas_call x1, Pallas kernels, shards(): call(adjoint_kernel, (sds((NBANDS + 1, TR, LANES), f32), sds((8, LANES),...  12.8 us
    pallas_call x1, Pallas kernels, shards(): call(main_kernel, (sds((QROWS, LANES), f32),) * 4 + (sds((NBANDS + 1,), f...  12.1 us
    unnamed x68, local copies, waits for them, and re-layouts  9.17 us
    pallas_call x1, Pallas kernels, shards(): call(scatter_kernel, (part,) * 8, [SMEM] + [ANY] * 9, scratch=scatter_scr...  9 us
    pallas_call x1, Pallas kernels, shards(): call(assemble_kernel, (sds((RQ, COLS), f32), sds((GROUPS, KROWS, 6 * LANE...  7.98 us
    pallas_call x1, Pallas kernels, shards(): call(bands_kernel, (sds((NBANDS + 1, RQ, COLS), bf16), sds((NBANDS, RQ, C...  6.82 us
  transfers between devices with their start and end apart: 31, of which 12 were waited for; matrix products, arithmetic and copies ran while one was open for 1% of the time, Pallas kernels for 31%

profile of v2, /device:TPU:2, one launch (start us, length us, event | category | flops | bytes accessed | tf_op | source)
XLA Modules:
  0.0 178.6 jit_solution(8908723758530544166)
XLA Ops:
  0.6 2.4 %slab.1 = (bf16[7,64,128]{2,1,0:T(8,128)(2,1)}, bf16[7,64,128]{2,1,0:T(8,128)(2,1)}) custom-call(bf16[6,512,128]{2,1,0:T(8,128)(2,1)} %reflect.3, s32[512,128]{1,0:T(8,128)} %land.3), custom_call_target="tpu_custom_call" | custom-call | tf_op jit(solution)/shard_map/slab/pallas_call | solution.py:725
  3.0 3.5 %collective-permute-start = (bf16[7,64,128]{2,1,0:T(8,128)(2,1)}, bf16[7,64,128]{2,1,0:T(8,128)(2,1)S(1)}, u32[]{:S(2)}, u32[]{:S(2)}) collective-permute-start(bf16[7,64,128]{2,1,0:T(8,128)(2,1)} %get-tuple-element.51), channel_id=1, source_target_pairs={{0,1},{1,2},{2,3},{4,5},{5,6},{6,7},{8,9},{9,10},{10,11},{12,13},{... | collective-permute-start | bytes 344072 | tf_op jit(solution)/shard_map/ppermute | solution.py:728
  6.5 1.3 collective-permute-start.1
  7.8 0.6 stack.63.info
  8.4 4.1 %pack.1 = (bf16[3088,128]{1,0:T(8,128)(2,1)}, bf16[3088,128]{1,0:T(8,128)(2,1)}, bf16[3088,128]{1,0:T(8,128)(2,1)}, bf16[3088,128]{1,0:T(8,128)(2,1)}) custom-call(s32[8]{0:T(128)} %stack.63.info, s32[12]{0:T(128)} %dest.1, s32[12]{0:T(128)} %offset.1, bf16[12,128,512]{2,1,0:T(8,128)(2,1)} %temp.1, bf16[12,128,512]{2,1,0:T(8,128)(2,1)} %qual.1), custom_call_target="tpu_custom_call" | custom-call | tf_op jit(solution)/shard_map/pack/pallas_call | solution.py:730
  12.6 0.8 collective-permute-done.1.refs_4_.right
  13.4 0.6 copy-done.4
  14.0 3.6 %collective-permute-start.5 = (bf16[3088,128]{1,0:T(8,128)(2,1)}, bf16[3088,128]{1,0:T(8,128)(2,1)S(1)}, u32[]{:S(2)}, u32[]{:S(2)}) collective-permute-start(bf16[3088,128]{1,0:T(8,128)(2,1)} %get-tuple-element.58), channel_id=1, source_target_pairs={{0,2},{1,3},{2,0},{3,1},{4,6},{5,7},{6,4},{7,5},{8,10},{9,11},{10,... | collective-permute-start | bytes 2371592 | tf_op jit(solution)/shard_map/ppermute | solution.py:683
  17.6 0.7 collective-permute-start.2
  18.3 2.6 %collective-permute-start.6 = (bf16[3088,128]{1,0:T(8,128)(2,1)}, bf16[3088,128]{1,0:T(8,128)(2,1)S(1)}, u32[]{:S(2)}, u32[]{:S(2)}) collective-permute-start(bf16[3088,128]{1,0:T(8,128)(2,1)} %get-tuple-element.60), channel_id=1, source_target_pairs={{0,3},{1,0},{2,1},{3,2},{4,7},{5,4},{6,5},{7,6},{8,11},{9,8},{10,9... | collective-permute-start | bytes 2371592 | tf_op jit(solution)/shard_map/ppermute | solution.py:683
  20.9 0.7 maximum_bitcast_fusion.taps
  21.6 1.8 %edges.1 = (bf16[9,16,256]{2,1,0:T(8,128)(2,1)}, bf16[9,16,256]{2,1,0:T(8,128)(2,1)}) custom-call(bf16[6,512,128]{2,1,0:T(8,128)(2,1)} %reflect.3, bf16[6,512,128]{2,1,0:T(8,128)(2,1)} %reflect.3, s32[512,128]{1,0:T(8,128)} %land.3, s32[512,128]{1,0:T(8,128)} %land.3, f32[512,128]{1,0:T(8,128)} %refs_8_.1, f32[512,128]{1,0:T(8,128)} %refs_8_.1, ...), custom_call_target="tpu_custom_call" | custom-call | tf_op jit(solution)/shard_map/edges/pallas_call | solution.py:741
  23.3 1.9 %collective-permute-start.3 = (bf16[9,16,256]{2,1,0:T(8,128)(2,1)}, bf16[9,16,256]{2,1,0:T(8,128)(2,1)S(1)}, u32[]{:S(2)}, u32[]{:S(2)}) collective-permute-start(bf16[9,16,256]{2,1,0:T(8,128)(2,1)} %get-tuple-element.54), channel_id=1, source_target_pairs={{0,4},{4,8},{8,12},{12,16},{16,20},{20,24},{24,28},{28,32},{32,36}... | collective-permute-start | bytes 221192 | tf_op jit(solution)/shard_map/ppermute | solution.py:744
  25.3 5.8 %collective-permute-start.4 = (bf16[9,16,256]{2,1,0:T(8,128)(2,1)}, bf16[9,16,256]{2,1,0:T(8,128)(2,1)S(1)}, u32[]{:S(2)}, u32[]{:S(2)}) collective-permute-start(bf16[9,16,256]{2,1,0:T(8,128)(2,1)} %get-tuple-element.55), channel_id=1, source_target_pairs={{4,0},{8,4},{12,8},{16,12},{20,16},{24,20},{28,24},{32,28},{36,32}... | collective-permute-start | bytes 221192 | tf_op jit(solution)/shard_map/ppermute | solution.py:745
  31.1 0.7 broadcast_in_dim.2.bias
  31.8 4.5 %matrices.1 = (bf16[3,128,480]{2,1,0:T(8,128)(2,1)}, f32[3,128,128]{2,1,0:T(8,128)}) custom-call(bf16[3,3,3,16,16]{4,3,2,1,0:T(8,128)(2,1)} %maximum_bitcast_fusion.taps, f32[48,128]{1,0:T(8,128)} %broadcast_in_dim.2.bias), custom_call_target="tpu_custom_call" | custom-call | tf_op jit(solution)/shard_map/matrices/pallas_call | solution.py:763
  37.0 0.6 copy-done.16
  37.6 12.8 %adjoint.1 = (f32[7,512,128]{2,1,0:T(8,128)}, f32[8,128]{1,0:T(8,128)}, bf16[7,544,128]{2,1,0:T(8,128)(2,1)}) custom-call(bf16[6,512,128]{2,1,0:T(8,128)(2,1)} %reflect.3, s32[512,128]{1,0:T(8,128)} %land.3, bf16[9,16,256]{2,1,0:T(8,128)(2,1)} %copy-done.15, bf16[9,16,256]{2,1,0:T(8,128)(2,1)} %copy-done.16, bf16[7,64,128]{2,1,0:T(8,128)(2,1)} %copy-done.3, ...), custom_call_target="tpu_custom_call" | custom-call | tf_op jit(solution)/shard_map/adjoint/pallas_call | solution.py:747
  50.4 0.9 copy-done
  51.3 2.3 %cut.1.refs_1_.refs_8_ = bf16[4,7,160,128]{3,2,1,0:T(8,128)(2,1)} custom-call(bf16[7,544,128]{2,1,0:T(8,128)(2,1)} %get-tuple-element.59.window, bf16[3088,128]{1,0:T(8,128)(2,1)} %copy-done), custom_call_target="tpu_custom_call" | custom-call | tf_op jit(solution)/shard_map/cut/pallas_call | solution.py:775
  53.6 0.9 copy-done.1
  55.1 3.5 %all-to-all-start = ((bf16[4,7,160,128]{3,2,1,0:T(8,128)(2,1)}), bf16[4,7,160,128]{3,2,1,0:T(8,128)(2,1)S(1)}, u32[]{:S(2)}, u32[]{:S(2)}) async-start(bf16[4,7,160,128]{3,2,1,0:T(8,128)(2,1)} %cut.1.refs_1_.refs_8_), calls=%async_computation | async-start | bytes 2293760 | tf_op jit(solution)/shard_map/all_to_all | solution.py:781
  58.7 0.9 copy-done.7
  59.6 9.0 %scatter.1 = (bf16[4,544,128]{2,1,0:T(8,128)(2,1)}, bf16[4,544,128]{2,1,0:T(8,128)(2,1)}, bf16[4,544,128]{2,1,0:T(8,128)(2,1)}, bf16[4,544,128]{2,1,0:T(8,128)(2...) custom-call(s32[8]{0:T(128)} %stack.63.info, ...), custom_call_target="tpu_custom_call" | custom-call | flops 12582912 | bytes 12582912 | tf_op jit(solution)/shard_map/scatter/pallas_call | solution.py:797
  68.8 3.6 %collective-permute-start.18 = (bf16[4,544,128]{2,1,0:T(8,128)(2,1)}, bf16[4,544,128]{2,1,0:T(8,128)(2,1)}, u32[]{:S(2)}, u32[]{:S(2)}) collective-permute-start(bf16[4,544,128]{2,1,0:T(8,128)(2,1)} %get-tuple-element.72), channel_id=1, source_target_pairs={{0,16},{4,20},{8,24},{12,28},{16,0},{20,4},{24,8},{28,12},{32,48},... | collective-permute-start | bytes 1671176 | tf_op jit(solution)/shard_map/ppermute | solution.py:683
  72.5 1.0 collective-permute-start.19
  73.5 1.5 collective-permute-start.11
  75.0 1.1 collective-permute-start.12
  76.1 9.7 %collective-permute-done.17.b = bf16[4,544,128]{2,1,0:T(8,128)(2,1)S(1)} collective-permute-done((bf16[4,544,128]{2,1,0:T(8,128)(2,1)}, bf16[4,544,128]{2,1,0:T(8,128)(2,1)S(1)}, u32[]{:S(2)}, u32[]{:S(2)}) %collective-permute-start.17) | collective-permute-done | bytes 557088 | tf_op jit(solution)/shard_map/ppermute | solution.py:683
  85.8 1.0 copy-done.2
  86.8 6.8 %bands.1 = (bf16[7,160,512]{2,1,0:T(8,128)(2,1)}, f32[6,160,512]{2,1,0:T(8,128)}) custom-call(s32[8]{0:T(128)} %stack.63.info, bf16[4,7,160,128]{3,2,1,0:T(8,128)(2,1)} %copy-done.2, bf16[160,160]{1,0:T(8,128)(2,1)} %constant.73.clone.row_h, bf16[160,160]{1,0:T(8,128)(2,1)} %constant.74.clone.row_l, bf16[512,512]{1,0:T(8,128)(2,1)} %constant.75.clone.col_h, ...), custom_call_target="tpu_custom_call" | custom-call | flops 1824522240 | bytes 10485760 | tf_op jit(solution)/shard_map/bands/pallas_call | solution.py:782
  93.6 3.4 %collective-permute-done.18.c = bf16[4,544,128]{2,1,0:T(8,128)(2,1)} collective-permute-done((bf16[4,544,128]{2,1,0:T(8,128)(2,1)}, bf16[4,544,128]{2,1,0:T(8,128)(2,1)}, u32[]{:S(2)}, u32[]{:S(2)}) %collective-permute-start.18) | collective-permute-done | bytes 557088 | tf_op jit(solution)/shard_map/ppermute | solution.py:683
  97.4 2.6 %add.14 = (f32[544,128]{1,0:T(8,128)}, f32[544,128]{1,0:T(8,128)}, f32[544,128]{1,0:T(8,128)}, f32[544,128]{1,0:T(8,128)}) custom-call(bf16[4,544,128]{2,1,0:T(8,128)(2,1)} %get-tuple-element.70.a, bf16[4,544,128]{2,1,0:T(8,128)(2,1)} %copy-done.11, bf16[4,544,128]{2,1,0:T(8,128)(2,1)} %collective-permute-done.18.c, ...), custom_call_target="tpu_custom_call" | custom-call | bytes 3145728 | tf_op jit(solution)/shard_map/add/pallas_call | solution.py:813
  100.1 1.6 collective-permute-start.20
  101.6 0.6 collective-permute-start.21
  102.2 2.6 %collective-permute-start.22 = (f32[544,128]{1,0:T(8,128)}, f32[544,128]{1,0:T(8,128)S(1)}, u32[]{:S(2)}, u32[]{:S(2)}) collective-permute-start(f32[544,128]{1,0:T(8,128)} %get-tuple-element.77), channel_id=1, source_target_pairs={{0,96},{4,100},{8,104},{12,108},{16,112},{20,116},{24,120},{28,124... | collective-permute-start | bytes 835592 | tf_op jit(solution)/shard_map/ppermute | solution.py:683
  104.8 0.8 copy-done.9
  105.8 2.6 %add.13 = (f32[544,128]{1,0:T(8,128)}, f32[544,128]{1,0:T(8,128)}, f32[544,128]{1,0:T(8,128)}, f32[544,128]{1,0:T(8,128)}) custom-call(bf16[4,544,128]{2,1,0:T(8,128)(2,1)} %get-tuple-element.61.a, bf16[4,544,128]{2,1,0:T(8,128)(2,1)} %copy-done.8, bf16[4,544,128]{2,1,0:T(8,128)(2,1)} %copy-done.9, bf16[4,544,128]{2,1,0:T(8,128)(2,1)} %copy-done.10, ...), custom_call_target="tpu_custom_call" | custom-call | bytes 3145728 | tf_op jit(solution)/shard_map/add/pallas_call | solution.py:812
  108.4 3.4 %collective-permute-start.14 = (f32[544,128]{1,0:T(8,128)}, f32[544,128]{1,0:T(8,128)S(1)}, u32[]{:S(2)}, u32[]{:S(2)}) collective-permute-start(f32[544,128]{1,0:T(8,128)} %get-tuple-element.67), channel_id=1, source_target_pairs={{0,8},{4,12},{8,16},{12,20},{16,24},{20,28},{24,0},{28,4},{32,40},... | collective-permute-start | bytes 835592 | tf_op jit(solution)/shard_map/ppermute | solution.py:683
  111.9 2.4 %collective-permute-start.15 = (f32[544,128]{1,0:T(8,128)}, f32[544,128]{1,0:T(8,128)S(1)}, u32[]{:S(2)}, u32[]{:S(2)}) collective-permute-start(f32[544,128]{1,0:T(8,128)} %get-tuple-element.68), channel_id=1, source_target_pairs={{0,16},{4,20},{8,24},{12,28},{16,0},{20,4},{24,8},{28,12},{32,48},... | collective-permute-start | bytes 835592 | tf_op jit(solution)/shard_map/ppermute | solution.py:683
  114.3 2.6 %collective-permute-start.16 = (f32[544,128]{1,0:T(8,128)}, f32[544,128]{1,0:T(8,128)S(1)}, u32[]{:S(2)}, u32[]{:S(2)}) collective-permute-start(f32[544,128]{1,0:T(8,128)} %get-tuple-element.69), channel_id=1, source_target_pairs={{0,24},{4,28},{8,0},{12,4},{16,8},{20,12},{24,16},{28,20},{32,56},... | collective-permute-start | bytes 835592 | tf_op jit(solution)/shard_map/ppermute | solution.py:683
  116.9 2.8 %collective-permute-done.14.refs_1_ = f32[544,128]{1,0:T(8,128)S(1)} collective-permute-done((f32[544,128]{1,0:T(8,128)}, f32[544,128]{1,0:T(8,128)S(1)}, u32[]{:S(2)}, u32[]{:S(2)}) %collective-permute-start.14) | collective-permute-done | bytes 278560 | tf_op jit(solution)/shard_map/ppermute | solution.py:683
  119.7 4.8 %collective-permute-done.15.refs_2_ = f32[544,128]{1,0:T(8,128)S(1)} collective-permute-done((f32[544,128]{1,0:T(8,128)}, f32[544,128]{1,0:T(8,128)S(1)}, u32[]{:S(2)}, u32[]{:S(2)}) %collective-permute-start.15) | collective-permute-done | bytes 278560 | tf_op jit(solution)/shard_map/ppermute | solution.py:683
  124.5 0.7 copy-done.21
  125.2 3.6 %blend.1 = (f32[168,128]{1,0:T(8,128)}, f32[168,128]{1,0:T(8,128)}, f32[168,128]{1,0:T(8,128)}, f32[168,128]{1,0:T(8,128)}) custom-call(s32[8]{0:T(128)} %stack.63.info, f32[544,128]{1,0:T(8,128)} %get-tuple-element.66.refs_0_, f32[544,128]{1,0:T(8,128)} %copy-done.20, f32[544,128]{1,0:T(8,128)} %copy-done.21, f32[544,128]{1,0:T(8,128)} %copy-done.22, ...), custom_call_target="tpu_custom_call" | custom-call | bytes 3145728 | tf_op jit(solution)/shard_map/blend/pallas_call | solution.py:816
  128.8 1.7 collective-permute-start.23
  130.5 2.7 %collective-permute-start.24 = (f32[168,128]{1,0:T(8,128)}, f32[168,128]{1,0:T(8,128)S(1)}, u32[]{:S(2)}, u32[]{:S(2)}) collective-permute-start(f32[168,128]{1,0:T(8,128)} %get-tuple-element.81), channel_id=1, source_target_pairs={{0,2},{1,3},{2,0},{3,1},{4,6},{5,7},{6,4},{7,5},{8,10},{9,11},{10,... | collective-permute-start | bytes 258056 | tf_op jit(solution)/shard_map/ppermute | solution.py:683
  133.2 1.5 collective-permute-start.25
  134.7 2.1 %collective-permute-done.24.b2 = f32[168,128]{1,0:T(8,128)S(1)} collective-permute-done((f32[168,128]{1,0:T(8,128)}, f32[168,128]{1,0:T(8,128)S(1)}, u32[]{:S(2)}, u32[]{:S(2)}) %collective-permute-start.24) | collective-permute-done | bytes 86048 | tf_op jit(solution)/shard_map/ppermute | solution.py:683
  136.8 1.1 collective-permute-done.25.b3
  137.9 0.6 copy-done.14
  138.5 1.4 merge.1
  139.9 6.3 %all-to-all-start.1 = ((f32[32,8,128]{2,1,0:T(8,128)}), f32[32,8,128]{2,1,0:T(8,128)S(1)}, u32[]{:S(2)}, u32[]{:S(2)}) async-start(f32[32,8,128]{2,1,0:T(8,128)} %merge.1), calls=%async_computation.1 | async-start | bytes 262144 | tf_op jit(solution)/shard_map/all_to_all | solution.py:832
  146.3 0.6 convert_element_type.2.head
  146.9 8.0 %assemble.1 = (f32[160,512]{1,0:T(8,128)}, bf16[20,160,768]{2,1,0:T(8,128)(2,1)}) custom-call(s32[8]{0:T(128)} %stack.63.info, f32[168,128]{1,0:T(8,128)} %get-tuple-element.79.b0, f32[168,128]{1,0:T(8,128)} %copy-done.12, f32[168,128]{1,0:T(8,128)} %copy-done.13, f32[168,128]{1,0:T(8,128)} %copy-done.14, bf16[160,160]{1,0:T(8,128)(2,1)} %constant.73.clone.row_h, ...), custom_call_target="tpu_custom_call" | custom-call | flops 330301440 | bytes 8388608 | tf_op jit(solution)/shard_map/assemble/pallas_call | solution.py:833
  154.9 0.6 copy-done.23
  155.5 12.1 %convolve.1 = (f32[128,128]{1,0:T(8,128)}, f32[128,128]{1,0:T(8,128)}, f32[128,128]{1,0:T(8,128)}, f32[128,128]{1,0:T(8,128)}, f32[7]{0:T(128)}) custom-call(s32[8]{0:T(128)} %stack.63.info, f32[16]{0:T(128)} %convert_element_type.2.head, f32[32,8,128]{2,1,0:T(8,128)} %copy-done.23, f32[160,512]{1,0:T(8,128)} %get-tuple-element.84.coarse_in, ...), custom_call_target="tpu_custom_call" | custom-call | flops 3397386240 | bytes 8388608 | tf_op jit(solution)/shard_map/convolve/pallas_call | solution.py:843
  167.6 0.7 collective-permute-start.26
  168.3 3.5 %collective-permute-start.27 = (f32[128,128]{1,0:T(8,128)}, f32[128,128]{1,0:T(8,128)S(1)}, u32[]{:S(2)}, u32[]{:S(2)}) collective-permute-start(f32[128,128]{1,0:T(8,128)} %get-tuple-element.89), channel_id=1, source_target_pairs={{0,2},{1,3},{2,0},{3,1},{4,6},{5,7},{6,4},{7,5},{8,10},{9,11},{10,... | collective-permute-start | bytes 196616 | tf_op jit(solution)/shard_map/ppermute | solution.py:683
  172.1 1.2 collective-permute-done.26.o1
  173.4 2.2 %collective-permute-done.27.o2 = f32[128,128]{1,0:T(8,128)S(1)} collective-permute-done((f32[128,128]{1,0:T(8,128)}, f32[128,128]{1,0:T(8,128)S(1)}, u32[]{:S(2)}, u32[]{:S(2)}) %collective-permute-start.27) | collective-permute-done | bytes 65568 | tf_op jit(solution)/shard_map/ppermute | solution.py:683
  175.5 0.7 collective-permute-done.28.o3
  176.3 0.6 copy-done.26
  176.9 1.7 join.1
  (89 shorter events, 2.8 us)
Async XLA Ops:
  3.0 9.6 %collective-permute-start = (bf16[7,64,128]{2,1,0:T(8,128)(2,1)}, bf16[7,64,128]{2,1,0:T(8,128)(2,1)S(1)}, u32[]{:S(2)}, u32[]{:S(2)}) collective-permute-start(bf16[7,64,128]{2,1,0:T(8,128)(2,1)} %get-tuple-element.51), channel_id=1, source_target_pairs={{0,1},{1,2},{2,3},{4,5},{5,6},{6,7},{8,9},{9,10},{10,11},{12,13},{... | collective-permute-start | bytes 344072 | tf_op jit(solution)/shard_map/ppermute | solution.py:728
  6.5 6.9 %collective-permute-start.1 = (bf16[7,64,128]{2,1,0:T(8,128)(2,1)}, bf16[7,64,128]{2,1,0:T(8,128)(2,1)S(1)}, u32[]{:S(2)}, u32[]{:S(2)}) collective-permute-start(bf16[7,64,128]{2,1,0:T(8,128)(2,1)} %get-tuple-element.52), channel_id=1, source_target_pairs={{1,0},{2,1},{3,2},{5,4},{6,5},{7,6},{9,8},{10,9},{11,10},{13,12},{... | collective-permute-start | bytes 344072 | tf_op jit(solution)/shard_map/ppermute | solution.py:729
  12.6 8.3 %copy-start.27 = (bf16[16,16,3,3]{1,0,3,2:T(8,128)(2,1)S(1)}, bf16[16,16,3,3]{1,0,3,2:T(8,128)(2,1)}, u32[]{:S(2)}) copy-start(bf16[16,16,3,3]{1,0,3,2:T(8,128)(2,1)} %param.33) | copy-start | bytes 13828
  12.6 8.3 %copy-start.28 = (bf16[16,16,3,3]{1,0,3,2:T(8,128)(2,1)S(1)}, bf16[16,16,3,3]{1,0,3,2:T(8,128)(2,1)}, u32[]{:S(2)}) copy-start(bf16[16,16,3,3]{1,0,3,2:T(8,128)(2,1)} %param.31) | copy-start | bytes 13828
  12.6 8.3 %copy-start.29 = (bf16[16,16,3,3]{1,0,3,2:T(8,128)(2,1)S(1)}, bf16[16,16,3,3]{1,0,3,2:T(8,128)(2,1)}, u32[]{:S(2)}) copy-start(bf16[16,16,3,3]{1,0,3,2:T(8,128)(2,1)} %param.29) | copy-start | bytes 13828
  12.6 0.8 copy-start.3
  13.4 0.7 copy-start.4
  14.0 17.0 %copy-start.30 = (f32[16]{0:T(128)S(1)}, f32[16]{0:T(128)}, u32[]{:S(2)}) copy-start(f32[16]{0:T(128)} %param.34) | copy-start | bytes 196
  14.0 17.0 %copy-start.31 = (f32[16]{0:T(128)S(1)}, f32[16]{0:T(128)}, u32[]{:S(2)}) copy-start(f32[16]{0:T(128)} %param.32) | copy-start | bytes 196
  14.0 17.0 %copy-start.32 = (f32[16]{0:T(128)S(1)}, f32[16]{0:T(128)}, u32[]{:S(2)}) copy-start(f32[16]{0:T(128)} %param.30) | copy-start | bytes 196
  14.0 36.4 %collective-permute-start.5 = (bf16[3088,128]{1,0:T(8,128)(2,1)}, bf16[3088,128]{1,0:T(8,128)(2,1)S(1)}, u32[]{:S(2)}, u32[]{:S(2)}) collective-permute-start(bf16[3088,128]{1,0:T(8,128)(2,1)} %get-tuple-element.58), channel_id=1, source_target_pairs={{0,2},{1,3},{2,0},{3,1},{4,6},{5,7},{6,4},{7,5},{8,10},{9,11},{10,... | collective-permute-start | bytes 2371592 | tf_op jit(solution)/shard_map/ppermute | solution.py:683
  17.6 35.9 %collective-permute-start.2 = (bf16[3088,128]{1,0:T(8,128)(2,1)}, bf16[3088,128]{1,0:T(8,128)(2,1)S(1)}, u32[]{:S(2)}, u32[]{:S(2)}) collective-permute-start(bf16[3088,128]{1,0:T(8,128)(2,1)} %get-tuple-element.53), channel_id=1, source_target_pairs={{0,1},{1,2},{2,3},{3,0},{4,5},{5,6},{6,7},{7,4},{8,9},{9,10},{10,1... | collective-permute-start | bytes 2371592 | tf_op jit(solution)/shard_map/ppermute | solution.py:683
  18.3 36.7 %collective-permute-start.6 = (bf16[3088,128]{1,0:T(8,128)(2,1)}, bf16[3088,128]{1,0:T(8,128)(2,1)S(1)}, u32[]{:S(2)}, u32[]{:S(2)}) collective-permute-start(bf16[3088,128]{1,0:T(8,128)(2,1)} %get-tuple-element.60), channel_id=1, source_target_pairs={{0,3},{1,0},{2,1},{3,2},{4,7},{5,4},{6,5},{7,6},{8,11},{9,8},{10,9... | collective-permute-start | bytes 2371592 | tf_op jit(solution)/shard_map/ppermute | solution.py:683
  20.9 15.4 %copy-start.5 = (bf16[3088,128]{1,0:T(8,128)(2,1)S(1)}, bf16[3088,128]{1,0:T(8,128)(2,1)}, u32[]{:S(2)}) copy-start(bf16[3088,128]{1,0:T(8,128)(2,1)} %get-tuple-element.47.refs_0_) | copy-start | bytes 2371588
  23.3 13.0 %collective-permute-start.3 = (bf16[9,16,256]{2,1,0:T(8,128)(2,1)}, bf16[9,16,256]{2,1,0:T(8,128)(2,1)S(1)}, u32[]{:S(2)}, u32[]{:S(2)}) collective-permute-start(bf16[9,16,256]{2,1,0:T(8,128)(2,1)} %get-tuple-element.54), channel_id=1, source_target_pairs={{0,4},{4,8},{8,12},{12,16},{16,20},{20,24},{24,28},{28,32},{32,36}... | collective-permute-start | bytes 221192 | tf_op jit(solution)/shard_map/ppermute | solution.py:744
  25.3 11.2 %collective-permute-start.4 = (bf16[9,16,256]{2,1,0:T(8,128)(2,1)}, bf16[9,16,256]{2,1,0:T(8,128)(2,1)S(1)}, u32[]{:S(2)}, u32[]{:S(2)}) collective-permute-start(bf16[9,16,256]{2,1,0:T(8,128)(2,1)} %get-tuple-element.55), channel_id=1, source_target_pairs={{4,0},{8,4},{12,8},{16,12},{20,16},{24,20},{28,24},{32,28},{36,32}... | collective-permute-start | bytes 221192 | tf_op jit(solution)/shard_map/ppermute | solution.py:745
  36.3 0.6 copy-start.15
  36.3 22.3 %collective-permute-start.7 = (bf16[3088,128]{1,0:T(8,128)(2,1)S(1)}, bf16[3088,128]{1,0:T(8,128)(2,1)S(1)}, u32[]{:S(2)}, u32[]{:S(2)}) collective-permute-start(bf16[3088,128]{1,0:T(8,128)(2,1)S(1)} %copy-done.5), channel_id=1, source_target_pairs={{0,4},{4,0},{8,12},{12,8},{16,20},{20,16},{24,28},{28,24},{32,36},... | collective-permute-start | bytes 2371592 | tf_op jit(solution)/shard_map/ppermute | solution.py:794
  50.4 0.9 copy-start
  53.6 5.1 %collective-permute-start.9 = (bf16[3088,128]{1,0:T(8,128)(2,1)}, bf16[3088,128]{1,0:T(8,128)(2,1)}, u32[]{:S(2)}, u32[]{:S(2)}) collective-permute-start(bf16[3088,128]{1,0:T(8,128)(2,1)} %order.5.refs_2_), channel_id=1, source_target_pairs={{0,4},{4,0},{8,12},{12,8},{16,20},{20,16},{24,28},{28,24},{32,36},... | collective-permute-start | bytes 2371592 | tf_op jit(solution)/shard_map/ppermute | solution.py:794
  53.6 0.9 copy-start.1
  54.5 4.2 %collective-permute-start.8 = (bf16[3088,128]{1,0:T(8,128)(2,1)}, bf16[3088,128]{1,0:T(8,128)(2,1)}, u32[]{:S(2)}, u32[]{:S(2)}) collective-permute-start(bf16[3088,128]{1,0:T(8,128)(2,1)} %order.4.refs_1_), channel_id=1, source_target_pairs={{0,4},{4,0},{8,12},{12,8},{16,20},{20,16},{24,28},{28,24},{32,36},... | collective-permute-start | bytes 2371592 | tf_op jit(solution)/shard_map/ppermute | solution.py:794
  55.0 3.7 %copy-start.6 = (bf16[3088,128]{1,0:T(8,128)(2,1)}, bf16[3088,128]{1,0:T(8,128)(2,1)S(1)}, u32[]{:S(2)}) copy-start(bf16[3088,128]{1,0:T(8,128)(2,1)S(1)} %collective-permute-done.6.refs_3_) | copy-start | bytes 2371588
  55.0 3.7 %collective-permute-start.10 = (bf16[3088,128]{1,0:T(8,128)(2,1)S(1)}, bf16[3088,128]{1,0:T(8,128)(2,1)}, u32[]{:S(2)}, u32[]{:S(2)}) collective-permute-start(bf16[3088,128]{1,0:T(8,128)(2,1)S(1)} %collective-permute-done.6.refs_3_), channel_id=1, source_target_pairs={{0,4},{4,0},{8,12},{12,8},{16,20},{20,16},{24,28},{28,24},{32,36},... | collective-permute-start | bytes 2371592 | tf_op jit(solution)/shard_map/ppermute | solution.py:794
  55.1 30.7 %all-to-all-start = ((bf16[4,7,160,128]{3,2,1,0:T(8,128)(2,1)}), bf16[4,7,160,128]{3,2,1,0:T(8,128)(2,1)S(1)}, u32[]{:S(2)}, u32[]{:S(2)}) async-start(bf16[4,7,160,128]{3,2,1,0:T(8,128)(2,1)} %cut.1.refs_1_.refs_8_), calls=%async_computation | async-start | bytes 2293760 | tf_op jit(solution)/shard_map/all_to_all | solution.py:781
  58.6 0.9 copy-start.7
  68.6 17.2 %collective-permute-start.17 = (bf16[4,544,128]{2,1,0:T(8,128)(2,1)}, bf16[4,544,128]{2,1,0:T(8,128)(2,1)S(1)}, u32[]{:S(2)}, u32[]{:S(2)}) collective-permute-start(bf16[4,544,128]{2,1,0:T(8,128)(2,1)} %get-tuple-element.71), channel_id=1, source_target_pairs={{0,8},{4,12},{8,16},{12,20},{16,24},{20,28},{24,0},{28,4},{32,40},... | collective-permute-start | bytes 1671176 | tf_op jit(solution)/shard_map/ppermute | solution.py:683
  68.8 28.2 %collective-permute-start.18 = (bf16[4,544,128]{2,1,0:T(8,128)(2,1)}, bf16[4,544,128]{2,1,0:T(8,128)(2,1)}, u32[]{:S(2)}, u32[]{:S(2)}) collective-permute-start(bf16[4,544,128]{2,1,0:T(8,128)(2,1)} %get-tuple-element.72), channel_id=1, source_target_pairs={{0,16},{4,20},{8,24},{12,28},{16,0},{20,4},{24,8},{28,12},{32,48},... | collective-permute-start | bytes 1671176 | tf_op jit(solution)/shard_map/ppermute | solution.py:683
  72.5 25.0 %collective-permute-start.19 = (bf16[4,544,128]{2,1,0:T(8,128)(2,1)}, bf16[4,544,128]{2,1,0:T(8,128)(2,1)}, u32[]{:S(2)}, u32[]{:S(2)}) collective-permute-start(bf16[4,544,128]{2,1,0:T(8,128)(2,1)} %get-tuple-element.73), channel_id=1, source_target_pairs={{0,24},{4,28},{8,0},{12,4},{16,8},{20,12},{24,16},{28,20},{32,56},... | collective-permute-start | bytes 1671176 | tf_op jit(solution)/shard_map/ppermute | solution.py:683
  73.5 28.7 %collective-permute-start.11 = (bf16[4,544,128]{2,1,0:T(8,128)(2,1)}, bf16[4,544,128]{2,1,0:T(8,128)(2,1)S(1)}, u32[]{:S(2)}, u32[]{:S(2)}) collective-permute-start(bf16[4,544,128]{2,1,0:T(8,128)(2,1)} %get-tuple-element.62), channel_id=1, source_target_pairs={{0,32},{4,36},{8,40},{12,44},{16,48},{20,52},{24,56},{28,60},{32,6... | collective-permute-start | bytes 1671176 | tf_op jit(solution)/shard_map/ppermute | solution.py:683
  75.0 29.9 %collective-permute-start.12 = (bf16[4,544,128]{2,1,0:T(8,128)(2,1)}, bf16[4,544,128]{2,1,0:T(8,128)(2,1)S(1)}, u32[]{:S(2)}, u32[]{:S(2)}) collective-permute-start(bf16[4,544,128]{2,1,0:T(8,128)(2,1)} %get-tuple-element.63), channel_id=1, source_target_pairs={{0,64},{4,68},{8,72},{12,76},{16,80},{20,84},{24,88},{28,92},{32,9... | collective-permute-start | bytes 1671176 | tf_op jit(solution)/shard_map/ppermute | solution.py:683
  85.8 11.7 %copy-start.11 = (bf16[4,544,128]{2,1,0:T(8,128)(2,1)}, bf16[4,544,128]{2,1,0:T(8,128)(2,1)S(1)}, u32[]{:S(2)}) copy-start(bf16[4,544,128]{2,1,0:T(8,128)(2,1)S(1)} %collective-permute-done.17.b) | copy-start | bytes 1671172
  85.8 19.1 %collective-permute-start.13 = (bf16[4,544,128]{2,1,0:T(8,128)(2,1)}, bf16[4,544,128]{2,1,0:T(8,128)(2,1)S(1)}, u32[]{:S(2)}, u32[]{:S(2)}) collective-permute-start(bf16[4,544,128]{2,1,0:T(8,128)(2,1)} %get-tuple-element.64), channel_id=1, source_target_pairs={{0,96},{4,100},{8,104},{12,108},{16,112},{20,116},{24,120},{28,124... | collective-permute-start | bytes 1671176 | tf_op jit(solution)/shard_map/ppermute | solution.py:683
  85.8 1.0 copy-start.2
  100.1 14.2 %collective-permute-start.20 = (f32[544,128]{1,0:T(8,128)}, f32[544,128]{1,0:T(8,128)S(1)}, u32[]{:S(2)}, u32[]{:S(2)}) collective-permute-start(f32[544,128]{1,0:T(8,128)} %get-tuple-element.75), channel_id=1, source_target_pairs={{0,32},{4,36},{8,40},{12,44},{16,48},{20,52},{24,56},{28,60},{32,6... | collective-permute-start | bytes 835592 | tf_op jit(solution)/shard_map/ppermute | solution.py:683
  101.6 15.3 %collective-permute-start.21 = (f32[544,128]{1,0:T(8,128)}, f32[544,128]{1,0:T(8,128)S(1)}, u32[]{:S(2)}, u32[]{:S(2)}) collective-permute-start(f32[544,128]{1,0:T(8,128)} %get-tuple-element.76), channel_id=1, source_target_pairs={{0,64},{4,68},{8,72},{12,76},{16,80},{20,84},{24,88},{28,92},{32,9... | collective-permute-start | bytes 835592 | tf_op jit(solution)/shard_map/ppermute | solution.py:683
  102.2 2.6 %copy-start.8 = (bf16[4,544,128]{2,1,0:T(8,128)(2,1)}, bf16[4,544,128]{2,1,0:T(8,128)(2,1)S(1)}, u32[]{:S(2)}) copy-start(bf16[4,544,128]{2,1,0:T(8,128)(2,1)S(1)} %collective-permute-done.11.b) | copy-start | bytes 1671172
  102.2 14.7 %collective-permute-start.22 = (f32[544,128]{1,0:T(8,128)}, f32[544,128]{1,0:T(8,128)S(1)}, u32[]{:S(2)}, u32[]{:S(2)}) collective-permute-start(f32[544,128]{1,0:T(8,128)} %get-tuple-element.77), channel_id=1, source_target_pairs={{0,96},{4,100},{8,104},{12,108},{16,112},{20,116},{24,120},{28,124... | collective-permute-start | bytes 835592 | tf_op jit(solution)/shard_map/ppermute | solution.py:683
  104.8 0.8 copy-start.9
  104.8 1.0 copy-start.10
  108.4 11.2 %collective-permute-start.14 = (f32[544,128]{1,0:T(8,128)}, f32[544,128]{1,0:T(8,128)S(1)}, u32[]{:S(2)}, u32[]{:S(2)}) collective-permute-start(f32[544,128]{1,0:T(8,128)} %get-tuple-element.67), channel_id=1, source_target_pairs={{0,8},{4,12},{8,16},{12,20},{16,24},{20,28},{24,0},{28,4},{32,40},... | collective-permute-start | bytes 835592 | tf_op jit(solution)/shard_map/ppermute | solution.py:683
  111.9 12.6 %collective-permute-start.15 = (f32[544,128]{1,0:T(8,128)}, f32[544,128]{1,0:T(8,128)S(1)}, u32[]{:S(2)}, u32[]{:S(2)}) collective-permute-start(f32[544,128]{1,0:T(8,128)} %get-tuple-element.68), channel_id=1, source_target_pairs={{0,16},{4,20},{8,24},{12,28},{16,0},{20,4},{24,8},{28,12},{32,48},... | collective-permute-start | bytes 835592 | tf_op jit(solution)/shard_map/ppermute | solution.py:683
  114.2 10.2 %copy-start.17 = (f32[544,128]{1,0:T(8,128)}, f32[544,128]{1,0:T(8,128)S(1)}, u32[]{:S(2)}) copy-start(f32[544,128]{1,0:T(8,128)S(1)} %collective-permute-done.20.refs_5_) | copy-start | bytes 835588
  114.3 10.2 %collective-permute-start.16 = (f32[544,128]{1,0:T(8,128)}, f32[544,128]{1,0:T(8,128)S(1)}, u32[]{:S(2)}, u32[]{:S(2)}) collective-permute-start(f32[544,128]{1,0:T(8,128)} %get-tuple-element.69), channel_id=1, source_target_pairs={{0,24},{4,28},{8,0},{12,4},{16,8},{20,12},{24,16},{28,20},{32,56},... | collective-permute-start | bytes 835592 | tf_op jit(solution)/shard_map/ppermute | solution.py:683
  116.9 7.6 %copy-start.18 = (f32[544,128]{1,0:T(8,128)}, f32[544,128]{1,0:T(8,128)S(1)}, u32[]{:S(2)}) copy-start(f32[544,128]{1,0:T(8,128)S(1)} %collective-permute-done.21.refs_6_) | copy-start | bytes 835588
  116.9 7.6 %copy-start.19 = (f32[544,128]{1,0:T(8,128)}, f32[544,128]{1,0:T(8,128)S(1)}, u32[]{:S(2)}) copy-start(f32[544,128]{1,0:T(8,128)S(1)} %collective-permute-done.22.refs_7_) | copy-start | bytes 835588
  119.7 4.8 %copy-start.20 = (f32[544,128]{1,0:T(8,128)}, f32[544,128]{1,0:T(8,128)S(1)}, u32[]{:S(2)}) copy-start(f32[544,128]{1,0:T(8,128)S(1)} %collective-permute-done.14.refs_1_) | copy-start | bytes 835588
  124.4 0.7 copy-start.21
  124.4 0.8 copy-start.22
  125.2 21.1 %copy-start.33 = (bf16[16]{0:T(256)(128)(2,1)S(1)}, bf16[16]{0:T(256)(128)(2,1)}, u32[]{:S(2)}) copy-start(bf16[16]{0:T(256)(128)(2,1)} %param.35) | copy-start | bytes 100
  128.8 5.9 %collective-permute-start.23 = (f32[168,128]{1,0:T(8,128)}, f32[168,128]{1,0:T(8,128)S(1)}, u32[]{:S(2)}, u32[]{:S(2)}) collective-permute-start(f32[168,128]{1,0:T(8,128)} %get-tuple-element.80), channel_id=1, source_target_pairs={{0,1},{1,2},{2,3},{3,0},{4,5},{5,6},{6,7},{7,4},{8,9},{9,10},{10,1... | collective-permute-start | bytes 258056 | tf_op jit(solution)/shard_map/ppermute | solution.py:683
  130.5 6.3 %collective-permute-start.24 = (f32[168,128]{1,0:T(8,128)}, f32[168,128]{1,0:T(8,128)S(1)}, u32[]{:S(2)}, u32[]{:S(2)}) collective-permute-start(f32[168,128]{1,0:T(8,128)} %get-tuple-element.81), channel_id=1, source_target_pairs={{0,2},{1,3},{2,0},{3,1},{4,6},{5,7},{6,4},{7,5},{8,10},{9,11},{10,... | collective-permute-start | bytes 258056 | tf_op jit(solution)/shard_map/ppermute | solution.py:683
  133.2 4.7 %collective-permute-start.25 = (f32[168,128]{1,0:T(8,128)}, f32[168,128]{1,0:T(8,128)S(1)}, u32[]{:S(2)}, u32[]{:S(2)}) collective-permute-start(f32[168,128]{1,0:T(8,128)} %get-tuple-element.82), channel_id=1, source_target_pairs={{0,3},{1,0},{2,1},{3,2},{4,7},{5,4},{6,5},{7,6},{8,11},{9,8},{10,9... | collective-permute-start | bytes 258056 | tf_op jit(solution)/shard_map/ppermute | solution.py:683
  134.7 3.2 %copy-start.12 = (f32[168,128]{1,0:T(8,128)}, f32[168,128]{1,0:T(8,128)S(1)}, u32[]{:S(2)}) copy-start(f32[168,128]{1,0:T(8,128)S(1)} %collective-permute-done.23.b1) | copy-start | bytes 258052
  136.8 1.1 copy-start.13
  137.9 0.6 copy-start.14
  139.9 14.9 %all-to-all-start.1 = ((f32[32,8,128]{2,1,0:T(8,128)}), f32[32,8,128]{2,1,0:T(8,128)S(1)}, u32[]{:S(2)}, u32[]{:S(2)}) async-start(f32[32,8,128]{2,1,0:T(8,128)} %merge.1), calls=%async_computation.1 | async-start | bytes 262144 | tf_op jit(solution)/shard_map/all_to_all | solution.py:832
  154.9 0.7 copy-start.23
  167.6 5.8 %collective-permute-start.26 = (f32[128,128]{1,0:T(8,128)}, f32[128,128]{1,0:T(8,128)S(1)}, u32[]{:S(2)}, u32[]{:S(2)}) collective-permute-start(f32[128,128]{1,0:T(8,128)} %get-tuple-element.88), channel_id=1, source_target_pairs={{0,1},{1,2},{2,3},{3,0},{4,5},{5,6},{6,7},{7,4},{8,9},{9,10},{10,1... | collective-permute-start | bytes 196616 | tf_op jit(solution)/shard_map/ppermute | solution.py:683
  168.3 7.2 %collective-permute-start.27 = (f32[128,128]{1,0:T(8,128)}, f32[128,128]{1,0:T(8,128)S(1)}, u32[]{:S(2)}, u32[]{:S(2)}) collective-permute-start(f32[128,128]{1,0:T(8,128)} %get-tuple-element.89), channel_id=1, source_target_pairs={{0,2},{1,3},{2,0},{3,1},{4,6},{5,7},{6,4},{7,5},{8,10},{9,11},{10,... | collective-permute-start | bytes 196616 | tf_op jit(solution)/shard_map/ppermute | solution.py:683
  171.8 4.5 %collective-permute-start.28 = (f32[128,128]{1,0:T(8,128)}, f32[128,128]{1,0:T(8,128)S(1)}, u32[]{:S(2)}, u32[]{:S(2)}) collective-permute-start(f32[128,128]{1,0:T(8,128)} %get-tuple-element.90), channel_id=1, source_target_pairs={{0,3},{1,0},{2,1},{3,2},{4,7},{5,4},{6,5},{7,6},{8,11},{9,8},{10,9... | collective-permute-start | bytes 196616 | tf_op jit(solution)/shard_map/ppermute | solution.py:683
  173.4 2.9 %copy-start.24 = (f32[128,128]{1,0:T(8,128)}, f32[128,128]{1,0:T(8,128)S(1)}, u32[]{:S(2)}) copy-start(f32[128,128]{1,0:T(8,128)S(1)} %collective-permute-done.26.o1) | copy-start | bytes 196612
  175.5 0.7 copy-start.25
  176.3 0.6 copy-start.26
  (1 other events, 0.6 us)

commit v3 on v2

--- a/solution.py
+++ b/solution.py
@@ -113,7 +113,7 @@
 
             return carry
 
-        lax.fori_loop(0, count, body, 0, unroll=2)
+        lax.fori_loop(0, count, body, 0, unroll=4)
 
 
 def pack_kernel(info, dest, offset, temp, qual, *outs):
@@ -546,7 +546,7 @@
         )
         return carry
 
-    lax.fori_loop(0, GROUPS // 2, start, 0)
+    lax.fori_loop(0, GROUPS // 2, start, 0, unroll=True)
     edge_row = lax.broadcasted_iota(jnp.int32, (CH, 6 * LANES), 0) == 0
 
     def with_base(g):
@@ -586,7 +586,7 @@
                 put(group.at[u], g, following)
             return carry
 
-        lax.fori_loop(0, (GROUPS - 2) // steps, body, 0)
+        lax.fori_loop(0, (GROUPS - 2) // steps, body, 0, unroll=True)
 
     def last(i, carry):
         mask = fields[NBANDS, pl.ds(pl.multiple_of(HALO + 32 * i, 32), 32), :].astype(f32)
@@ -603,7 +603,7 @@
             )
         return carry
 
-    lax.fori_loop(0, QROWS // 32, last, 0)
+    lax.fori_loop(0, QROWS // 32, last, 0, unroll=True)
     turn_copy.wait()
     high, low = split(result[...])
     result[...] = dot(high, turn_back[...]) + dot(low, turn_back[...])

time: 180 us -> 178 us (0.989)
  Pallas kernels: 75.7 us -> 73.5 us
    pallas_call x1, Pallas kernels: 12.1 us -> 10.2 us  [shards(): call(main_kernel, (sds((QROWS, LANES), f32),) * 4 + (sds((NBANDS + 1,), f...]
where the time goes in v3:
time: 178 us; the launch traced here: 177 us
  Pallas kernels  73.5 us (41%)
  starting transfers between devices  60.8 us (34%)
  waiting for transfers between devices  29.6 us (17%)
  local copies, waits for them, and re-layouts  10.5 us (6%)
    ppermute x21, starting transfers between devices, exchange(): lax.ppermute(pieces[k], axis, route(k))  37.9 us
    ppermute x21, waiting for transfers between devices, exchange(): lax.ppermute(pieces[k], axis, route(k))  28.8 us
    pallas_call x1, Pallas kernels, shards(): call(adjoint_kernel, (sds((NBANDS + 1, TR, LANES), f32), sds((8, LANES),...  12.8 us
    pallas_call x1, Pallas kernels, shards(): call(main_kernel, (sds((QROWS, LANES), f32),) * 4 + (sds((NBANDS + 1,), f...  10.2 us
    unnamed x68, local copies, waits for them, and re-layouts  9.17 us
    pallas_call x1, Pallas kernels, shards(): call(scatter_kernel, (part,) * 8, [SMEM] + [ANY] * 9, scratch=scatter_scr...  8.65 us
    pallas_call x1, Pallas kernels, shards(): call(assemble_kernel, (sds((RQ, COLS), f32), sds((GROUPS, KROWS, 6 * LANE...  7.98 us
    pallas_call x1, Pallas kernels, shards(): call(bands_kernel, (sds((NBANDS + 1, RQ, COLS), bf16), sds((NBANDS, RQ, C...  6.82 us
  transfers between devices with their start and end apart: 31, of which 12 were waited for; matrix products, arithmetic and copies ran while one was open for 1% of the time, Pallas kernels for 31%

profile of v3, /device:TPU:2, one launch (start us, length us, event | category | flops | bytes accessed | tf_op | source)
XLA Modules:
  0.0 176.8 jit_solution(13443956378239964458)
XLA Ops:
  0.6 2.4 %slab.1 = (bf16[7,64,128]{2,1,0:T(8,128)(2,1)}, bf16[7,64,128]{2,1,0:T(8,128)(2,1)}) custom-call(bf16[6,512,128]{2,1,0:T(8,128)(2,1)} %reflect.3, s32[512,128]{1,0:T(8,128)} %land.3), custom_call_target="tpu_custom_call" | custom-call | tf_op jit(solution)/shard_map/slab/pallas_call | solution.py:725
  3.0 3.5 %collective-permute-start = (bf16[7,64,128]{2,1,0:T(8,128)(2,1)}, bf16[7,64,128]{2,1,0:T(8,128)(2,1)S(1)}, u32[]{:S(2)}, u32[]{:S(2)}) collective-permute-start(bf16[7,64,128]{2,1,0:T(8,128)(2,1)} %get-tuple-element.51), channel_id=1, source_target_pairs={{0,1},{1,2},{2,3},{4,5},{5,6},{6,7},{8,9},{9,10},{10,11},{12,13},{... | collective-permute-start | bytes 344072 | tf_op jit(solution)/shard_map/ppermute | solution.py:728
  6.5 1.3 collective-permute-start.1
  7.8 0.6 stack.63.info
  8.4 4.1 %pack.1 = (bf16[3088,128]{1,0:T(8,128)(2,1)}, bf16[3088,128]{1,0:T(8,128)(2,1)}, bf16[3088,128]{1,0:T(8,128)(2,1)}, bf16[3088,128]{1,0:T(8,128)(2,1)}) custom-call(s32[8]{0:T(128)} %stack.63.info, s32[12]{0:T(128)} %dest.1, s32[12]{0:T(128)} %offset.1, bf16[12,128,512]{2,1,0:T(8,128)(2,1)} %temp.1, bf16[12,128,512]{2,1,0:T(8,128)(2,1)} %qual.1), custom_call_target="tpu_custom_call" | custom-call | tf_op jit(solution)/shard_map/pack/pallas_call | solution.py:730
  12.6 0.8 collective-permute-done.1.refs_4_.right
  13.4 0.6 copy-done.4
  14.0 3.6 %collective-permute-start.5 = (bf16[3088,128]{1,0:T(8,128)(2,1)}, bf16[3088,128]{1,0:T(8,128)(2,1)S(1)}, u32[]{:S(2)}, u32[]{:S(2)}) collective-permute-start(bf16[3088,128]{1,0:T(8,128)(2,1)} %get-tuple-element.58), channel_id=1, source_target_pairs={{0,2},{1,3},{2,0},{3,1},{4,6},{5,7},{6,4},{7,5},{8,10},{9,11},{10,... | collective-permute-start | bytes 2371592 | tf_op jit(solution)/shard_map/ppermute | solution.py:683
  17.6 0.7 collective-permute-start.2
  18.3 2.6 %collective-permute-start.6 = (bf16[3088,128]{1,0:T(8,128)(2,1)}, bf16[3088,128]{1,0:T(8,128)(2,1)S(1)}, u32[]{:S(2)}, u32[]{:S(2)}) collective-permute-start(bf16[3088,128]{1,0:T(8,128)(2,1)} %get-tuple-element.60), channel_id=1, source_target_pairs={{0,3},{1,0},{2,1},{3,2},{4,7},{5,4},{6,5},{7,6},{8,11},{9,8},{10,9... | collective-permute-start | bytes 2371592 | tf_op jit(solution)/shard_map/ppermute | solution.py:683
  20.9 0.7 maximum_bitcast_fusion.taps
  21.6 1.8 %edges.1 = (bf16[9,16,256]{2,1,0:T(8,128)(2,1)}, bf16[9,16,256]{2,1,0:T(8,128)(2,1)}) custom-call(bf16[6,512,128]{2,1,0:T(8,128)(2,1)} %reflect.3, bf16[6,512,128]{2,1,0:T(8,128)(2,1)} %reflect.3, s32[512,128]{1,0:T(8,128)} %land.3, s32[512,128]{1,0:T(8,128)} %land.3, f32[512,128]{1,0:T(8,128)} %refs_8_.1, f32[512,128]{1,0:T(8,128)} %refs_8_.1, ...), custom_call_target="tpu_custom_call" | custom-call | tf_op jit(solution)/shard_map/edges/pallas_call | solution.py:741
  23.3 1.9 %collective-permute-start.3 = (bf16[9,16,256]{2,1,0:T(8,128)(2,1)}, bf16[9,16,256]{2,1,0:T(8,128)(2,1)S(1)}, u32[]{:S(2)}, u32[]{:S(2)}) collective-permute-start(bf16[9,16,256]{2,1,0:T(8,128)(2,1)} %get-tuple-element.54), channel_id=1, source_target_pairs={{0,4},{4,8},{8,12},{12,16},{16,20},{20,24},{24,28},{28,32},{32,36}... | collective-permute-start | bytes 221192 | tf_op jit(solution)/shard_map/ppermute | solution.py:744
  25.3 5.8 %collective-permute-start.4 = (bf16[9,16,256]{2,1,0:T(8,128)(2,1)}, bf16[9,16,256]{2,1,0:T(8,128)(2,1)S(1)}, u32[]{:S(2)}, u32[]{:S(2)}) collective-permute-start(bf16[9,16,256]{2,1,0:T(8,128)(2,1)} %get-tuple-element.55), channel_id=1, source_target_pairs={{4,0},{8,4},{12,8},{16,12},{20,16},{24,20},{28,24},{32,28},{36,32}... | collective-permute-start | bytes 221192 | tf_op jit(solution)/shard_map/ppermute | solution.py:745
  31.1 0.7 broadcast_in_dim.2.bias
  31.8 4.5 %matrices.1 = (bf16[3,128,480]{2,1,0:T(8,128)(2,1)}, f32[3,128,128]{2,1,0:T(8,128)}) custom-call(bf16[3,3,3,16,16]{4,3,2,1,0:T(8,128)(2,1)} %maximum_bitcast_fusion.taps, f32[48,128]{1,0:T(8,128)} %broadcast_in_dim.2.bias), custom_call_target="tpu_custom_call" | custom-call | tf_op jit(solution)/shard_map/matrices/pallas_call | solution.py:763
  37.0 0.6 copy-done.16
  37.6 12.8 %adjoint.1 = (f32[7,512,128]{2,1,0:T(8,128)}, f32[8,128]{1,0:T(8,128)}, bf16[7,544,128]{2,1,0:T(8,128)(2,1)}) custom-call(bf16[6,512,128]{2,1,0:T(8,128)(2,1)} %reflect.3, s32[512,128]{1,0:T(8,128)} %land.3, bf16[9,16,256]{2,1,0:T(8,128)(2,1)} %copy-done.15, bf16[9,16,256]{2,1,0:T(8,128)(2,1)} %copy-done.16, bf16[7,64,128]{2,1,0:T(8,128)(2,1)} %copy-done.3, ...), custom_call_target="tpu_custom_call" | custom-call | tf_op jit(solution)/shard_map/adjoint/pallas_call | solution.py:747
  50.4 0.9 copy-done
  51.3 2.3 %cut.1.refs_1_.refs_8_ = bf16[4,7,160,128]{3,2,1,0:T(8,128)(2,1)} custom-call(bf16[7,544,128]{2,1,0:T(8,128)(2,1)} %get-tuple-element.59.window, bf16[3088,128]{1,0:T(8,128)(2,1)} %copy-done), custom_call_target="tpu_custom_call" | custom-call | tf_op jit(solution)/shard_map/cut/pallas_call | solution.py:775
  53.6 0.9 copy-done.1
  55.1 3.5 %all-to-all-start = ((bf16[4,7,160,128]{3,2,1,0:T(8,128)(2,1)}), bf16[4,7,160,128]{3,2,1,0:T(8,128)(2,1)S(1)}, u32[]{:S(2)}, u32[]{:S(2)}) async-start(bf16[4,7,160,128]{3,2,1,0:T(8,128)(2,1)} %cut.1.refs_1_.refs_8_), calls=%async_computation | async-start | bytes 2293760 | tf_op jit(solution)/shard_map/all_to_all | solution.py:781
  58.7 0.9 copy-done.7
  59.6 8.7 %scatter.1 = (bf16[4,544,128]{2,1,0:T(8,128)(2,1)}, bf16[4,544,128]{2,1,0:T(8,128)(2,1)}, bf16[4,544,128]{2,1,0:T(8,128)(2,1)}, bf16[4,544,128]{2,1,0:T(8,128)(2...) custom-call(s32[8]{0:T(128)} %stack.63.info, ...), custom_call_target="tpu_custom_call" | custom-call | flops 12582912 | bytes 12582912 | tf_op jit(solution)/shard_map/scatter/pallas_call | solution.py:797
  68.6 3.5 %collective-permute-start.18 = (bf16[4,544,128]{2,1,0:T(8,128)(2,1)}, bf16[4,544,128]{2,1,0:T(8,128)(2,1)}, u32[]{:S(2)}, u32[]{:S(2)}) collective-permute-start(bf16[4,544,128]{2,1,0:T(8,128)(2,1)} %get-tuple-element.72), channel_id=1, source_target_pairs={{0,16},{4,20},{8,24},{12,28},{16,0},{20,4},{24,8},{28,12},{32,48},... | collective-permute-start | bytes 1671176 | tf_op jit(solution)/shard_map/ppermute | solution.py:683
  72.1 1.1 collective-permute-start.19
  73.2 1.4 collective-permute-start.11
  74.7 1.1 collective-permute-start.12
  75.8 9.4 %collective-permute-done.17.b = bf16[4,544,128]{2,1,0:T(8,128)(2,1)S(1)} collective-permute-done((bf16[4,544,128]{2,1,0:T(8,128)(2,1)}, bf16[4,544,128]{2,1,0:T(8,128)(2,1)S(1)}, u32[]{:S(2)}, u32[]{:S(2)}) %collective-permute-start.17) | collective-permute-done | bytes 557088 | tf_op jit(solution)/shard_map/ppermute | solution.py:683
  85.3 1.0 copy-done.2
  86.3 6.8 %bands.1 = (bf16[7,160,512]{2,1,0:T(8,128)(2,1)}, f32[6,160,512]{2,1,0:T(8,128)}) custom-call(s32[8]{0:T(128)} %stack.63.info, bf16[4,7,160,128]{3,2,1,0:T(8,128)(2,1)} %copy-done.2, bf16[160,160]{1,0:T(8,128)(2,1)} %constant.73.clone.row_h, bf16[160,160]{1,0:T(8,128)(2,1)} %constant.74.clone.row_l, bf16[512,512]{1,0:T(8,128)(2,1)} %constant.75.clone.col_h, ...), custom_call_target="tpu_custom_call" | custom-call | flops 1824522240 | bytes 10485760 | tf_op jit(solution)/shard_map/bands/pallas_call | solution.py:782
  93.1 4.0 %collective-permute-done.18.c = bf16[4,544,128]{2,1,0:T(8,128)(2,1)} collective-permute-done((bf16[4,544,128]{2,1,0:T(8,128)(2,1)}, bf16[4,544,128]{2,1,0:T(8,128)(2,1)}, u32[]{:S(2)}, u32[]{:S(2)}) %collective-permute-start.18) | collective-permute-done | bytes 557088 | tf_op jit(solution)/shard_map/ppermute | solution.py:683
  97.5 2.6 %add.14 = (f32[544,128]{1,0:T(8,128)}, f32[544,128]{1,0:T(8,128)}, f32[544,128]{1,0:T(8,128)}, f32[544,128]{1,0:T(8,128)}) custom-call(bf16[4,544,128]{2,1,0:T(8,128)(2,1)} %get-tuple-element.70.a, bf16[4,544,128]{2,1,0:T(8,128)(2,1)} %copy-done.11, bf16[4,544,128]{2,1,0:T(8,128)(2,1)} %collective-permute-done.18.c, ...), custom_call_target="tpu_custom_call" | custom-call | bytes 3145728 | tf_op jit(solution)/shard_map/add/pallas_call | solution.py:813
  100.1 1.5 collective-permute-start.20
  101.7 0.6 collective-permute-start.21
  102.3 2.6 %collective-permute-start.22 = (f32[544,128]{1,0:T(8,128)}, f32[544,128]{1,0:T(8,128)S(1)}, u32[]{:S(2)}, u32[]{:S(2)}) collective-permute-start(f32[544,128]{1,0:T(8,128)} %get-tuple-element.77), channel_id=1, source_target_pairs={{0,96},{4,100},{8,104},{12,108},{16,112},{20,116},{24,120},{28,124... | collective-permute-start | bytes 835592 | tf_op jit(solution)/shard_map/ppermute | solution.py:683
  105.0 0.8 copy-done.9
  105.9 2.6 %add.13 = (f32[544,128]{1,0:T(8,128)}, f32[544,128]{1,0:T(8,128)}, f32[544,128]{1,0:T(8,128)}, f32[544,128]{1,0:T(8,128)}) custom-call(bf16[4,544,128]{2,1,0:T(8,128)(2,1)} %get-tuple-element.61.a, bf16[4,544,128]{2,1,0:T(8,128)(2,1)} %copy-done.8, bf16[4,544,128]{2,1,0:T(8,128)(2,1)} %copy-done.9, bf16[4,544,128]{2,1,0:T(8,128)(2,1)} %copy-done.10, ...), custom_call_target="tpu_custom_call" | custom-call | bytes 3145728 | tf_op jit(solution)/shard_map/add/pallas_call | solution.py:812
  108.6 3.3 %collective-permute-start.14 = (f32[544,128]{1,0:T(8,128)}, f32[544,128]{1,0:T(8,128)S(1)}, u32[]{:S(2)}, u32[]{:S(2)}) collective-permute-start(f32[544,128]{1,0:T(8,128)} %get-tuple-element.67), channel_id=1, source_target_pairs={{0,8},{4,12},{8,16},{12,20},{16,24},{20,28},{24,0},{28,4},{32,40},... | collective-permute-start | bytes 835592 | tf_op jit(solution)/shard_map/ppermute | solution.py:683
  111.9 2.4 %collective-permute-start.15 = (f32[544,128]{1,0:T(8,128)}, f32[544,128]{1,0:T(8,128)S(1)}, u32[]{:S(2)}, u32[]{:S(2)}) collective-permute-start(f32[544,128]{1,0:T(8,128)} %get-tuple-element.68), channel_id=1, source_target_pairs={{0,16},{4,20},{8,24},{12,28},{16,0},{20,4},{24,8},{28,12},{32,48},... | collective-permute-start | bytes 835592 | tf_op jit(solution)/shard_map/ppermute | solution.py:683
  114.3 2.6 %collective-permute-start.16 = (f32[544,128]{1,0:T(8,128)}, f32[544,128]{1,0:T(8,128)S(1)}, u32[]{:S(2)}, u32[]{:S(2)}) collective-permute-start(f32[544,128]{1,0:T(8,128)} %get-tuple-element.69), channel_id=1, source_target_pairs={{0,24},{4,28},{8,0},{12,4},{16,8},{20,12},{24,16},{28,20},{32,56},... | collective-permute-start | bytes 835592 | tf_op jit(solution)/shard_map/ppermute | solution.py:683
  116.9 2.8 %collective-permute-done.14.refs_1_ = f32[544,128]{1,0:T(8,128)S(1)} collective-permute-done((f32[544,128]{1,0:T(8,128)}, f32[544,128]{1,0:T(8,128)S(1)}, u32[]{:S(2)}, u32[]{:S(2)}) %collective-permute-start.14) | collective-permute-done | bytes 278560 | tf_op jit(solution)/shard_map/ppermute | solution.py:683
  119.7 4.9 %collective-permute-done.15.refs_2_ = f32[544,128]{1,0:T(8,128)S(1)} collective-permute-done((f32[544,128]{1,0:T(8,128)}, f32[544,128]{1,0:T(8,128)S(1)}, u32[]{:S(2)}, u32[]{:S(2)}) %collective-permute-start.15) | collective-permute-done | bytes 278560 | tf_op jit(solution)/shard_map/ppermute | solution.py:683
  124.6 0.7 copy-done.21
  125.3 3.6 %blend.1 = (f32[168,128]{1,0:T(8,128)}, f32[168,128]{1,0:T(8,128)}, f32[168,128]{1,0:T(8,128)}, f32[168,128]{1,0:T(8,128)}) custom-call(s32[8]{0:T(128)} %stack.63.info, f32[544,128]{1,0:T(8,128)} %get-tuple-element.66.refs_0_, f32[544,128]{1,0:T(8,128)} %copy-done.20, f32[544,128]{1,0:T(8,128)} %copy-done.21, f32[544,128]{1,0:T(8,128)} %copy-done.22, ...), custom_call_target="tpu_custom_call" | custom-call | bytes 3145728 | tf_op jit(solution)/shard_map/blend/pallas_call | solution.py:816
  128.9 1.7 collective-permute-start.23
  130.7 2.7 %collective-permute-start.24 = (f32[168,128]{1,0:T(8,128)}, f32[168,128]{1,0:T(8,128)S(1)}, u32[]{:S(2)}, u32[]{:S(2)}) collective-permute-start(f32[168,128]{1,0:T(8,128)} %get-tuple-element.81), channel_id=1, source_target_pairs={{0,2},{1,3},{2,0},{3,1},{4,6},{5,7},{6,4},{7,5},{8,10},{9,11},{10,... | collective-permute-start | bytes 258056 | tf_op jit(solution)/shard_map/ppermute | solution.py:683
  133.3 1.5 collective-permute-start.25
  134.9 2.1 %collective-permute-done.24.b2 = f32[168,128]{1,0:T(8,128)S(1)} collective-permute-done((f32[168,128]{1,0:T(8,128)}, f32[168,128]{1,0:T(8,128)S(1)}, u32[]{:S(2)}, u32[]{:S(2)}) %collective-permute-start.24) | collective-permute-done | bytes 86048 | tf_op jit(solution)/shard_map/ppermute | solution.py:683
  136.9 1.1 collective-permute-done.25.b3
  138.0 0.6 copy-done.14
  138.7 1.4 merge.1
  140.0 6.3 %all-to-all-start.1 = ((f32[32,8,128]{2,1,0:T(8,128)}), f32[32,8,128]{2,1,0:T(8,128)S(1)}, u32[]{:S(2)}, u32[]{:S(2)}) async-start(f32[32,8,128]{2,1,0:T(8,128)} %merge.1), calls=%async_computation.1 | async-start | bytes 262144 | tf_op jit(solution)/shard_map/all_to_all | solution.py:832
  146.3 0.6 convert_element_type.2.head
  146.9 8.0 %assemble.1 = (f32[160,512]{1,0:T(8,128)}, bf16[20,160,768]{2,1,0:T(8,128)(2,1)}) custom-call(s32[8]{0:T(128)} %stack.63.info, f32[168,128]{1,0:T(8,128)} %get-tuple-element.79.b0, f32[168,128]{1,0:T(8,128)} %copy-done.12, f32[168,128]{1,0:T(8,128)} %copy-done.13, f32[168,128]{1,0:T(8,128)} %copy-done.14, bf16[160,160]{1,0:T(8,128)(2,1)} %constant.73.clone.row_h, ...), custom_call_target="tpu_custom_call" | custom-call | flops 330301440 | bytes 8388608 | tf_op jit(solution)/shard_map/assemble/pallas_call | solution.py:833
  154.9 0.6 copy-done.23
  155.6 10.2 %convolve.1 = (f32[128,128]{1,0:T(8,128)}, f32[128,128]{1,0:T(8,128)}, f32[128,128]{1,0:T(8,128)}, f32[128,128]{1,0:T(8,128)}, f32[7]{0:T(128)}) custom-call(s32[8]{0:T(128)} %stack.63.info, f32[16]{0:T(128)} %convert_element_type.2.head, f32[32,8,128]{2,1,0:T(8,128)} %copy-done.23, f32[160,512]{1,0:T(8,128)} %get-tuple-element.84.coarse_in, ...), custom_call_target="tpu_custom_call" | custom-call | flops 3397386240 | bytes 8388608 | tf_op jit(solution)/shard_map/convolve/pallas_call | solution.py:843
  165.8 0.7 collective-permute-start.26
  166.5 3.5 %collective-permute-start.27 = (f32[128,128]{1,0:T(8,128)}, f32[128,128]{1,0:T(8,128)S(1)}, u32[]{:S(2)}, u32[]{:S(2)}) collective-permute-start(f32[128,128]{1,0:T(8,128)} %get-tuple-element.89), channel_id=1, source_target_pairs={{0,2},{1,3},{2,0},{3,1},{4,6},{5,7},{6,4},{7,5},{8,10},{9,11},{10,... | collective-permute-start | bytes 196616 | tf_op jit(solution)/shard_map/ppermute | solution.py:683
  170.3 1.2 collective-permute-done.26.o1
  171.5 2.2 %collective-permute-done.27.o2 = f32[128,128]{1,0:T(8,128)S(1)} collective-permute-done((f32[128,128]{1,0:T(8,128)}, f32[128,128]{1,0:T(8,128)S(1)}, u32[]{:S(2)}, u32[]{:S(2)}) %collective-permute-start.27) | collective-permute-done | bytes 65568 | tf_op jit(solution)/shard_map/ppermute | solution.py:683
  173.8 0.7 collective-permute-done.28.o3
  174.5 0.6 copy-done.26
  175.1 1.7 join.1
  (89 shorter events, 2.9 us)
Async XLA Ops:
  3.0 9.6 %collective-permute-start = (bf16[7,64,128]{2,1,0:T(8,128)(2,1)}, bf16[7,64,128]{2,1,0:T(8,128)(2,1)S(1)}, u32[]{:S(2)}, u32[]{:S(2)}) collective-permute-start(bf16[7,64,128]{2,1,0:T(8,128)(2,1)} %get-tuple-element.51), channel_id=1, source_target_pairs={{0,1},{1,2},{2,3},{4,5},{5,6},{6,7},{8,9},{9,10},{10,11},{12,13},{... | collective-permute-start | bytes 344072 | tf_op jit(solution)/shard_map/ppermute | solution.py:728
  6.5 6.9 %collective-permute-start.1 = (bf16[7,64,128]{2,1,0:T(8,128)(2,1)}, bf16[7,64,128]{2,1,0:T(8,128)(2,1)S(1)}, u32[]{:S(2)}, u32[]{:S(2)}) collective-permute-start(bf16[7,64,128]{2,1,0:T(8,128)(2,1)} %get-tuple-element.52), channel_id=1, source_target_pairs={{1,0},{2,1},{3,2},{5,4},{6,5},{7,6},{9,8},{10,9},{11,10},{13,12},{... | collective-permute-start | bytes 344072 | tf_op jit(solution)/shard_map/ppermute | solution.py:729
  12.6 8.3 %copy-start.27 = (bf16[16,16,3,3]{1,0,3,2:T(8,128)(2,1)S(1)}, bf16[16,16,3,3]{1,0,3,2:T(8,128)(2,1)}, u32[]{:S(2)}) copy-start(bf16[16,16,3,3]{1,0,3,2:T(8,128)(2,1)} %param.33) | copy-start | bytes 13828
  12.6 8.3 %copy-start.28 = (bf16[16,16,3,3]{1,0,3,2:T(8,128)(2,1)S(1)}, bf16[16,16,3,3]{1,0,3,2:T(8,128)(2,1)}, u32[]{:S(2)}) copy-start(bf16[16,16,3,3]{1,0,3,2:T(8,128)(2,1)} %param.31) | copy-start | bytes 13828
  12.6 8.3 %copy-start.29 = (bf16[16,16,3,3]{1,0,3,2:T(8,128)(2,1)S(1)}, bf16[16,16,3,3]{1,0,3,2:T(8,128)(2,1)}, u32[]{:S(2)}) copy-start(bf16[16,16,3,3]{1,0,3,2:T(8,128)(2,1)} %param.29) | copy-start | bytes 13828
  12.6 0.8 copy-start.3
  13.4 0.7 copy-start.4
  14.0 17.0 %copy-start.30 = (f32[16]{0:T(128)S(1)}, f32[16]{0:T(128)}, u32[]{:S(2)}) copy-start(f32[16]{0:T(128)} %param.34) | copy-start | bytes 196
  14.0 17.0 %copy-start.31 = (f32[16]{0:T(128)S(1)}, f32[16]{0:T(128)}, u32[]{:S(2)}) copy-start(f32[16]{0:T(128)} %param.32) | copy-start | bytes 196
  14.0 17.0 %copy-start.32 = (f32[16]{0:T(128)S(1)}, f32[16]{0:T(128)}, u32[]{:S(2)}) copy-start(f32[16]{0:T(128)} %param.30) | copy-start | bytes 196
  14.0 36.4 %collective-permute-start.5 = (bf16[3088,128]{1,0:T(8,128)(2,1)}, bf16[3088,128]{1,0:T(8,128)(2,1)S(1)}, u32[]{:S(2)}, u32[]{:S(2)}) collective-permute-start(bf16[3088,128]{1,0:T(8,128)(2,1)} %get-tuple-element.58), channel_id=1, source_target_pairs={{0,2},{1,3},{2,0},{3,1},{4,6},{5,7},{6,4},{7,5},{8,10},{9,11},{10,... | collective-permute-start | bytes 2371592 | tf_op jit(solution)/shard_map/ppermute | solution.py:683
  17.6 35.9 %collective-permute-start.2 = (bf16[3088,128]{1,0:T(8,128)(2,1)}, bf16[3088,128]{1,0:T(8,128)(2,1)S(1)}, u32[]{:S(2)}, u32[]{:S(2)}) collective-permute-start(bf16[3088,128]{1,0:T(8,128)(2,1)} %get-tuple-element.53), channel_id=1, source_target_pairs={{0,1},{1,2},{2,3},{3,0},{4,5},{5,6},{6,7},{7,4},{8,9},{9,10},{10,1... | collective-permute-start | bytes 2371592 | tf_op jit(solution)/shard_map/ppermute | solution.py:683
  18.3 36.7 %collective-permute-start.6 = (bf16[3088,128]{1,0:T(8,128)(2,1)}, bf16[3088,128]{1,0:T(8,128)(2,1)S(1)}, u32[]{:S(2)}, u32[]{:S(2)}) collective-permute-start(bf16[3088,128]{1,0:T(8,128)(2,1)} %get-tuple-element.60), channel_id=1, source_target_pairs={{0,3},{1,0},{2,1},{3,2},{4,7},{5,4},{6,5},{7,6},{8,11},{9,8},{10,9... | collective-permute-start | bytes 2371592 | tf_op jit(solution)/shard_map/ppermute | solution.py:683
  20.9 15.4 %copy-start.5 = (bf16[3088,128]{1,0:T(8,128)(2,1)S(1)}, bf16[3088,128]{1,0:T(8,128)(2,1)}, u32[]{:S(2)}) copy-start(bf16[3088,128]{1,0:T(8,128)(2,1)} %get-tuple-element.47.refs_0_) | copy-start | bytes 2371588
  23.3 13.0 %collective-permute-start.3 = (bf16[9,16,256]{2,1,0:T(8,128)(2,1)}, bf16[9,16,256]{2,1,0:T(8,128)(2,1)S(1)}, u32[]{:S(2)}, u32[]{:S(2)}) collective-permute-start(bf16[9,16,256]{2,1,0:T(8,128)(2,1)} %get-tuple-element.54), channel_id=1, source_target_pairs={{0,4},{4,8},{8,12},{12,16},{16,20},{20,24},{24,28},{28,32},{32,36}... | collective-permute-start | bytes 221192 | tf_op jit(solution)/shard_map/ppermute | solution.py:744
  25.3 11.2 %collective-permute-start.4 = (bf16[9,16,256]{2,1,0:T(8,128)(2,1)}, bf16[9,16,256]{2,1,0:T(8,128)(2,1)S(1)}, u32[]{:S(2)}, u32[]{:S(2)}) collective-permute-start(bf16[9,16,256]{2,1,0:T(8,128)(2,1)} %get-tuple-element.55), channel_id=1, source_target_pairs={{4,0},{8,4},{12,8},{16,12},{20,16},{24,20},{28,24},{32,28},{36,32}... | collective-permute-start | bytes 221192 | tf_op jit(solution)/shard_map/ppermute | solution.py:745
  36.3 0.6 copy-start.15
  36.3 22.3 %collective-permute-start.7 = (bf16[3088,128]{1,0:T(8,128)(2,1)S(1)}, bf16[3088,128]{1,0:T(8,128)(2,1)S(1)}, u32[]{:S(2)}, u32[]{:S(2)}) collective-permute-start(bf16[3088,128]{1,0:T(8,128)(2,1)S(1)} %copy-done.5), channel_id=1, source_target_pairs={{0,4},{4,0},{8,12},{12,8},{16,20},{20,16},{24,28},{28,24},{32,36},... | collective-permute-start | bytes 2371592 | tf_op jit(solution)/shard_map/ppermute | solution.py:794
  50.4 0.9 copy-start
  53.6 5.1 %collective-permute-start.9 = (bf16[3088,128]{1,0:T(8,128)(2,1)}, bf16[3088,128]{1,0:T(8,128)(2,1)}, u32[]{:S(2)}, u32[]{:S(2)}) collective-permute-start(bf16[3088,128]{1,0:T(8,128)(2,1)} %order.5.refs_2_), channel_id=1, source_target_pairs={{0,4},{4,0},{8,12},{12,8},{16,20},{20,16},{24,28},{28,24},{32,36},... | collective-permute-start | bytes 2371592 | tf_op jit(solution)/shard_map/ppermute | solution.py:794
  53.6 0.9 copy-start.1
  54.5 4.2 %collective-permute-start.8 = (bf16[3088,128]{1,0:T(8,128)(2,1)}, bf16[3088,128]{1,0:T(8,128)(2,1)}, u32[]{:S(2)}, u32[]{:S(2)}) collective-permute-start(bf16[3088,128]{1,0:T(8,128)(2,1)} %order.4.refs_1_), channel_id=1, source_target_pairs={{0,4},{4,0},{8,12},{12,8},{16,20},{20,16},{24,28},{28,24},{32,36},... | collective-permute-start | bytes 2371592 | tf_op jit(solution)/shard_map/ppermute | solution.py:794
  55.0 3.7 %copy-start.6 = (bf16[3088,128]{1,0:T(8,128)(2,1)}, bf16[3088,128]{1,0:T(8,128)(2,1)S(1)}, u32[]{:S(2)}) copy-start(bf16[3088,128]{1,0:T(8,128)(2,1)S(1)} %collective-permute-done.6.refs_3_) | copy-start | bytes 2371588
  55.0 3.7 %collective-permute-start.10 = (bf16[3088,128]{1,0:T(8,128)(2,1)S(1)}, bf16[3088,128]{1,0:T(8,128)(2,1)}, u32[]{:S(2)}, u32[]{:S(2)}) collective-permute-start(bf16[3088,128]{1,0:T(8,128)(2,1)S(1)} %collective-permute-done.6.refs_3_), channel_id=1, source_target_pairs={{0,4},{4,0},{8,12},{12,8},{16,20},{20,16},{24,28},{28,24},{32,36},... | collective-permute-start | bytes 2371592 | tf_op jit(solution)/shard_map/ppermute | solution.py:794
  55.1 30.2 %all-to-all-start = ((bf16[4,7,160,128]{3,2,1,0:T(8,128)(2,1)}), bf16[4,7,160,128]{3,2,1,0:T(8,128)(2,1)S(1)}, u32[]{:S(2)}, u32[]{:S(2)}) async-start(bf16[4,7,160,128]{3,2,1,0:T(8,128)(2,1)} %cut.1.refs_1_.refs_8_), calls=%async_computation | async-start | bytes 2293760 | tf_op jit(solution)/shard_map/all_to_all | solution.py:781
  58.6 0.9 copy-start.7
  68.2 17.0 %collective-permute-start.17 = (bf16[4,544,128]{2,1,0:T(8,128)(2,1)}, bf16[4,544,128]{2,1,0:T(8,128)(2,1)S(1)}, u32[]{:S(2)}, u32[]{:S(2)}) collective-permute-start(bf16[4,544,128]{2,1,0:T(8,128)(2,1)} %get-tuple-element.71), channel_id=1, source_target_pairs={{0,8},{4,12},{8,16},{12,20},{16,24},{20,28},{24,0},{28,4},{32,40},... | collective-permute-start | bytes 1671176 | tf_op jit(solution)/shard_map/ppermute | solution.py:683
  68.6 28.5 %collective-permute-start.18 = (bf16[4,544,128]{2,1,0:T(8,128)(2,1)}, bf16[4,544,128]{2,1,0:T(8,128)(2,1)}, u32[]{:S(2)}, u32[]{:S(2)}) collective-permute-start(bf16[4,544,128]{2,1,0:T(8,128)(2,1)} %get-tuple-element.72), channel_id=1, source_target_pairs={{0,16},{4,20},{8,24},{12,28},{16,0},{20,4},{24,8},{28,12},{32,48},... | collective-permute-start | bytes 1671176 | tf_op jit(solution)/shard_map/ppermute | solution.py:683
  72.1 25.4 %collective-permute-start.19 = (bf16[4,544,128]{2,1,0:T(8,128)(2,1)}, bf16[4,544,128]{2,1,0:T(8,128)(2,1)}, u32[]{:S(2)}, u32[]{:S(2)}) collective-permute-start(bf16[4,544,128]{2,1,0:T(8,128)(2,1)} %get-tuple-element.73), channel_id=1, source_target_pairs={{0,24},{4,28},{8,0},{12,4},{16,8},{20,12},{24,16},{28,20},{32,56},... | collective-permute-start | bytes 1671176 | tf_op jit(solution)/shard_map/ppermute | solution.py:683
  73.2 29.1 %collective-permute-start.11 = (bf16[4,544,128]{2,1,0:T(8,128)(2,1)}, bf16[4,544,128]{2,1,0:T(8,128)(2,1)S(1)}, u32[]{:S(2)}, u32[]{:S(2)}) collective-permute-start(bf16[4,544,128]{2,1,0:T(8,128)(2,1)} %get-tuple-element.62), channel_id=1, source_target_pairs={{0,32},{4,36},{8,40},{12,44},{16,48},{20,52},{24,56},{28,60},{32,6... | collective-permute-start | bytes 1671176 | tf_op jit(solution)/shard_map/ppermute | solution.py:683
  74.7 30.3 %collective-permute-start.12 = (bf16[4,544,128]{2,1,0:T(8,128)(2,1)}, bf16[4,544,128]{2,1,0:T(8,128)(2,1)S(1)}, u32[]{:S(2)}, u32[]{:S(2)}) collective-permute-start(bf16[4,544,128]{2,1,0:T(8,128)(2,1)} %get-tuple-element.63), channel_id=1, source_target_pairs={{0,64},{4,68},{8,72},{12,76},{16,80},{20,84},{24,88},{28,92},{32,9... | collective-permute-start | bytes 1671176 | tf_op jit(solution)/shard_map/ppermute | solution.py:683
  85.3 12.3 %copy-start.11 = (bf16[4,544,128]{2,1,0:T(8,128)(2,1)}, bf16[4,544,128]{2,1,0:T(8,128)(2,1)S(1)}, u32[]{:S(2)}) copy-start(bf16[4,544,128]{2,1,0:T(8,128)(2,1)S(1)} %collective-permute-done.17.b) | copy-start | bytes 1671172
  85.3 19.7 %collective-permute-start.13 = (bf16[4,544,128]{2,1,0:T(8,128)(2,1)}, bf16[4,544,128]{2,1,0:T(8,128)(2,1)S(1)}, u32[]{:S(2)}, u32[]{:S(2)}) collective-permute-start(bf16[4,544,128]{2,1,0:T(8,128)(2,1)} %get-tuple-element.64), channel_id=1, source_target_pairs={{0,96},{4,100},{8,104},{12,108},{16,112},{20,116},{24,120},{28,124... | collective-permute-start | bytes 1671176 | tf_op jit(solution)/shard_map/ppermute | solution.py:683
  85.3 1.0 copy-start.2
  100.1 14.1 %collective-permute-start.20 = (f32[544,128]{1,0:T(8,128)}, f32[544,128]{1,0:T(8,128)S(1)}, u32[]{:S(2)}, u32[]{:S(2)}) collective-permute-start(f32[544,128]{1,0:T(8,128)} %get-tuple-element.75), channel_id=1, source_target_pairs={{0,32},{4,36},{8,40},{12,44},{16,48},{20,52},{24,56},{28,60},{32,6... | collective-permute-start | bytes 835592 | tf_op jit(solution)/shard_map/ppermute | solution.py:683
  101.7 15.2 %collective-permute-start.21 = (f32[544,128]{1,0:T(8,128)}, f32[544,128]{1,0:T(8,128)S(1)}, u32[]{:S(2)}, u32[]{:S(2)}) collective-permute-start(f32[544,128]{1,0:T(8,128)} %get-tuple-element.76), channel_id=1, source_target_pairs={{0,64},{4,68},{8,72},{12,76},{16,80},{20,84},{24,88},{28,92},{32,9... | collective-permute-start | bytes 835592 | tf_op jit(solution)/shard_map/ppermute | solution.py:683
  102.3 2.6 %copy-start.8 = (bf16[4,544,128]{2,1,0:T(8,128)(2,1)}, bf16[4,544,128]{2,1,0:T(8,128)(2,1)S(1)}, u32[]{:S(2)}) copy-start(bf16[4,544,128]{2,1,0:T(8,128)(2,1)S(1)} %collective-permute-done.11.b) | copy-start | bytes 1671172
  102.3 14.6 %collective-permute-start.22 = (f32[544,128]{1,0:T(8,128)}, f32[544,128]{1,0:T(8,128)S(1)}, u32[]{:S(2)}, u32[]{:S(2)}) collective-permute-start(f32[544,128]{1,0:T(8,128)} %get-tuple-element.77), channel_id=1, source_target_pairs={{0,96},{4,100},{8,104},{12,108},{16,112},{20,116},{24,120},{28,124... | collective-permute-start | bytes 835592 | tf_op jit(solution)/shard_map/ppermute | solution.py:683
  104.9 0.8 copy-start.9
  104.9 1.0 copy-start.10
  108.6 11.1 %collective-permute-start.14 = (f32[544,128]{1,0:T(8,128)}, f32[544,128]{1,0:T(8,128)S(1)}, u32[]{:S(2)}, u32[]{:S(2)}) collective-permute-start(f32[544,128]{1,0:T(8,128)} %get-tuple-element.67), channel_id=1, source_target_pairs={{0,8},{4,12},{8,16},{12,20},{16,24},{20,28},{24,0},{28,4},{32,40},... | collective-permute-start | bytes 835592 | tf_op jit(solution)/shard_map/ppermute | solution.py:683
  111.9 12.7 %collective-permute-start.15 = (f32[544,128]{1,0:T(8,128)}, f32[544,128]{1,0:T(8,128)S(1)}, u32[]{:S(2)}, u32[]{:S(2)}) collective-permute-start(f32[544,128]{1,0:T(8,128)} %get-tuple-element.68), channel_id=1, source_target_pairs={{0,16},{4,20},{8,24},{12,28},{16,0},{20,4},{24,8},{28,12},{32,48},... | collective-permute-start | bytes 835592 | tf_op jit(solution)/shard_map/ppermute | solution.py:683
  114.3 10.3 %copy-start.17 = (f32[544,128]{1,0:T(8,128)}, f32[544,128]{1,0:T(8,128)S(1)}, u32[]{:S(2)}) copy-start(f32[544,128]{1,0:T(8,128)S(1)} %collective-permute-done.20.refs_5_) | copy-start | bytes 835588
  114.3 10.3 %collective-permute-start.16 = (f32[544,128]{1,0:T(8,128)}, f32[544,128]{1,0:T(8,128)S(1)}, u32[]{:S(2)}, u32[]{:S(2)}) collective-permute-start(f32[544,128]{1,0:T(8,128)} %get-tuple-element.69), channel_id=1, source_target_pairs={{0,24},{4,28},{8,0},{12,4},{16,8},{20,12},{24,16},{28,20},{32,56},... | collective-permute-start | bytes 835592 | tf_op jit(solution)/shard_map/ppermute | solution.py:683
  116.9 7.6 %copy-start.18 = (f32[544,128]{1,0:T(8,128)}, f32[544,128]{1,0:T(8,128)S(1)}, u32[]{:S(2)}) copy-start(f32[544,128]{1,0:T(8,128)S(1)} %collective-permute-done.21.refs_6_) | copy-start | bytes 835588
  116.9 7.6 %copy-start.19 = (f32[544,128]{1,0:T(8,128)}, f32[544,128]{1,0:T(8,128)S(1)}, u32[]{:S(2)}) copy-start(f32[544,128]{1,0:T(8,128)S(1)} %collective-permute-done.22.refs_7_) | copy-start | bytes 835588
  119.7 4.9 %copy-start.20 = (f32[544,128]{1,0:T(8,128)}, f32[544,128]{1,0:T(8,128)S(1)}, u32[]{:S(2)}) copy-start(f32[544,128]{1,0:T(8,128)S(1)} %collective-permute-done.14.refs_1_) | copy-start | bytes 835588
  124.5 0.7 copy-start.21
  124.5 0.8 copy-start.22
  125.3 21.0 %copy-start.33 = (bf16[16]{0:T(256)(128)(2,1)S(1)}, bf16[16]{0:T(256)(128)(2,1)}, u32[]{:S(2)}) copy-start(bf16[16]{0:T(256)(128)(2,1)} %param.35) | copy-start | bytes 100
  128.9 5.9 %collective-permute-start.23 = (f32[168,128]{1,0:T(8,128)}, f32[168,128]{1,0:T(8,128)S(1)}, u32[]{:S(2)}, u32[]{:S(2)}) collective-permute-start(f32[168,128]{1,0:T(8,128)} %get-tuple-element.80), channel_id=1, source_target_pairs={{0,1},{1,2},{2,3},{3,0},{4,5},{5,6},{6,7},{7,4},{8,9},{9,10},{10,1... | collective-permute-start | bytes 258056 | tf_op jit(solution)/shard_map/ppermute | solution.py:683
  130.7 6.3 %collective-permute-start.24 = (f32[168,128]{1,0:T(8,128)}, f32[168,128]{1,0:T(8,128)S(1)}, u32[]{:S(2)}, u32[]{:S(2)}) collective-permute-start(f32[168,128]{1,0:T(8,128)} %get-tuple-element.81), channel_id=1, source_target_pairs={{0,2},{1,3},{2,0},{3,1},{4,6},{5,7},{6,4},{7,5},{8,10},{9,11},{10,... | collective-permute-start | bytes 258056 | tf_op jit(solution)/shard_map/ppermute | solution.py:683
  133.3 4.7 %collective-permute-start.25 = (f32[168,128]{1,0:T(8,128)}, f32[168,128]{1,0:T(8,128)S(1)}, u32[]{:S(2)}, u32[]{:S(2)}) collective-permute-start(f32[168,128]{1,0:T(8,128)} %get-tuple-element.82), channel_id=1, source_target_pairs={{0,3},{1,0},{2,1},{3,2},{4,7},{5,4},{6,5},{7,6},{8,11},{9,8},{10,9... | collective-permute-start | bytes 258056 | tf_op jit(solution)/shard_map/ppermute | solution.py:683
  134.8 3.2 %copy-start.12 = (f32[168,128]{1,0:T(8,128)}, f32[168,128]{1,0:T(8,128)S(1)}, u32[]{:S(2)}) copy-start(f32[168,128]{1,0:T(8,128)S(1)} %collective-permute-done.23.b1) | copy-start | bytes 258052
  136.9 1.1 copy-start.13
  138.0 0.6 copy-start.14
  140.0 14.9 %all-to-all-start.1 = ((f32[32,8,128]{2,1,0:T(8,128)}), f32[32,8,128]{2,1,0:T(8,128)S(1)}, u32[]{:S(2)}, u32[]{:S(2)}) async-start(f32[32,8,128]{2,1,0:T(8,128)} %merge.1), calls=%async_computation.1 | async-start | bytes 262144 | tf_op jit(solution)/shard_map/all_to_all | solution.py:832
  154.9 0.7 copy-start.23
  165.8 5.8 %collective-permute-start.26 = (f32[128,128]{1,0:T(8,128)}, f32[128,128]{1,0:T(8,128)S(1)}, u32[]{:S(2)}, u32[]{:S(2)}) collective-permute-start(f32[128,128]{1,0:T(8,128)} %get-tuple-element.88), channel_id=1, source_target_pairs={{0,1},{1,2},{2,3},{3,0},{4,5},{5,6},{6,7},{7,4},{8,9},{9,10},{10,1... | collective-permute-start | bytes 196616 | tf_op jit(solution)/shard_map/ppermute | solution.py:683
  166.5 7.3 %collective-permute-start.27 = (f32[128,128]{1,0:T(8,128)}, f32[128,128]{1,0:T(8,128)S(1)}, u32[]{:S(2)}, u32[]{:S(2)}) collective-permute-start(f32[128,128]{1,0:T(8,128)} %get-tuple-element.89), channel_id=1, source_target_pairs={{0,2},{1,3},{2,0},{3,1},{4,6},{5,7},{6,4},{7,5},{8,10},{9,11},{10,... | collective-permute-start | bytes 196616 | tf_op jit(solution)/shard_map/ppermute | solution.py:683
  170.0 4.5 %collective-permute-start.28 = (f32[128,128]{1,0:T(8,128)}, f32[128,128]{1,0:T(8,128)S(1)}, u32[]{:S(2)}, u32[]{:S(2)}) collective-permute-start(f32[128,128]{1,0:T(8,128)} %get-tuple-element.90), channel_id=1, source_target_pairs={{0,3},{1,0},{2,1},{3,2},{4,7},{5,4},{6,5},{7,6},{8,11},{9,8},{10,9... | collective-permute-start | bytes 196616 | tf_op jit(solution)/shard_map/ppermute | solution.py:683
  171.5 2.9 %copy-start.24 = (f32[128,128]{1,0:T(8,128)}, f32[128,128]{1,0:T(8,128)S(1)}, u32[]{:S(2)}) copy-start(f32[128,128]{1,0:T(8,128)S(1)} %collective-permute-done.26.o1) | copy-start | bytes 196612
  173.7 0.7 copy-start.25
  174.5 0.6 copy-start.26
  (1 other events, 0.6 us)

commit v4 on v3

--- a/solution.py
+++ b/solution.py
@@ -349,7 +349,7 @@
             new.append(total + (v[0:8] + v[8:16]))
         return tuple(new)
 
-    totals = lax.fori_loop(0, TR // 16, step, tuple(totals))
+    totals = lax.fori_loop(0, TR // 16, step, tuple(totals), unroll=4)
     row = lax.broadcasted_iota(jnp.int32, (8, LANES), 0)
     lane = lax.broadcasted_iota(jnp.int32, (8, LANES), 1)
     sums = normal[...]

time: 178 us -> 177 us (level)
  no operation moved by 1% of the time
where the time goes in v4:
time: 177 us; the launch traced here: 176 us
  Pallas kernels  73.5 us (42%)
  starting transfers between devices  60.8 us (34%)
  waiting for transfers between devices  29.3 us (17%)
  local copies, waits for them, and re-layouts  10.5 us (6%)
    ppermute x21, starting transfers between devices, exchange(): lax.ppermute(pieces[k], axis, route(k))  37.9 us
    ppermute x21, waiting for transfers between devices, exchange(): lax.ppermute(pieces[k], axis, route(k))  28.6 us
    pallas_call x1, Pallas kernels, shards(): call(adjoint_kernel, (sds((NBANDS + 1, TR, LANES), f32), sds((8, LANES),...  12.8 us
    pallas_call x1, Pallas kernels, shards(): call(main_kernel, (sds((QROWS, LANES), f32),) * 4 + (sds((NBANDS + 1,), f...  10.2 us
    unnamed x68, local copies, waits for them, and re-layouts  9.17 us
    pallas_call x1, Pallas kernels, shards(): call(scatter_kernel, (part,) * 8, [SMEM] + [ANY] * 9, scratch=scatter_scr...  8.82 us
    pallas_call x1, Pallas kernels, shards(): call(assemble_kernel, (sds((RQ, COLS), f32), sds((GROUPS, KROWS, 6 * LANE...  7.98 us
    pallas_call x1, Pallas kernels, shards(): call(bands_kernel, (sds((NBANDS + 1, RQ, COLS), bf16), sds((NBANDS, RQ, C...  6.82 us
  transfers between devices with their start and end apart: 31, of which 12 were waited for; matrix products, arithmetic and copies ran while one was open for 1% of the time, Pallas kernels for 31%

profile of v4, /device:TPU:2, one launch (start us, length us, event | category | flops | bytes accessed | tf_op | source)
XLA Modules:
  0.0 176.4 jit_solution(5891686691688499284)
XLA Ops:
  0.6 2.4 %slab.1 = (bf16[7,64,128]{2,1,0:T(8,128)(2,1)}, bf16[7,64,128]{2,1,0:T(8,128)(2,1)}) custom-call(bf16[6,512,128]{2,1,0:T(8,128)(2,1)} %reflect.3, s32[512,128]{1,0:T(8,128)} %land.3), custom_call_target="tpu_custom_call" | custom-call | tf_op jit(solution)/shard_map/slab/pallas_call | solution.py:725
  3.0 3.5 %collective-permute-start = (bf16[7,64,128]{2,1,0:T(8,128)(2,1)}, bf16[7,64,128]{2,1,0:T(8,128)(2,1)S(1)}, u32[]{:S(2)}, u32[]{:S(2)}) collective-permute-start(bf16[7,64,128]{2,1,0:T(8,128)(2,1)} %get-tuple-element.51), channel_id=1, source_target_pairs={{0,1},{1,2},{2,3},{4,5},{5,6},{6,7},{8,9},{9,10},{10,11},{12,13},{... | collective-permute-start | bytes 344072 | tf_op jit(solution)/shard_map/ppermute | solution.py:728
  6.5 1.3 collective-permute-start.1
  7.8 0.6 stack.63.info
  8.4 4.1 %pack.1 = (bf16[3088,128]{1,0:T(8,128)(2,1)}, bf16[3088,128]{1,0:T(8,128)(2,1)}, bf16[3088,128]{1,0:T(8,128)(2,1)}, bf16[3088,128]{1,0:T(8,128)(2,1)}) custom-call(s32[8]{0:T(128)} %stack.63.info, s32[12]{0:T(128)} %dest.1, s32[12]{0:T(128)} %offset.1, bf16[12,128,512]{2,1,0:T(8,128)(2,1)} %temp.1, bf16[12,128,512]{2,1,0:T(8,128)(2,1)} %qual.1), custom_call_target="tpu_custom_call" | custom-call | tf_op jit(solution)/shard_map/pack/pallas_call | solution.py:730
  12.6 0.8 collective-permute-done.1.refs_4_.right
  13.4 0.6 copy-done.4
  14.0 3.6 %collective-permute-start.5 = (bf16[3088,128]{1,0:T(8,128)(2,1)}, bf16[3088,128]{1,0:T(8,128)(2,1)S(1)}, u32[]{:S(2)}, u32[]{:S(2)}) collective-permute-start(bf16[3088,128]{1,0:T(8,128)(2,1)} %get-tuple-element.58), channel_id=1, source_target_pairs={{0,2},{1,3},{2,0},{3,1},{4,6},{5,7},{6,4},{7,5},{8,10},{9,11},{10,... | collective-permute-start | bytes 2371592 | tf_op jit(solution)/shard_map/ppermute | solution.py:683
  17.6 0.7 collective-permute-start.2
  18.3 2.6 %collective-permute-start.6 = (bf16[3088,128]{1,0:T(8,128)(2,1)}, bf16[3088,128]{1,0:T(8,128)(2,1)S(1)}, u32[]{:S(2)}, u32[]{:S(2)}) collective-permute-start(bf16[3088,128]{1,0:T(8,128)(2,1)} %get-tuple-element.60), channel_id=1, source_target_pairs={{0,3},{1,0},{2,1},{3,2},{4,7},{5,4},{6,5},{7,6},{8,11},{9,8},{10,9... | collective-permute-start | bytes 2371592 | tf_op jit(solution)/shard_map/ppermute | solution.py:683
  20.9 0.7 maximum_bitcast_fusion.taps
  21.6 1.8 %edges.1 = (bf16[9,16,256]{2,1,0:T(8,128)(2,1)}, bf16[9,16,256]{2,1,0:T(8,128)(2,1)}) custom-call(bf16[6,512,128]{2,1,0:T(8,128)(2,1)} %reflect.3, bf16[6,512,128]{2,1,0:T(8,128)(2,1)} %reflect.3, s32[512,128]{1,0:T(8,128)} %land.3, s32[512,128]{1,0:T(8,128)} %land.3, f32[512,128]{1,0:T(8,128)} %refs_8_.1, f32[512,128]{1,0:T(8,128)} %refs_8_.1, ...), custom_call_target="tpu_custom_call" | custom-call | tf_op jit(solution)/shard_map/edges/pallas_call | solution.py:741
  23.3 1.9 %collective-permute-start.3 = (bf16[9,16,256]{2,1,0:T(8,128)(2,1)}, bf16[9,16,256]{2,1,0:T(8,128)(2,1)S(1)}, u32[]{:S(2)}, u32[]{:S(2)}) collective-permute-start(bf16[9,16,256]{2,1,0:T(8,128)(2,1)} %get-tuple-element.54), channel_id=1, source_target_pairs={{0,4},{4,8},{8,12},{12,16},{16,20},{20,24},{24,28},{28,32},{32,36}... | collective-permute-start | bytes 221192 | tf_op jit(solution)/shard_map/ppermute | solution.py:744
  25.3 5.8 %collective-permute-start.4 = (bf16[9,16,256]{2,1,0:T(8,128)(2,1)}, bf16[9,16,256]{2,1,0:T(8,128)(2,1)S(1)}, u32[]{:S(2)}, u32[]{:S(2)}) collective-permute-start(bf16[9,16,256]{2,1,0:T(8,128)(2,1)} %get-tuple-element.55), channel_id=1, source_target_pairs={{4,0},{8,4},{12,8},{16,12},{20,16},{24,20},{28,24},{32,28},{36,32}... | collective-permute-start | bytes 221192 | tf_op jit(solution)/shard_map/ppermute | solution.py:745
  31.1 0.7 broadcast_in_dim.2.bias
  31.8 4.5 %matrices.1 = (bf16[3,128,480]{2,1,0:T(8,128)(2,1)}, f32[3,128,128]{2,1,0:T(8,128)}) custom-call(bf16[3,3,3,16,16]{4,3,2,1,0:T(8,128)(2,1)} %maximum_bitcast_fusion.taps, f32[48,128]{1,0:T(8,128)} %broadcast_in_dim.2.bias), custom_call_target="tpu_custom_call" | custom-call | tf_op jit(solution)/shard_map/matrices/pallas_call | solution.py:763
  37.0 0.6 copy-done.16
  37.6 12.8 %adjoint.1 = (f32[7,512,128]{2,1,0:T(8,128)}, f32[8,128]{1,0:T(8,128)}, bf16[7,544,128]{2,1,0:T(8,128)(2,1)}) custom-call(bf16[6,512,128]{2,1,0:T(8,128)(2,1)} %reflect.3, s32[512,128]{1,0:T(8,128)} %land.3, bf16[9,16,256]{2,1,0:T(8,128)(2,1)} %copy-done.15, bf16[9,16,256]{2,1,0:T(8,128)(2,1)} %copy-done.16, bf16[7,64,128]{2,1,0:T(8,128)(2,1)} %copy-done.3, ...), custom_call_target="tpu_custom_call" | custom-call | tf_op jit(solution)/shard_map/adjoint/pallas_call | solution.py:747
  50.4 0.9 copy-done
  51.3 2.3 %cut.1.refs_1_.refs_8_ = bf16[4,7,160,128]{3,2,1,0:T(8,128)(2,1)} custom-call(bf16[7,544,128]{2,1,0:T(8,128)(2,1)} %get-tuple-element.59.window, bf16[3088,128]{1,0:T(8,128)(2,1)} %copy-done), custom_call_target="tpu_custom_call" | custom-call | tf_op jit(solution)/shard_map/cut/pallas_call | solution.py:775
  53.6 0.9 copy-done.1
  55.1 3.5 %all-to-all-start = ((bf16[4,7,160,128]{3,2,1,0:T(8,128)(2,1)}), bf16[4,7,160,128]{3,2,1,0:T(8,128)(2,1)S(1)}, u32[]{:S(2)}, u32[]{:S(2)}) async-start(bf16[4,7,160,128]{3,2,1,0:T(8,128)(2,1)} %cut.1.refs_1_.refs_8_), calls=%async_computation | async-start | bytes 2293760 | tf_op jit(solution)/shard_map/all_to_all | solution.py:781
  58.7 0.9 copy-done.7
  59.6 8.8 %scatter.1 = (bf16[4,544,128]{2,1,0:T(8,128)(2,1)}, bf16[4,544,128]{2,1,0:T(8,128)(2,1)}, bf16[4,544,128]{2,1,0:T(8,128)(2,1)}, bf16[4,544,128]{2,1,0:T(8,128)(2...) custom-call(s32[8]{0:T(128)} %stack.63.info, ...), custom_call_target="tpu_custom_call" | custom-call | flops 12582912 | bytes 12582912 | tf_op jit(solution)/shard_map/scatter/pallas_call | solution.py:797
  68.7 3.7 %collective-permute-start.18 = (bf16[4,544,128]{2,1,0:T(8,128)(2,1)}, bf16[4,544,128]{2,1,0:T(8,128)(2,1)}, u32[]{:S(2)}, u32[]{:S(2)}) collective-permute-start(bf16[4,544,128]{2,1,0:T(8,128)(2,1)} %get-tuple-element.72), channel_id=1, source_target_pairs={{0,16},{4,20},{8,24},{12,28},{16,0},{20,4},{24,8},{28,12},{32,48},... | collective-permute-start | bytes 1671176 | tf_op jit(solution)/shard_map/ppermute | solution.py:683
  72.4 1.1 collective-permute-start.19
  73.4 1.5 collective-permute-start.11
  74.9 1.1 collective-permute-start.12
  76.0 9.9 %collective-permute-done.17.b = bf16[4,544,128]{2,1,0:T(8,128)(2,1)S(1)} collective-permute-done((bf16[4,544,128]{2,1,0:T(8,128)(2,1)}, bf16[4,544,128]{2,1,0:T(8,128)(2,1)S(1)}, u32[]{:S(2)}, u32[]{:S(2)}) %collective-permute-start.17) | collective-permute-done | bytes 557088 | tf_op jit(solution)/shard_map/ppermute | solution.py:683
  85.9 1.0 copy-done.2
  86.9 6.8 %bands.1 = (bf16[7,160,512]{2,1,0:T(8,128)(2,1)}, f32[6,160,512]{2,1,0:T(8,128)}) custom-call(s32[8]{0:T(128)} %stack.63.info, bf16[4,7,160,128]{3,2,1,0:T(8,128)(2,1)} %copy-done.2, bf16[160,160]{1,0:T(8,128)(2,1)} %constant.73.clone.row_h, bf16[160,160]{1,0:T(8,128)(2,1)} %constant.74.clone.row_l, bf16[512,512]{1,0:T(8,128)(2,1)} %constant.75.clone.col_h, ...), custom_call_target="tpu_custom_call" | custom-call | flops 1824522240 | bytes 10485760 | tf_op jit(solution)/shard_map/bands/pallas_call | solution.py:782
  93.8 3.1 %collective-permute-done.18.c = bf16[4,544,128]{2,1,0:T(8,128)(2,1)} collective-permute-done((bf16[4,544,128]{2,1,0:T(8,128)(2,1)}, bf16[4,544,128]{2,1,0:T(8,128)(2,1)}, u32[]{:S(2)}, u32[]{:S(2)}) %collective-permute-start.18) | collective-permute-done | bytes 557088 | tf_op jit(solution)/shard_map/ppermute | solution.py:683
  97.4 2.6 %add.14 = (f32[544,128]{1,0:T(8,128)}, f32[544,128]{1,0:T(8,128)}, f32[544,128]{1,0:T(8,128)}, f32[544,128]{1,0:T(8,128)}) custom-call(bf16[4,544,128]{2,1,0:T(8,128)(2,1)} %get-tuple-element.70.a, bf16[4,544,128]{2,1,0:T(8,128)(2,1)} %copy-done.11, bf16[4,544,128]{2,1,0:T(8,128)(2,1)} %collective-permute-done.18.c, ...), custom_call_target="tpu_custom_call" | custom-call | bytes 3145728 | tf_op jit(solution)/shard_map/add/pallas_call | solution.py:813
  100.0 1.5 collective-permute-start.20
  101.5 0.7 collective-permute-start.21
  102.2 2.6 %collective-permute-start.22 = (f32[544,128]{1,0:T(8,128)}, f32[544,128]{1,0:T(8,128)S(1)}, u32[]{:S(2)}, u32[]{:S(2)}) collective-permute-start(f32[544,128]{1,0:T(8,128)} %get-tuple-element.77), channel_id=1, source_target_pairs={{0,96},{4,100},{8,104},{12,108},{16,112},{20,116},{24,120},{28,124... | collective-permute-start | bytes 835592 | tf_op jit(solution)/shard_map/ppermute | solution.py:683
  104.8 0.8 copy-done.9
  105.8 2.6 %add.13 = (f32[544,128]{1,0:T(8,128)}, f32[544,128]{1,0:T(8,128)}, f32[544,128]{1,0:T(8,128)}, f32[544,128]{1,0:T(8,128)}) custom-call(bf16[4,544,128]{2,1,0:T(8,128)(2,1)} %get-tuple-element.61.a, bf16[4,544,128]{2,1,0:T(8,128)(2,1)} %copy-done.8, bf16[4,544,128]{2,1,0:T(8,128)(2,1)} %copy-done.9, bf16[4,544,128]{2,1,0:T(8,128)(2,1)} %copy-done.10, ...), custom_call_target="tpu_custom_call" | custom-call | bytes 3145728 | tf_op jit(solution)/shard_map/add/pallas_call | solution.py:812
  108.4 3.3 %collective-permute-start.14 = (f32[544,128]{1,0:T(8,128)}, f32[544,128]{1,0:T(8,128)S(1)}, u32[]{:S(2)}, u32[]{:S(2)}) collective-permute-start(f32[544,128]{1,0:T(8,128)} %get-tuple-element.67), channel_id=1, source_target_pairs={{0,8},{4,12},{8,16},{12,20},{16,24},{20,28},{24,0},{28,4},{32,40},... | collective-permute-start | bytes 835592 | tf_op jit(solution)/shard_map/ppermute | solution.py:683
  111.7 2.4 %collective-permute-start.15 = (f32[544,128]{1,0:T(8,128)}, f32[544,128]{1,0:T(8,128)S(1)}, u32[]{:S(2)}, u32[]{:S(2)}) collective-permute-start(f32[544,128]{1,0:T(8,128)} %get-tuple-element.68), channel_id=1, source_target_pairs={{0,16},{4,20},{8,24},{12,28},{16,0},{20,4},{24,8},{28,12},{32,48},... | collective-permute-start | bytes 835592 | tf_op jit(solution)/shard_map/ppermute | solution.py:683
  114.1 2.6 %collective-permute-start.16 = (f32[544,128]{1,0:T(8,128)}, f32[544,128]{1,0:T(8,128)S(1)}, u32[]{:S(2)}, u32[]{:S(2)}) collective-permute-start(f32[544,128]{1,0:T(8,128)} %get-tuple-element.69), channel_id=1, source_target_pairs={{0,24},{4,28},{8,0},{12,4},{16,8},{20,12},{24,16},{28,20},{32,56},... | collective-permute-start | bytes 835592 | tf_op jit(solution)/shard_map/ppermute | solution.py:683
  116.8 2.8 %collective-permute-done.14.refs_1_ = f32[544,128]{1,0:T(8,128)S(1)} collective-permute-done((f32[544,128]{1,0:T(8,128)}, f32[544,128]{1,0:T(8,128)S(1)}, u32[]{:S(2)}, u32[]{:S(2)}) %collective-permute-start.14) | collective-permute-done | bytes 278560 | tf_op jit(solution)/shard_map/ppermute | solution.py:683
  119.5 4.9 %collective-permute-done.15.refs_2_ = f32[544,128]{1,0:T(8,128)S(1)} collective-permute-done((f32[544,128]{1,0:T(8,128)}, f32[544,128]{1,0:T(8,128)S(1)}, u32[]{:S(2)}, u32[]{:S(2)}) %collective-permute-start.15) | collective-permute-done | bytes 278560 | tf_op jit(solution)/shard_map/ppermute | solution.py:683
  124.5 0.7 copy-done.21
  125.2 3.4 %blend.1 = (f32[168,128]{1,0:T(8,128)}, f32[168,128]{1,0:T(8,128)}, f32[168,128]{1,0:T(8,128)}, f32[168,128]{1,0:T(8,128)}) custom-call(s32[8]{0:T(128)} %stack.63.info, f32[544,128]{1,0:T(8,128)} %get-tuple-element.66.refs_0_, f32[544,128]{1,0:T(8,128)} %copy-done.20, f32[544,128]{1,0:T(8,128)} %copy-done.21, f32[544,128]{1,0:T(8,128)} %copy-done.22, ...), custom_call_target="tpu_custom_call" | custom-call | bytes 3145728 | tf_op jit(solution)/shard_map/blend/pallas_call | solution.py:816
  128.6 1.7 collective-permute-start.23
  130.4 2.7 %collective-permute-start.24 = (f32[168,128]{1,0:T(8,128)}, f32[168,128]{1,0:T(8,128)S(1)}, u32[]{:S(2)}, u32[]{:S(2)}) collective-permute-start(f32[168,128]{1,0:T(8,128)} %get-tuple-element.81), channel_id=1, source_target_pairs={{0,2},{1,3},{2,0},{3,1},{4,6},{5,7},{6,4},{7,5},{8,10},{9,11},{10,... | collective-permute-start | bytes 258056 | tf_op jit(solution)/shard_map/ppermute | solution.py:683
  133.0 1.5 collective-permute-start.25
  134.6 2.1 %collective-permute-done.24.b2 = f32[168,128]{1,0:T(8,128)S(1)} collective-permute-done((f32[168,128]{1,0:T(8,128)}, f32[168,128]{1,0:T(8,128)S(1)}, u32[]{:S(2)}, u32[]{:S(2)}) %collective-permute-start.24) | collective-permute-done | bytes 86048 | tf_op jit(solution)/shard_map/ppermute | solution.py:683
  136.6 1.1 collective-permute-done.25.b3
  137.7 0.6 copy-done.14
  138.4 1.4 merge.1
  139.7 6.2 %all-to-all-start.1 = ((f32[32,8,128]{2,1,0:T(8,128)}), f32[32,8,128]{2,1,0:T(8,128)S(1)}, u32[]{:S(2)}, u32[]{:S(2)}) async-start(f32[32,8,128]{2,1,0:T(8,128)} %merge.1), calls=%async_computation.1 | async-start | bytes 262144 | tf_op jit(solution)/shard_map/all_to_all | solution.py:832
  146.0 0.6 convert_element_type.2.head
  146.6 8.0 %assemble.1 = (f32[160,512]{1,0:T(8,128)}, bf16[20,160,768]{2,1,0:T(8,128)(2,1)}) custom-call(s32[8]{0:T(128)} %stack.63.info, f32[168,128]{1,0:T(8,128)} %get-tuple-element.79.b0, f32[168,128]{1,0:T(8,128)} %copy-done.12, f32[168,128]{1,0:T(8,128)} %copy-done.13, f32[168,128]{1,0:T(8,128)} %copy-done.14, bf16[160,160]{1,0:T(8,128)(2,1)} %constant.73.clone.row_h, ...), custom_call_target="tpu_custom_call" | custom-call | flops 330301440 | bytes 8388608 | tf_op jit(solution)/shard_map/assemble/pallas_call | solution.py:833
  154.6 0.6 copy-done.23
  155.2 10.2 %convolve.1 = (f32[128,128]{1,0:T(8,128)}, f32[128,128]{1,0:T(8,128)}, f32[128,128]{1,0:T(8,128)}, f32[128,128]{1,0:T(8,128)}, f32[7]{0:T(128)}) custom-call(s32[8]{0:T(128)} %stack.63.info, f32[16]{0:T(128)} %convert_element_type.2.head, f32[32,8,128]{2,1,0:T(8,128)} %copy-done.23, f32[160,512]{1,0:T(8,128)} %get-tuple-element.84.coarse_in, ...), custom_call_target="tpu_custom_call" | custom-call | flops 3397386240 | bytes 8388608 | tf_op jit(solution)/shard_map/convolve/pallas_call | solution.py:843
  165.5 0.7 collective-permute-start.26
  166.2 3.5 %collective-permute-start.27 = (f32[128,128]{1,0:T(8,128)}, f32[128,128]{1,0:T(8,128)S(1)}, u32[]{:S(2)}, u32[]{:S(2)}) collective-permute-start(f32[128,128]{1,0:T(8,128)} %get-tuple-element.89), channel_id=1, source_target_pairs={{0,2},{1,3},{2,0},{3,1},{4,6},{5,7},{6,4},{7,5},{8,10},{9,11},{10,... | collective-permute-start | bytes 196616 | tf_op jit(solution)/shard_map/ppermute | solution.py:683
  170.0 1.2 collective-permute-done.26.o1
  171.2 2.2 %collective-permute-done.27.o2 = f32[128,128]{1,0:T(8,128)S(1)} collective-permute-done((f32[128,128]{1,0:T(8,128)}, f32[128,128]{1,0:T(8,128)S(1)}, u32[]{:S(2)}, u32[]{:S(2)}) %collective-permute-start.27) | collective-permute-done | bytes 65568 | tf_op jit(solution)/shard_map/ppermute | solution.py:683
  173.4 0.7 collective-permute-done.28.o3
  174.1 0.6 copy-done.26
  174.8 1.7 join.1
  (89 shorter events, 2.9 us)
Async XLA Ops:
  3.0 9.6 %collective-permute-start = (bf16[7,64,128]{2,1,0:T(8,128)(2,1)}, bf16[7,64,128]{2,1,0:T(8,128)(2,1)S(1)}, u32[]{:S(2)}, u32[]{:S(2)}) collective-permute-start(bf16[7,64,128]{2,1,0:T(8,128)(2,1)} %get-tuple-element.51), channel_id=1, source_target_pairs={{0,1},{1,2},{2,3},{4,5},{5,6},{6,7},{8,9},{9,10},{10,11},{12,13},{... | collective-permute-start | bytes 344072 | tf_op jit(solution)/shard_map/ppermute | solution.py:728
  6.5 6.9 %collective-permute-start.1 = (bf16[7,64,128]{2,1,0:T(8,128)(2,1)}, bf16[7,64,128]{2,1,0:T(8,128)(2,1)S(1)}, u32[]{:S(2)}, u32[]{:S(2)}) collective-permute-start(bf16[7,64,128]{2,1,0:T(8,128)(2,1)} %get-tuple-element.52), channel_id=1, source_target_pairs={{1,0},{2,1},{3,2},{5,4},{6,5},{7,6},{9,8},{10,9},{11,10},{13,12},{... | collective-permute-start | bytes 344072 | tf_op jit(solution)/shard_map/ppermute | solution.py:729
  12.6 8.3 %copy-start.27 = (bf16[16,16,3,3]{1,0,3,2:T(8,128)(2,1)S(1)}, bf16[16,16,3,3]{1,0,3,2:T(8,128)(2,1)}, u32[]{:S(2)}) copy-start(bf16[16,16,3,3]{1,0,3,2:T(8,128)(2,1)} %param.33) | copy-start | bytes 13828
  12.6 8.3 %copy-start.28 = (bf16[16,16,3,3]{1,0,3,2:T(8,128)(2,1)S(1)}, bf16[16,16,3,3]{1,0,3,2:T(8,128)(2,1)}, u32[]{:S(2)}) copy-start(bf16[16,16,3,3]{1,0,3,2:T(8,128)(2,1)} %param.31) | copy-start | bytes 13828
  12.6 8.3 %copy-start.29 = (bf16[16,16,3,3]{1,0,3,2:T(8,128)(2,1)S(1)}, bf16[16,16,3,3]{1,0,3,2:T(8,128)(2,1)}, u32[]{:S(2)}) copy-start(bf16[16,16,3,3]{1,0,3,2:T(8,128)(2,1)} %param.29) | copy-start | bytes 13828
  12.6 0.8 copy-start.3
  13.4 0.7 copy-start.4
  14.0 17.0 %copy-start.30 = (f32[16]{0:T(128)S(1)}, f32[16]{0:T(128)}, u32[]{:S(2)}) copy-start(f32[16]{0:T(128)} %param.34) | copy-start | bytes 196
  14.0 17.0 %copy-start.31 = (f32[16]{0:T(128)S(1)}, f32[16]{0:T(128)}, u32[]{:S(2)}) copy-start(f32[16]{0:T(128)} %param.32) | copy-start | bytes 196
  14.0 17.0 %copy-start.32 = (f32[16]{0:T(128)S(1)}, f32[16]{0:T(128)}, u32[]{:S(2)}) copy-start(f32[16]{0:T(128)} %param.30) | copy-start | bytes 196
  14.0 36.4 %collective-permute-start.5 = (bf16[3088,128]{1,0:T(8,128)(2,1)}, bf16[3088,128]{1,0:T(8,128)(2,1)S(1)}, u32[]{:S(2)}, u32[]{:S(2)}) collective-permute-start(bf16[3088,128]{1,0:T(8,128)(2,1)} %get-tuple-element.58), channel_id=1, source_target_pairs={{0,2},{1,3},{2,0},{3,1},{4,6},{5,7},{6,4},{7,5},{8,10},{9,11},{10,... | collective-permute-start | bytes 2371592 | tf_op jit(solution)/shard_map/ppermute | solution.py:683
  17.6 35.9 %collective-permute-start.2 = (bf16[3088,128]{1,0:T(8,128)(2,1)}, bf16[3088,128]{1,0:T(8,128)(2,1)S(1)}, u32[]{:S(2)}, u32[]{:S(2)}) collective-permute-start(bf16[3088,128]{1,0:T(8,128)(2,1)} %get-tuple-element.53), channel_id=1, source_target_pairs={{0,1},{1,2},{2,3},{3,0},{4,5},{5,6},{6,7},{7,4},{8,9},{9,10},{10,1... | collective-permute-start | bytes 2371592 | tf_op jit(solution)/shard_map/ppermute | solution.py:683
  18.3 36.7 %collective-permute-start.6 = (bf16[3088,128]{1,0:T(8,128)(2,1)}, bf16[3088,128]{1,0:T(8,128)(2,1)S(1)}, u32[]{:S(2)}, u32[]{:S(2)}) collective-permute-start(bf16[3088,128]{1,0:T(8,128)(2,1)} %get-tuple-element.60), channel_id=1, source_target_pairs={{0,3},{1,0},{2,1},{3,2},{4,7},{5,4},{6,5},{7,6},{8,11},{9,8},{10,9... | collective-permute-start | bytes 2371592 | tf_op jit(solution)/shard_map/ppermute | solution.py:683
  20.9 15.4 %copy-start.5 = (bf16[3088,128]{1,0:T(8,128)(2,1)S(1)}, bf16[3088,128]{1,0:T(8,128)(2,1)}, u32[]{:S(2)}) copy-start(bf16[3088,128]{1,0:T(8,128)(2,1)} %get-tuple-element.47.refs_0_) | copy-start | bytes 2371588
  23.3 13.0 %collective-permute-start.3 = (bf16[9,16,256]{2,1,0:T(8,128)(2,1)}, bf16[9,16,256]{2,1,0:T(8,128)(2,1)S(1)}, u32[]{:S(2)}, u32[]{:S(2)}) collective-permute-start(bf16[9,16,256]{2,1,0:T(8,128)(2,1)} %get-tuple-element.54), channel_id=1, source_target_pairs={{0,4},{4,8},{8,12},{12,16},{16,20},{20,24},{24,28},{28,32},{32,36}... | collective-permute-start | bytes 221192 | tf_op jit(solution)/shard_map/ppermute | solution.py:744
  25.3 11.2 %collective-permute-start.4 = (bf16[9,16,256]{2,1,0:T(8,128)(2,1)}, bf16[9,16,256]{2,1,0:T(8,128)(2,1)S(1)}, u32[]{:S(2)}, u32[]{:S(2)}) collective-permute-start(bf16[9,16,256]{2,1,0:T(8,128)(2,1)} %get-tuple-element.55), channel_id=1, source_target_pairs={{4,0},{8,4},{12,8},{16,12},{20,16},{24,20},{28,24},{32,28},{36,32}... | collective-permute-start | bytes 221192 | tf_op jit(solution)/shard_map/ppermute | solution.py:745
  36.3 0.6 copy-start.15
  36.3 22.3 %collective-permute-start.7 = (bf16[3088,128]{1,0:T(8,128)(2,1)S(1)}, bf16[3088,128]{1,0:T(8,128)(2,1)S(1)}, u32[]{:S(2)}, u32[]{:S(2)}) collective-permute-start(bf16[3088,128]{1,0:T(8,128)(2,1)S(1)} %copy-done.5), channel_id=1, source_target_pairs={{0,4},{4,0},{8,12},{12,8},{16,20},{20,16},{24,28},{28,24},{32,36},... | collective-permute-start | bytes 2371592 | tf_op jit(solution)/shard_map/ppermute | solution.py:794
  50.4 0.9 copy-start
  53.6 5.1 %collective-permute-start.9 = (bf16[3088,128]{1,0:T(8,128)(2,1)}, bf16[3088,128]{1,0:T(8,128)(2,1)}, u32[]{:S(2)}, u32[]{:S(2)}) collective-permute-start(bf16[3088,128]{1,0:T(8,128)(2,1)} %order.5.refs_2_), channel_id=1, source_target_pairs={{0,4},{4,0},{8,12},{12,8},{16,20},{20,16},{24,28},{28,24},{32,36},... | collective-permute-start | bytes 2371592 | tf_op jit(solution)/shard_map/ppermute | solution.py:794
  53.6 0.9 copy-start.1
  54.5 4.2 %collective-permute-start.8 = (bf16[3088,128]{1,0:T(8,128)(2,1)}, bf16[3088,128]{1,0:T(8,128)(2,1)}, u32[]{:S(2)}, u32[]{:S(2)}) collective-permute-start(bf16[3088,128]{1,0:T(8,128)(2,1)} %order.4.refs_1_), channel_id=1, source_target_pairs={{0,4},{4,0},{8,12},{12,8},{16,20},{20,16},{24,28},{28,24},{32,36},... | collective-permute-start | bytes 2371592 | tf_op jit(solution)/shard_map/ppermute | solution.py:794
  55.0 3.7 %copy-start.6 = (bf16[3088,128]{1,0:T(8,128)(2,1)}, bf16[3088,128]{1,0:T(8,128)(2,1)S(1)}, u32[]{:S(2)}) copy-start(bf16[3088,128]{1,0:T(8,128)(2,1)S(1)} %collective-permute-done.6.refs_3_) | copy-start | bytes 2371588
  55.0 3.7 %collective-permute-start.10 = (bf16[3088,128]{1,0:T(8,128)(2,1)S(1)}, bf16[3088,128]{1,0:T(8,128)(2,1)}, u32[]{:S(2)}, u32[]{:S(2)}) collective-permute-start(bf16[3088,128]{1,0:T(8,128)(2,1)S(1)} %collective-permute-done.6.refs_3_), channel_id=1, source_target_pairs={{0,4},{4,0},{8,12},{12,8},{16,20},{20,16},{24,28},{28,24},{32,36},... | collective-permute-start | bytes 2371592 | tf_op jit(solution)/shard_map/ppermute | solution.py:794
  55.1 30.8 %all-to-all-start = ((bf16[4,7,160,128]{3,2,1,0:T(8,128)(2,1)}), bf16[4,7,160,128]{3,2,1,0:T(8,128)(2,1)S(1)}, u32[]{:S(2)}, u32[]{:S(2)}) async-start(bf16[4,7,160,128]{3,2,1,0:T(8,128)(2,1)} %cut.1.refs_1_.refs_8_), calls=%async_computation | async-start | bytes 2293760 | tf_op jit(solution)/shard_map/all_to_all | solution.py:781
  58.6 0.9 copy-start.7
  68.4 17.5 %collective-permute-start.17 = (bf16[4,544,128]{2,1,0:T(8,128)(2,1)}, bf16[4,544,128]{2,1,0:T(8,128)(2,1)S(1)}, u32[]{:S(2)}, u32[]{:S(2)}) collective-permute-start(bf16[4,544,128]{2,1,0:T(8,128)(2,1)} %get-tuple-element.71), channel_id=1, source_target_pairs={{0,8},{4,12},{8,16},{12,20},{16,24},{20,28},{24,0},{28,4},{32,40},... | collective-permute-start | bytes 1671176 | tf_op jit(solution)/shard_map/ppermute | solution.py:683
  68.7 28.2 %collective-permute-start.18 = (bf16[4,544,128]{2,1,0:T(8,128)(2,1)}, bf16[4,544,128]{2,1,0:T(8,128)(2,1)}, u32[]{:S(2)}, u32[]{:S(2)}) collective-permute-start(bf16[4,544,128]{2,1,0:T(8,128)(2,1)} %get-tuple-element.72), channel_id=1, source_target_pairs={{0,16},{4,20},{8,24},{12,28},{16,0},{20,4},{24,8},{28,12},{32,48},... | collective-permute-start | bytes 1671176 | tf_op jit(solution)/shard_map/ppermute | solution.py:683
  72.4 25.0 %collective-permute-start.19 = (bf16[4,544,128]{2,1,0:T(8,128)(2,1)}, bf16[4,544,128]{2,1,0:T(8,128)(2,1)}, u32[]{:S(2)}, u32[]{:S(2)}) collective-permute-start(bf16[4,544,128]{2,1,0:T(8,128)(2,1)} %get-tuple-element.73), channel_id=1, source_target_pairs={{0,24},{4,28},{8,0},{12,4},{16,8},{20,12},{24,16},{28,20},{32,56},... | collective-permute-start | bytes 1671176 | tf_op jit(solution)/shard_map/ppermute | solution.py:683
  73.4 28.8 %collective-permute-start.11 = (bf16[4,544,128]{2,1,0:T(8,128)(2,1)}, bf16[4,544,128]{2,1,0:T(8,128)(2,1)S(1)}, u32[]{:S(2)}, u32[]{:S(2)}) collective-permute-start(bf16[4,544,128]{2,1,0:T(8,128)(2,1)} %get-tuple-element.62), channel_id=1, source_target_pairs={{0,32},{4,36},{8,40},{12,44},{16,48},{20,52},{24,56},{28,60},{32,6... | collective-permute-start | bytes 1671176 | tf_op jit(solution)/shard_map/ppermute | solution.py:683
  74.9 29.9 %collective-permute-start.12 = (bf16[4,544,128]{2,1,0:T(8,128)(2,1)}, bf16[4,544,128]{2,1,0:T(8,128)(2,1)S(1)}, u32[]{:S(2)}, u32[]{:S(2)}) collective-permute-start(bf16[4,544,128]{2,1,0:T(8,128)(2,1)} %get-tuple-element.63), channel_id=1, source_target_pairs={{0,64},{4,68},{8,72},{12,76},{16,80},{20,84},{24,88},{28,92},{32,9... | collective-permute-start | bytes 1671176 | tf_op jit(solution)/shard_map/ppermute | solution.py:683
  85.9 11.5 %copy-start.11 = (bf16[4,544,128]{2,1,0:T(8,128)(2,1)}, bf16[4,544,128]{2,1,0:T(8,128)(2,1)S(1)}, u32[]{:S(2)}) copy-start(bf16[4,544,128]{2,1,0:T(8,128)(2,1)S(1)} %collective-permute-done.17.b) | copy-start | bytes 1671172
  85.9 18.9 %collective-permute-start.13 = (bf16[4,544,128]{2,1,0:T(8,128)(2,1)}, bf16[4,544,128]{2,1,0:T(8,128)(2,1)S(1)}, u32[]{:S(2)}, u32[]{:S(2)}) collective-permute-start(bf16[4,544,128]{2,1,0:T(8,128)(2,1)} %get-tuple-element.64), channel_id=1, source_target_pairs={{0,96},{4,100},{8,104},{12,108},{16,112},{20,116},{24,120},{28,124... | collective-permute-start | bytes 1671176 | tf_op jit(solution)/shard_map/ppermute | solution.py:683
  85.9 1.0 copy-start.2
  100.0 14.1 %collective-permute-start.20 = (f32[544,128]{1,0:T(8,128)}, f32[544,128]{1,0:T(8,128)S(1)}, u32[]{:S(2)}, u32[]{:S(2)}) collective-permute-start(f32[544,128]{1,0:T(8,128)} %get-tuple-element.75), channel_id=1, source_target_pairs={{0,32},{4,36},{8,40},{12,44},{16,48},{20,52},{24,56},{28,60},{32,6... | collective-permute-start | bytes 835592 | tf_op jit(solution)/shard_map/ppermute | solution.py:683
  101.5 15.3 %collective-permute-start.21 = (f32[544,128]{1,0:T(8,128)}, f32[544,128]{1,0:T(8,128)S(1)}, u32[]{:S(2)}, u32[]{:S(2)}) collective-permute-start(f32[544,128]{1,0:T(8,128)} %get-tuple-element.76), channel_id=1, source_target_pairs={{0,64},{4,68},{8,72},{12,76},{16,80},{20,84},{24,88},{28,92},{32,9... | collective-permute-start | bytes 835592 | tf_op jit(solution)/shard_map/ppermute | solution.py:683
  102.2 2.6 %copy-start.8 = (bf16[4,544,128]{2,1,0:T(8,128)(2,1)}, bf16[4,544,128]{2,1,0:T(8,128)(2,1)S(1)}, u32[]{:S(2)}) copy-start(bf16[4,544,128]{2,1,0:T(8,128)(2,1)S(1)} %collective-permute-done.11.b) | copy-start | bytes 1671172
  102.2 14.6 %collective-permute-start.22 = (f32[544,128]{1,0:T(8,128)}, f32[544,128]{1,0:T(8,128)S(1)}, u32[]{:S(2)}, u32[]{:S(2)}) collective-permute-start(f32[544,128]{1,0:T(8,128)} %get-tuple-element.77), channel_id=1, source_target_pairs={{0,96},{4,100},{8,104},{12,108},{16,112},{20,116},{24,120},{28,124... | collective-permute-start | bytes 835592 | tf_op jit(solution)/shard_map/ppermute | solution.py:683
  104.8 0.8 copy-start.9
  104.8 1.0 copy-start.10
  108.4 11.1 %collective-permute-start.14 = (f32[544,128]{1,0:T(8,128)}, f32[544,128]{1,0:T(8,128)S(1)}, u32[]{:S(2)}, u32[]{:S(2)}) collective-permute-start(f32[544,128]{1,0:T(8,128)} %get-tuple-element.67), channel_id=1, source_target_pairs={{0,8},{4,12},{8,16},{12,20},{16,24},{20,28},{24,0},{28,4},{32,40},... | collective-permute-start | bytes 835592 | tf_op jit(solution)/shard_map/ppermute | solution.py:683
  111.7 12.7 %collective-permute-start.15 = (f32[544,128]{1,0:T(8,128)}, f32[544,128]{1,0:T(8,128)S(1)}, u32[]{:S(2)}, u32[]{:S(2)}) collective-permute-start(f32[544,128]{1,0:T(8,128)} %get-tuple-element.68), channel_id=1, source_target_pairs={{0,16},{4,20},{8,24},{12,28},{16,0},{20,4},{24,8},{28,12},{32,48},... | collective-permute-start | bytes 835592 | tf_op jit(solution)/shard_map/ppermute | solution.py:683
  114.1 10.3 %copy-start.17 = (f32[544,128]{1,0:T(8,128)}, f32[544,128]{1,0:T(8,128)S(1)}, u32[]{:S(2)}) copy-start(f32[544,128]{1,0:T(8,128)S(1)} %collective-permute-done.20.refs_5_) | copy-start | bytes 835588
  114.1 10.3 %collective-permute-start.16 = (f32[544,128]{1,0:T(8,128)}, f32[544,128]{1,0:T(8,128)S(1)}, u32[]{:S(2)}, u32[]{:S(2)}) collective-permute-start(f32[544,128]{1,0:T(8,128)} %get-tuple-element.69), channel_id=1, source_target_pairs={{0,24},{4,28},{8,0},{12,4},{16,8},{20,12},{24,16},{28,20},{32,56},... | collective-permute-start | bytes 835592 | tf_op jit(solution)/shard_map/ppermute | solution.py:683
  116.7 7.7 %copy-start.18 = (f32[544,128]{1,0:T(8,128)}, f32[544,128]{1,0:T(8,128)S(1)}, u32[]{:S(2)}) copy-start(f32[544,128]{1,0:T(8,128)S(1)} %collective-permute-done.21.refs_6_) | copy-start | bytes 835588
  116.8 7.7 %copy-start.19 = (f32[544,128]{1,0:T(8,128)}, f32[544,128]{1,0:T(8,128)S(1)}, u32[]{:S(2)}) copy-start(f32[544,128]{1,0:T(8,128)S(1)} %collective-permute-done.22.refs_7_) | copy-start | bytes 835588
  119.5 4.9 %copy-start.20 = (f32[544,128]{1,0:T(8,128)}, f32[544,128]{1,0:T(8,128)S(1)}, u32[]{:S(2)}) copy-start(f32[544,128]{1,0:T(8,128)S(1)} %collective-permute-done.14.refs_1_) | copy-start | bytes 835588
  124.4 0.7 copy-start.21
  124.4 0.8 copy-start.22
  125.2 20.8 %copy-start.33 = (bf16[16]{0:T(256)(128)(2,1)S(1)}, bf16[16]{0:T(256)(128)(2,1)}, u32[]{:S(2)}) copy-start(bf16[16]{0:T(256)(128)(2,1)} %param.35) | copy-start | bytes 100
  128.6 5.9 %collective-permute-start.23 = (f32[168,128]{1,0:T(8,128)}, f32[168,128]{1,0:T(8,128)S(1)}, u32[]{:S(2)}, u32[]{:S(2)}) collective-permute-start(f32[168,128]{1,0:T(8,128)} %get-tuple-element.80), channel_id=1, source_target_pairs={{0,1},{1,2},{2,3},{3,0},{4,5},{5,6},{6,7},{7,4},{8,9},{9,10},{10,1... | collective-permute-start | bytes 258056 | tf_op jit(solution)/shard_map/ppermute | solution.py:683
  130.4 6.3 %collective-permute-start.24 = (f32[168,128]{1,0:T(8,128)}, f32[168,128]{1,0:T(8,128)S(1)}, u32[]{:S(2)}, u32[]{:S(2)}) collective-permute-start(f32[168,128]{1,0:T(8,128)} %get-tuple-element.81), channel_id=1, source_target_pairs={{0,2},{1,3},{2,0},{3,1},{4,6},{5,7},{6,4},{7,5},{8,10},{9,11},{10,... | collective-permute-start | bytes 258056 | tf_op jit(solution)/shard_map/ppermute | solution.py:683
  133.0 4.7 %collective-permute-start.25 = (f32[168,128]{1,0:T(8,128)}, f32[168,128]{1,0:T(8,128)S(1)}, u32[]{:S(2)}, u32[]{:S(2)}) collective-permute-start(f32[168,128]{1,0:T(8,128)} %get-tuple-element.82), channel_id=1, source_target_pairs={{0,3},{1,0},{2,1},{3,2},{4,7},{5,4},{6,5},{7,6},{8,11},{9,8},{10,9... | collective-permute-start | bytes 258056 | tf_op jit(solution)/shard_map/ppermute | solution.py:683
  134.6 3.2 %copy-start.12 = (f32[168,128]{1,0:T(8,128)}, f32[168,128]{1,0:T(8,128)S(1)}, u32[]{:S(2)}) copy-start(f32[168,128]{1,0:T(8,128)S(1)} %collective-permute-done.23.b1) | copy-start | bytes 258052
  136.6 1.1 copy-start.13
  137.7 0.6 copy-start.14
  139.7 14.8 %all-to-all-start.1 = ((f32[32,8,128]{2,1,0:T(8,128)}), f32[32,8,128]{2,1,0:T(8,128)S(1)}, u32[]{:S(2)}, u32[]{:S(2)}) async-start(f32[32,8,128]{2,1,0:T(8,128)} %merge.1), calls=%async_computation.1 | async-start | bytes 262144 | tf_op jit(solution)/shard_map/all_to_all | solution.py:832
  154.6 0.7 copy-start.23
  165.5 5.8 %collective-permute-start.26 = (f32[128,128]{1,0:T(8,128)}, f32[128,128]{1,0:T(8,128)S(1)}, u32[]{:S(2)}, u32[]{:S(2)}) collective-permute-start(f32[128,128]{1,0:T(8,128)} %get-tuple-element.88), channel_id=1, source_target_pairs={{0,1},{1,2},{2,3},{3,0},{4,5},{5,6},{6,7},{7,4},{8,9},{9,10},{10,1... | collective-permute-start | bytes 196616 | tf_op jit(solution)/shard_map/ppermute | solution.py:683
  166.2 7.2 %collective-permute-start.27 = (f32[128,128]{1,0:T(8,128)}, f32[128,128]{1,0:T(8,128)S(1)}, u32[]{:S(2)}, u32[]{:S(2)}) collective-permute-start(f32[128,128]{1,0:T(8,128)} %get-tuple-element.89), channel_id=1, source_target_pairs={{0,2},{1,3},{2,0},{3,1},{4,6},{5,7},{6,4},{7,5},{8,10},{9,11},{10,... | collective-permute-start | bytes 196616 | tf_op jit(solution)/shard_map/ppermute | solution.py:683
  169.7 4.5 %collective-permute-start.28 = (f32[128,128]{1,0:T(8,128)}, f32[128,128]{1,0:T(8,128)S(1)}, u32[]{:S(2)}, u32[]{:S(2)}) collective-permute-start(f32[128,128]{1,0:T(8,128)} %get-tuple-element.90), channel_id=1, source_target_pairs={{0,3},{1,0},{2,1},{3,2},{4,7},{5,4},{6,5},{7,6},{8,11},{9,8},{10,9... | collective-permute-start | bytes 196616 | tf_op jit(solution)/shard_map/ppermute | solution.py:683
  171.2 2.9 %copy-start.24 = (f32[128,128]{1,0:T(8,128)}, f32[128,128]{1,0:T(8,128)S(1)}, u32[]{:S(2)}) copy-start(f32[128,128]{1,0:T(8,128)S(1)} %collective-permute-done.26.o1) | copy-start | bytes 196612
  173.4 0.7 copy-start.25
  174.1 0.6 copy-start.26
  (1 other events, 0.6 us)
